TPU v7x, 32 devices: a whole 2x2x4 slice. The times are simulated.
32 devices in a mesh: fsdp: 8 (over y, x, core), sp: 4 (over z).
Axes of the slice: x: 2, y: 2, z: 4, core: 2. Of those that a mesh axis runs over, the one named last changes fastest.
Arguments:
- inputs: bfloat16 [8, 1024, 768], P('fsdp', 'sp'), may hold values from -6 to 6
- w_qkv: bfloat16 [2, 768, 3, 768], P(None, 'fsdp'), may hold values from -0.21875 to 0.21875
- w_out: bfloat16 [2, 768, 768], P(None, 'fsdp'), may hold values from -0.875 to 0.875
- w_up: bfloat16 [2, 768, 3072], P(None, 'fsdp'), may hold values from -0.21875 to 0.21875
- w_down: bfloat16 [2, 3072, 768], P(None, 'fsdp'), may hold values from -0.109375 to 0.109375
- norm_gain: bfloat16 [2, 2, 768], P(None, None, 'fsdp'), may hold values from 0.5 to 1.5
- norm_shift: bfloat16 [2, 2, 768], P(None, None, 'fsdp'), may hold values from -4 to 4
- qv_bias: bfloat16 [2, 2, 768], P(None, None, 'fsdp'), may hold values from -4 to 4
- branch_bias: bfloat16 [2, 2, 768], P(None, None, 'fsdp'), may hold values from -4 to 4
- up_bias: bfloat16 [2, 3072], P(None, 'fsdp'), may hold values from -6 to 6
- cotangent: bfloat16 [8, 1024, 768], P('fsdp', 'sp'), may hold values from -6 to 6
Outputs:
- output: bfloat16 [8, 1024, 768], P('fsdp', 'sp')
- grad_inputs: bfloat16 [8, 1024, 768], P('fsdp', 'sp')
- grad_w_qkv: float32 [2, 768, 3, 768], P(None, 'fsdp')
- grad_w_out: float32 [2, 768, 768], P(None, 'fsdp')
- grad_w_up: float32 [2, 768, 3072], P(None, 'fsdp')
- grad_w_down: float32 [2, 3072, 768], P(None, 'fsdp')
- grad_norm_gain: float32 [2, 2, 768], P(None, None, 'fsdp')
- grad_norm_shift: float32 [2, 2, 768], P(None, None, 'fsdp')
- grad_qv_bias: float32 [2, 2, 768], P(None, None, 'fsdp')
- grad_branch_bias: float32 [2, 2, 768], P(None, None, 'fsdp')
- grad_up_bias: float32 [2, 3072], P(None, 'fsdp')
All inputs are finite; a program needn't handle non-finite values.
Results may differ from a plain program's by a relative error of at most 0.014.
Values may be sent and summed in bfloat16 or wider, within the bound.
A program may use at most 256 MiB of HBM per device.

v0:
```python
import jax
import jax.numpy as jnp
from jax import lax
from jax.sharding import PartitionSpec as P

HD = 64
LAYERS = 2


epsilon = 1e-05


def norm_rows(values, gain, shift):
    center = values - jnp.mean(values, axis=-1, keepdims=True)
    variance = jnp.mean(center * center, axis=-1, keepdims=True)
    return center * lax.rsqrt(variance + epsilon) * gain + shift


def gelu_exact(values):
    return jax.nn.gelu(values, approximate=False)


def product(left, right):
    return jnp.dot(left, right, preferred_element_type=jnp.float32)


def product_back(left, right):
    return jnp.einsum("te,fe->tf", left, right, preferred_element_type=jnp.float32)


def outer_sum(left, right):
    return jnp.einsum("td,te->de", left, right, preferred_element_type=jnp.float32)


def column_sums(values):
    return jnp.sum(values.astype(jnp.float32), axis=0)


def pack_layer(
    layer_index, w_qkv, w_out, w_up, w_down, norm_gain, norm_shift, qv_bias, branch_bias, up_bias
):
    shard = w_out.shape[1]
    matrices = jnp.concatenate(
        [
            w_qkv[layer_index].reshape(shard, -1),
            w_out[layer_index],
            w_up[layer_index],
            w_down[layer_index].reshape(shard, -1),
        ],
        axis=1,
    )
    vectors = jnp.concatenate(
        [
            norm_gain[layer_index].T,
            norm_shift[layer_index].T,
            qv_bias[layer_index].T,
            branch_bias[layer_index].T,
            up_bias[layer_index].reshape(shard, -1),
        ],
        axis=1,
    )
    return (matrices, vectors)


def fetch(matrices, vectors):
    return (
        lax.all_gather(matrices, "fsdp", axis=0, tiled=True),
        lax.all_gather(vectors, "fsdp", axis=0, tiled=True),
    )


def settle(matrix_grads, vector_grads):
    matrix_grads, vector_grads = (
        lax.psum_scatter(matrix_grads, "fsdp", scatter_dimension=0, tiled=True),
        lax.psum_scatter(vector_grads, "fsdp", scatter_dimension=0, tiled=True),
    )
    matrix_grads, vector_grads = (
        lax.psum_scatter(
            matrix_grads.astype(jnp.bfloat16), "sp", scatter_dimension=1, tiled=True
        ).astype(jnp.float32),
        lax.psum_scatter(
            vector_grads.astype(jnp.bfloat16), "sp", scatter_dimension=1, tiled=True
        ).astype(jnp.float32),
    )
    return (
        lax.all_gather(matrix_grads.astype(jnp.bfloat16), "sp", axis=1, tiled=True).astype(
            matrix_grads.dtype
        ),
        lax.all_gather(vector_grads.astype(jnp.bfloat16), "sp", axis=1, tiled=True).astype(
            vector_grads.dtype
        ),
    )


def attend(query_rows, key_rows, value_rows):
    clips, length, local_heads, head_size = query_rows.shape
    block = min(512, length)
    scale = head_size ** (-0.5)

    def one_block(start):
        query_block = lax.dynamic_slice_in_dim(query_rows, start, block, 1)
        scores = (
            jnp.einsum("cqhd,ckhd->chqk", query_block, key_rows, preferred_element_type=jnp.float32)
            * scale
        )
        highest = jnp.max(scores, axis=-1, keepdims=True)
        powered = jnp.exp(scores - highest)
        summed = jnp.sum(powered, axis=-1, keepdims=True)
        weights_low = (powered / summed).astype(jnp.bfloat16)
        mixed = jnp.einsum(
            "chqk,ckhd->cqhd", weights_low, value_rows, preferred_element_type=jnp.float32
        )
        return (mixed.astype(jnp.bfloat16), (highest + jnp.log(summed))[..., 0])

    starts = jnp.arange(length // block, dtype=jnp.int32) * block
    mixed, log_total = lax.map(one_block, starts)
    mixed = jnp.moveaxis(mixed, 0, 1).reshape(clips, length, local_heads, head_size)
    log_total = jnp.moveaxis(log_total, 0, 2).reshape(clips, local_heads, length)
    return (mixed, log_total)


def attend_back(query_rows, key_rows, value_rows, log_total, grad_mixed):
    clips, length, local_heads, head_size = query_rows.shape
    block = min(512, length)
    scale = head_size ** (-0.5)

    def one_block(carry, start):
        grad_keys, grad_values = carry
        query_block = lax.dynamic_slice_in_dim(query_rows, start, block, 1)
        grad_block = lax.dynamic_slice_in_dim(grad_mixed, start, block, 1)
        total_block = lax.dynamic_slice_in_dim(log_total, start, block, 2)
        scores = (
            jnp.einsum("cqhd,ckhd->chqk", query_block, key_rows, preferred_element_type=jnp.float32)
            * scale
        )
        weights_full = jnp.exp(scores - total_block[..., None])
        grad_weights = jnp.einsum(
            "cqhd,ckhd->chqk", grad_block, value_rows, preferred_element_type=jnp.float32
        )
        inner = jnp.sum(weights_full * grad_weights, axis=-1, keepdims=True)
        grad_scores = (weights_full * (grad_weights - inner)).astype(jnp.bfloat16)
        grad_query = (
            jnp.einsum("chqk,ckhd->cqhd", grad_scores, key_rows, preferred_element_type=jnp.float32)
            * scale
        )
        grad_keys = (
            grad_keys
            + jnp.einsum(
                "chqk,cqhd->ckhd", grad_scores, query_block, preferred_element_type=jnp.float32
            )
            * scale
        )
        grad_values = grad_values + jnp.einsum(
            "chqk,cqhd->ckhd",
            weights_full.astype(jnp.bfloat16),
            grad_block,
            preferred_element_type=jnp.float32,
        )
        return ((grad_keys, grad_values), grad_query.astype(jnp.bfloat16))

    starts = jnp.arange(length // block, dtype=jnp.int32) * block
    zeros_start = jnp.zeros(key_rows.shape, jnp.float32)
    (grad_keys, grad_values), grad_query = lax.scan(one_block, (zeros_start, zeros_start), starts)
    grad_query = jnp.moveaxis(grad_query, 0, 1).reshape(clips, length, local_heads, head_size)
    return (grad_query, grad_keys.astype(jnp.bfloat16), grad_values.astype(jnp.bfloat16))


def local(
    inputs,
    w_qkv,
    w_out,
    w_up,
    w_down,
    norm_gain,
    norm_shift,
    qv_bias,
    branch_bias,
    up_bias,
    cotangent,
):
    clips, frames, width = inputs.shape
    groups = lax.axis_size("sp")
    length = frames * groups
    hidden = w_up.shape[2]
    local_heads = width // groups // HD
    rows_all = clips * frames
    stream = inputs.astype(jnp.float32).reshape(rows_all, width)
    kept = []
    for layer_index in range(LAYERS):
        matrices, vectors = pack_layer(
            layer_index,
            w_qkv,
            w_out,
            w_up,
            w_down,
            norm_gain,
            norm_shift,
            qv_bias,
            branch_bias,
            up_bias,
        )
        matrices, vectors = fetch(matrices, vectors)
        weight_qkv = matrices[:, : 3 * width]
        weight_out = matrices[:, 3 * width : 4 * width]
        weight_up = matrices[:, 4 * width : 4 * width + hidden]
        weight_down = matrices[:, 4 * width + hidden :].reshape(hidden, width)
        vector_full = vectors.astype(jnp.float32)
        gains = vector_full[:, 0:2]
        shifts = vector_full[:, 2:4]
        attn_bias = vector_full[:, 4:6]
        branch = vector_full[:, 6:8]
        up_shift = vector_full[:, 8:].reshape(hidden)
        normed = norm_rows(stream, gains[:, 0], shifts[:, 0]).astype(jnp.bfloat16)
        bias_qkv = jnp.concatenate(
            [attn_bias[:, 0], jnp.zeros((width,), jnp.float32), attn_bias[:, 1]]
        )
        projected = (product(normed, weight_qkv) + bias_qkv).astype(jnp.bfloat16)
        heads = lax.all_to_all(
            projected.reshape(clips, frames, 3, groups, width // groups),
            "sp",
            split_axis=3,
            concat_axis=1,
            tiled=True,
        )
        heads = heads.reshape(clips, length, 3, local_heads, HD)
        query_rows = heads[:, :, 0]
        key_rows = heads[:, :, 1]
        value_rows = heads[:, :, 2]
        mixed, log_total = attend(query_rows, key_rows, value_rows)
        returned = lax.all_to_all(
            mixed.reshape(clips, length, 1, width // groups),
            "sp",
            split_axis=1,
            concat_axis=2,
            tiled=True,
        )
        mixed_rows = returned.reshape(rows_all, width)
        middle = stream + product(mixed_rows, weight_out) + branch[:, 0]
        normed_two = norm_rows(middle, gains[:, 1], shifts[:, 1]).astype(jnp.bfloat16)
        pre_act = product(normed_two, weight_up) + up_shift
        activated = gelu_exact(pre_act).astype(jnp.bfloat16)
        kept.append(
            (
                stream,
                weight_qkv,
                weight_out,
                weight_up,
                weight_down,
                gains,
                shifts,
                normed,
                query_rows,
                key_rows,
                value_rows,
                log_total,
                mixed_rows,
                middle,
                normed_two,
                pre_act,
                activated,
            )
        )
        stream = middle + product(activated, weight_down) + branch[:, 1]
    output = stream.astype(jnp.bfloat16).reshape(clips, frames, width)
    grad_stream = cotangent.astype(jnp.float32).reshape(rows_all, width)
    layer_grads = []
    for layer_index in reversed(range(LAYERS)):
        (
            layer_input,
            weight_qkv,
            weight_out,
            weight_up,
            weight_down,
            gains,
            shifts,
            normed,
            query_rows,
            key_rows,
            value_rows,
            log_total,
            mixed_rows,
            middle,
            normed_two,
            pre_act,
            activated,
        ) = kept[layer_index]
        grad_branch = grad_stream.astype(jnp.bfloat16)
        grad_down = outer_sum(activated, grad_branch)
        grad_down_bias = column_sums(grad_branch)
        grad_act = product_back(grad_branch, weight_down)
        grad_pre = jax.vjp(gelu_exact, pre_act)[1](grad_act)[0].astype(jnp.bfloat16)
        grad_up = outer_sum(normed_two, grad_pre)
        grad_up_bias = column_sums(grad_pre)
        grad_norm_two = product_back(grad_pre, weight_up)
        norm_pull = jax.vjp(norm_rows, middle, gains[:, 1], shifts[:, 1])[1]
        grad_middle, grad_gain_two, grad_shift_two = norm_pull(grad_norm_two)
        grad_middle = grad_middle + grad_stream
        grad_branch_one = grad_middle.astype(jnp.bfloat16)
        grad_out = outer_sum(mixed_rows, grad_branch_one)
        grad_out_bias = column_sums(grad_branch_one)
        grad_mixed = product_back(grad_branch_one, weight_out).astype(jnp.bfloat16)
        grad_heads = lax.all_to_all(
            grad_mixed.reshape(clips, frames, groups, width // groups),
            "sp",
            split_axis=2,
            concat_axis=1,
            tiled=True,
        )
        grad_heads = grad_heads.reshape(clips, length, local_heads, HD)
        grad_query, grad_key, grad_value = attend_back(
            query_rows, key_rows, value_rows, log_total, grad_heads
        )
        stacked = jnp.stack([grad_query, grad_key, grad_value], axis=2).reshape(
            clips, length, 3, 1, width // groups
        )
        grad_proj = lax.all_to_all(stacked, "sp", split_axis=1, concat_axis=3, tiled=True).reshape(
            rows_all, 3 * width
        )
        grad_qkv = outer_sum(normed, grad_proj)
        proj_sums = column_sums(grad_proj)
        grad_norm_one = product_back(grad_proj, weight_qkv)
        norm_pull = jax.vjp(norm_rows, layer_input, gains[:, 0], shifts[:, 0])[1]
        grad_input, grad_gain_one, grad_shift_one = norm_pull(grad_norm_one)
        grad_stream = grad_middle + grad_input
        matrix_grads = jnp.concatenate(
            [grad_qkv, grad_out, grad_up, grad_down.reshape(width, hidden)], axis=1
        )
        vector_grads = jnp.concatenate(
            [
                jnp.stack([grad_gain_one, grad_gain_two], axis=1),
                jnp.stack([grad_shift_one, grad_shift_two], axis=1),
                jnp.stack([proj_sums[:width], proj_sums[2 * width :]], axis=1),
                jnp.stack([grad_out_bias, grad_down_bias], axis=1),
                grad_up_bias.reshape(width, hidden // width),
            ],
            axis=1,
        )
        layer_grads.append(settle(matrix_grads, vector_grads))
    layer_grads = layer_grads[::-1]
    grad_inputs = grad_stream.astype(jnp.bfloat16).reshape(clips, frames, width)
    shard = w_out.shape[1]
    qkv_list, out_list, up_list, down_list = ([], [], [], [])
    gain_list, shift_list, bias_list, branch_list, upbias_list = ([], [], [], [], [])
    for matrix_part, vector_part in layer_grads:
        qkv_list.append(matrix_part[:, : 3 * width].reshape(shard, 3, width))
        out_list.append(matrix_part[:, 3 * width : 4 * width])
        up_list.append(matrix_part[:, 4 * width : 4 * width + hidden])
        down_list.append(matrix_part[:, 4 * width + hidden :].reshape(-1, width))
        gain_list.append(vector_part[:, 0:2].T)
        shift_list.append(vector_part[:, 2:4].T)
        bias_list.append(vector_part[:, 4:6].T)
        branch_list.append(vector_part[:, 6:8].T)
        upbias_list.append(vector_part[:, 8:].reshape(-1))
    return (
        output,
        grad_inputs,
        jnp.stack(qkv_list),
        jnp.stack(out_list),
        jnp.stack(up_list),
        jnp.stack(down_list),
        jnp.stack(gain_list),
        jnp.stack(shift_list),
        jnp.stack(bias_list),
        jnp.stack(branch_list),
        jnp.stack(upbias_list),
    )


def solution(mesh):
    placed = (
        P("fsdp", "sp", None),
        P(None, "fsdp", None, None),
        P(None, "fsdp", None),
        P(None, "fsdp", None),
        P(None, "fsdp", None),
        P(None, None, "fsdp"),
        P(None, None, "fsdp"),
        P(None, None, "fsdp"),
        P(None, None, "fsdp"),
        P(None, "fsdp"),
        P("fsdp", "sp", None),
    )
    return jax.shard_map(
        local,
        mesh=mesh,
        in_specs=placed,
        out_specs=(
            P("fsdp", "sp", None),
            P("fsdp", "sp", None),
            P(None, "fsdp", None, None),
            P(None, "fsdp", None),
            P(None, "fsdp", None),
            P(None, "fsdp", None),
            P(None, None, "fsdp"),
            P(None, None, "fsdp"),
            P(None, None, "fsdp"),
            P(None, None, "fsdp"),
            P(None, "fsdp"),
        ),
        check_vma=False,
    )
```

profile of v0, /device:TPU:0, one launch (start us, length us, event | category | flops | bytes accessed | tf_op | source)
XLA Modules:
  0.0 1065.3 jit_solution(18408592276132677847)
XLA Ops:
  15.0 10.5 all-gather.1
  25.9 9.2 all-gather
  36.9 57.1 %all-gather.9.cloned.1.call-done = bf16[768,9216]{1,0:T(8,128)(2,1)} async-done(((bf16[96,9216]{1,0:T(8,128)(2,1)}), bf16[768,9216]{1,0:T(8,128)(2,1)}) %all-gather.9.cloned.1.call-update) | async-done | bytes 14155792 | tf_op jit(solution)/shard_map/all_gather | solution.py:67
  99.0 4.8 all-to-all-start
  104.3 28.5 %all-to-all-done = bf16[1,256,3,4,192]{1,4,2,0,3:T(8,128)(2,1)S(1)} async-done(((bf16[1,256,3,4,192]{1,4,2,0,3:T(8,128)(2,1)}), bf16[1,256,3,4,192]{1,4,2,0,3:T(8,128)(2,1)S(1)}, u32[]{:S(2)}, u32[]{:S(2)}) %all-to-all-start) | async-done | bytes 1179680 | tf_op jit(solution)/shard_map/all_to_all | solution.py:218
  136.2 20.0 %while.54 = (s32[]{:T(128)}, bf16[2,1,512,3,64]{2,4,3,1,0:T(8,128)(2,1)S(1)}, f32[2,1,3,512]{3,2,1,0:T(4,128)}, s32[2]{0:T(128)}, bf16[1,1024,3,64]{1,3,2,0:T(8,...) while((s32[]{:T(128)}, ...), condition=%wide.region_5.6_spmd, body=%wide.region_2.5_spmd.sunk | while | flops 416905728 | bytes 20109480 | solution.py:116
  167.8 5.0 slice.334
  172.7 8.5 reshape.509
  185.3 11.4 %multiply_convert_fusion.3 = (bf16[256,3072]{1,0:T(8,128)(2,1)S(1)}, f32[256,3072]{1,0:T(8,128)}, f32[256,3072]{1,0:T(8,128)}) fusion(f32[3072]{0:T(1024)S(1)} %add.289, bf16[768,9216]{1,0:T(8,128)(2,1)} %all-gather.9.cloned.1.call-done, f32[256,768]{1,0:T(8,128)S(1)} %get-tuple-element.511, f32[768]{0:T(1024)S(1)} %get-tuple-element.370, ...), kind=kOutput, calls=%fused_computation.140 | convolution fusion | flops 1260847104 | bytes 13389824 | tf_op jit(solution)/shard_map/dot_general | solution.py:24
  203.5 5.5 all-to-all-start.2
  208.9 27.5 %all-to-all-done.2 = bf16[1,256,3,4,192]{1,4,2,0,3:T(8,128)(2,1)S(1)} async-done(((bf16[1,256,3,4,192]{1,4,2,0,3:T(8,128)(2,1)}), bf16[1,256,3,4,192]{1,4,2,0,3:T(8,128)(2,1)S(1)}, u32[]{:S(2)}, u32[]{:S(2)}) %all-to-all-start.2) | async-done | bytes 1179680 | tf_op jit(solution)/shard_map/all_to_all | solution.py:218
  239.9 20.0 %while.55 = (s32[]{:T(128)}, bf16[2,1,512,3,64]{2,4,3,1,0:T(8,128)(2,1)S(1)}, f32[2,1,3,512]{3,2,1,0:T(4,128)}, s32[2]{0:T(128)}, bf16[1,1024,3,64]{1,3,2,0:T(8,...) while((s32[]{:T(128)}, ...), condition=%wide.region_13.14_spmd, body=%wide.region_10.13_spmd.sunk | while | flops 416905728 | bytes 20109480 | solution.py:116
  261.5 4.0 reduce.54
  270.9 4.9 slice.350
  275.8 8.5 reshape.513
  288.5 10.7 %multiply_convert_fusion.2 = (bf16[256,3072]{1,0:T(8,128)(2,1)}, f32[256,3072]{1,0:T(8,128)S(1)}, f32[256,3072]{1,0:T(8,128)S(1)}) fusion(f32[3072]{0:T(1024)S(1)} %add.310, bf16[768,9216]{1,0:T(8,128)(2,1)} %all-gather.11.cloned.1.call-done, f32[256,768]{1,0:T(8,128)S(1)} %get-tuple-element.516, f32[768]{0:T(1024)S(1)} %copy-done.76, ...), kind=kOutput, calls=%fused_computation.127 | convolution fusion | flops 1260847104 | bytes 13389824 | tf_op jit(solution)/shard_map/dot_general | solution.py:24
  301.9 5.1 multiply_reduce_fusion.4
  312.6 5.3 all-to-all-start.4
  317.9 10.6 all-to-all-done.4
  330.6 38.7 %while.56 = (s32[]{:T(128)}, f32[1,1024,3,64]{1,3,2,0:T(8,128)}, f32[1,1024,3,64]{1,3,2,0:T(8,128)}, bf16[2,1,512,3,64]{2,4,3,1,0:T(8,128)(2,1)}, s32[2]{0:T(128...) while((s32[]{:T(128)}, f32[1,1024,3,64]{1,3,2,0:T(8,128)}, ...), condition=%wide.region_20.21_spmd.clone, body=%wide.region_18.20_spmd.clone.sunk | while | flops 1026685440 | bytes 106015048 | solution.py:163
  379.7 6.5 fusion.158
  386.2 11.9 %reshape.526 = f32[768,3072]{1,0:T(8,128)} reshape(f32[3072,768]{1,0:T(8,128)} %fusion.158) | data formatting | bytes 18874368 | tf_op jit(solution)/shard_map/reshape | solution.py:326
  400.2 5.3 fusion.185
  405.5 20.3 %all-to-all-done.5 = bf16[1,1024,3,1,192]{4,2,3,0,1:T(4,128)(2,1)S(1)} async-done(((bf16[1,1024,3,1,192]{4,2,3,0,1:T(4,128)(2,1)}), bf16[1,1024,3,1,192]{4,2,3,0,1:T(4,128)(2,1)S(1)}, u32[]{:S(2)}, u32[]{:S(2)}) %all-to-all-start.5) | async-done | bytes 1179680 | tf_op jit(solution)/shard_map/all_to_all | solution.py:316
  431.2 4.1 fusion.184
  435.4 19.2 %pad_maximum_fusion.1 = f32[768,9216]{1,0:T(8,128)} fusion(f32[768,3072]{1,0:T(8,128)} %reshape.526, f32[768,3072]{1,0:T(8,128)} %fusion.185, f32[768,768]{1,0:T(8,128)} %fusion.202, f32[768,2304]{1,0:T(8,128)} %fusion.184), kind=kLoop, calls=%fused_computation.103 | loop fusion | flops 21233664 | bytes 56623104 | tf_op jit(solution)/shard_map/concatenate | solution.py:325
  454.7 4.1 multiply_reduce_fusion.5
  460.8 6.4 convert_reduce_fusion.1
  467.2 6.2 multiply_reduce_fusion.6
  482.1 12.3 %all-to-all-done.6 = bf16[1,256,4,192]{1,3,0,2:T(8,128)(2,1)S(1)} async-done(((bf16[1,256,4,192]{1,3,0,2:T(8,128)(2,1)}), bf16[1,256,4,192]{1,3,0,2:T(8,128)(2,1)S(1)}, u32[]{:S(2)}, u32[]{:S(2)}) %all-to-all-start.6) | async-done | bytes 393248 | tf_op jit(solution)/shard_map/all_to_all | solution.py:302
  496.5 39.7 %while.57 = (s32[]{:T(128)}, f32[1,1024,3,64]{1,3,2,0:T(8,128)}, f32[1,1024,3,64]{1,3,2,0:T(8,128)}, bf16[2,1,512,3,64]{2,4,3,1,0:T(8,128)(2,1)}, s32[2]{0:T(128...) while((s32[]{:T(128)}, f32[1,1024,3,64]{1,3,2,0:T(8,128)}, ...), condition=%wide.region_27.28_spmd.clone, body=%wide.region_25.27_spmd.clone.sunk | while | flops 1026685440 | bytes 106015048 | solution.py:163
  543.0 4.5 all-to-all-start.7
  547.6 5.1 fusion.176
  552.7 11.9 %reshape.525 = f32[768,3072]{1,0:T(8,128)} reshape(f32[3072,768]{1,0:T(8,128)} %fusion.176) | data formatting | bytes 18874368 | tf_op jit(solution)/shard_map/reshape | solution.py:326
  566.8 5.2 fusion.183
  572.1 23.7 %all-to-all-done.7 = bf16[1,1024,3,1,192]{4,2,3,0,1:T(4,128)(2,1)} async-done(((bf16[1,1024,3,1,192]{4,2,3,0,1:T(4,128)(2,1)}), bf16[1,1024,3,1,192]{4,2,3,0,1:T(4,128)(2,1)}, u32[]{:S(2)}, u32[]{:S(2)}) %all-to-all-start.7) | async-done | bytes 1179680 | tf_op jit(solution)/shard_map/all_to_all | solution.py:316
  601.0 4.2 fusion.155
  605.3 20.5 %pad_maximum_fusion = f32[768,9216]{1,0:T(8,128)} fusion(f32[768,3072]{1,0:T(8,128)} %reshape.525, f32[768,3072]{1,0:T(8,128)} %fusion.183, f32[768,768]{1,0:T(8,128)} %fusion.201, f32[768,2304]{1,0:T(8,128)} %fusion.155), kind=kLoop, calls=%fused_computation.102 | loop fusion | flops 21233664 | bytes 56623104 | tf_op jit(solution)/shard_map/concatenate | solution.py:325
  641.7 161.4 %reduce-scatter.9.cloned.1.call-done = f32[96,9216]{1,0:T(8,128)} async-done(((f32[768,9216]{1,0:T(8,128)}), f32[96,9216]{1,0:T(8,128)}) %reduce-scatter.9.cloned.1.call-update) | async-done | bytes 3538960 | tf_op jit(solution)/shard_map/reduce_scatter | solution.py:74
  825.9 18.3 %reduce-scatter.15.cloned.1.call-done = bf16[96,2304]{1,0:T(8,128)(2,1)} async-done(((bf16[96,9216]{1,0:T(8,128)(2,1)}), bf16[96,2304]{1,0:T(8,128)(2,1)}) %reduce-scatter.15.cloned.1.call-update) | async-done | bytes 442384 | tf_op jit(solution)/shard_map/reduce_scatter | solution.py:78
  846.2 5.1 fusion.131
  851.3 29.1 %reduce-scatter.19.cloned.1.call-done = f32[96,12]{1,0:T(8,128)} async-done(((f32[768,12]{1,0:T(8,128)}), f32[96,12]{1,0:T(8,128)}) %reduce-scatter.19.cloned.1.call-update) | async-done | bytes 4624 | tf_op jit(solution)/shard_map/reduce_scatter | solution.py:75
  881.2 40.6 %reduce-scatter.11.cloned.1.call-done = bf16[96,2304]{1,0:T(8,128)(2,1)} async-done(((bf16[96,9216]{1,0:T(8,128)(2,1)}), bf16[96,2304]{1,0:T(8,128)(2,1)}) %reduce-scatter.11.cloned.1.call-update) | async-done | bytes 442384 | tf_op jit(solution)/shard_map/reduce_scatter | solution.py:78
  924.3 34.1 %reduce-scatter.17.cloned.1.call-done = f32[96,12]{1,0:T(8,128)} async-done(((f32[768,12]{1,0:T(8,128)}), f32[96,12]{1,0:T(8,128)}) %reduce-scatter.17.cloned.1.call-update) | async-done | bytes 4624 | tf_op jit(solution)/shard_map/reduce_scatter | solution.py:75
  959.2 20.4 %all-reduce.2 = (bf16[96,12]{1,0:T(8,128)(2,1)S(1)}, bf16[96,12]{1,0:T(8,128)(2,1)S(1)}) all-reduce(bf16[96,12]{1,0:T(8,128)(2,1)S(1)} %convert_element_type.245, bf16[96,12]{1,0:T(8,128)(2,1)S(1)} %convert_element_type.250), channel_id=7, replica_groups=mesh['fsdp'=8,'sp'=4] {'sp'}, use_global_device_ids=true, to_apply=%region_43.44.clone | all-reduce | flops 2304 | bytes 9216
  979.8 7.8 all-gather.3
  987.8 10.4 all-gather.2
  1007.1 34.4 %all-gather.13.cloned.1.call-done = bf16[96,9216]{1,0:T(8,128)(2,1)} async-done(((bf16[96,2304]{1,0:T(8,128)(2,1)}), bf16[96,9216]{1,0:T(8,128)(2,1)}) %all-gather.13.cloned.1.call-update) | async-done | bytes 1769488 | tf_op jit(solution)/shard_map/all_gather | solution.py:86
  (559 shorter events, 282.9 us)
Async XLA Ops:
  7.2 86.9 %all-gather.9.cloned.1.call-start = ((), (), s32[]{:S(2)}) async-start(), calls=%async_computation.14 | async-start | bytes 15925248 | tf_op jit(solution)/shard_map/all_gather | solution.py:67
  12.4 186.2 %all-gather.11.cloned.1.call-start = ((), (), s32[]{:S(2)}) async-start(), calls=%async_computation.15 | async-start | bytes 15925248 | tf_op jit(solution)/shard_map/all_gather | solution.py:67
  25.6 71.6 %copy-start.64 = (f32[768,12]{0,1:T(8,128)}, f32[768,12]{0,1:T(8,128)S(1)}, u32[]{:S(2)}) copy-start(f32[768,12]{0,1:T(8,128)S(1)} %reshape.538) | copy-start | bytes 110596
  35.8 162.8 %copy-start.67 = (f32[768]{0:T(1024)}, f32[768]{0:T(1024)S(1)}, u32[]{:S(2)}) copy-start(f32[768]{0:T(1024)S(1)} %get-tuple-element.368) | copy-start | bytes 9220
  35.8 162.8 %copy-start.74 = (f32[768]{0:T(1024)}, f32[768]{0:T(1024)S(1)}, u32[]{:S(2)}) copy-start(f32[768]{0:T(1024)S(1)} %get-tuple-element.367) | copy-start | bytes 9220
  35.8 61.4 %copy-start.62 = (f32[768]{0:T(1024)}, f32[768]{0:T(1024)S(1)}, u32[]{:S(2)}) copy-start(f32[768]{0:T(1024)S(1)} %get-tuple-element.376) | copy-start | bytes 9220
  35.8 61.4 %copy-start.70 = (f32[768]{0:T(1024)}, f32[768]{0:T(1024)S(1)}, u32[]{:S(2)}) copy-start(f32[768]{0:T(1024)S(1)} %get-tuple-element.375) | copy-start | bytes 9220
  35.9 149.4 %copy-start.65 = (f32[768]{0:T(1024)}, f32[768]{0:T(1024)S(1)}, u32[]{:S(2)}) copy-start(f32[768]{0:T(1024)S(1)} %get-tuple-element.371) | copy-start | bytes 9220
  35.9 149.4 %copy-start.72 = (f32[768]{0:T(1024)}, f32[768]{0:T(1024)S(1)}, u32[]{:S(2)}) copy-start(f32[768]{0:T(1024)S(1)} %get-tuple-element.370) | copy-start | bytes 9220
  36.6 60.6 %copy-start.77 = (f32[256]{0:T(256)}, f32[256]{0:T(256)S(1)}, u32[]{:S(2)}) copy-start(f32[256]{0:T(256)S(1)} %broadcast_multiply_fusion.3) | copy-start | bytes 3076
  36.9 60.4 %copy-start.103 = (f32[256]{0:T(256)}, f32[256]{0:T(256)S(1)}, u32[]{:S(2)}) copy-start(f32[256]{0:T(256)S(1)} %fusion.146) | copy-start | bytes 3076
  36.9 60.4 %copy-start.79 = (f32[256]{0:T(256)}, f32[256]{0:T(256)S(1)}, u32[]{:S(2)}) copy-start(f32[256]{0:T(256)S(1)} %fusion.172) | copy-start | bytes 3076
  99.0 33.7 %all-to-all-start = ((bf16[1,256,3,4,192]{1,4,2,0,3:T(8,128)(2,1)}), bf16[1,256,3,4,192]{1,4,2,0,3:T(8,128)(2,1)S(1)}, u32[]{:S(2)}, u32[]{:S(2)}) async-start(bf16[1,256,3,4,192]{1,4,2,0,3:T(8,128)(2,1)} %copy.330), calls=%async_computation | async-start | bytes 2359296 | tf_op jit(solution)/shard_map/all_to_all | solution.py:218
  163.7 17.5 %all-to-all-start.1 = ((bf16[4,2,24576]{2,1,0:T(2,128)(2,1)}), bf16[4,2,24576]{2,1,0:T(2,128)(2,1)S(1)}, u32[]{:S(2)}, u32[]{:S(2)}) async-start(bf16[4,2,24576]{2,1,0:T(2,128)(2,1)} %reshape.579), calls=%async_computation.1 | async-start | bytes 786432 | tf_op jit(solution)/shard_map/all_to_all | solution.py:230
  198.2 87.9 %copy-start.6 = (f32[256,768]{1,0:T(8,128)}, f32[256,768]{1,0:T(8,128)S(1)}, u32[]{:S(2)}) copy-start(f32[256,768]{1,0:T(8,128)S(1)} %get-tuple-element.514) | copy-start | bytes 2359300
  203.5 33.0 %all-to-all-start.2 = ((bf16[1,256,3,4,192]{1,4,2,0,3:T(8,128)(2,1)}), bf16[1,256,3,4,192]{1,4,2,0,3:T(8,128)(2,1)S(1)}, u32[]{:S(2)}, u32[]{:S(2)}) async-start(bf16[1,256,3,4,192]{1,4,2,0,3:T(8,128)(2,1)} %copy.341), calls=%async_computation.2 | async-start | bytes 2359296 | tf_op jit(solution)/shard_map/all_to_all | solution.py:218
  266.9 17.5 %all-to-all-start.3 = ((bf16[4,2,24576]{2,1,0:T(2,128)(2,1)}), bf16[4,2,24576]{2,1,0:T(2,128)(2,1)S(1)}, u32[]{:S(2)}, u32[]{:S(2)}) async-start(bf16[4,2,24576]{2,1,0:T(2,128)(2,1)} %reshape.581), calls=%async_computation.3 | async-start | bytes 786432 | tf_op jit(solution)/shard_map/all_to_all | solution.py:230
  312.6 15.9 %all-to-all-start.4 = ((bf16[1,256,4,192]{1,3,0,2:T(8,128)(2,1)}), bf16[1,256,4,192]{1,3,0,2:T(8,128)(2,1)S(1)}, u32[]{:S(2)}, u32[]{:S(2)}) async-start(bf16[1,256,4,192]{1,3,0,2:T(8,128)(2,1)} %bitcast.63), calls=%async_computation.4 | async-start | bytes 786432 | tf_op jit(solution)/shard_map/all_to_all | solution.py:302
  376.0 49.8 %all-to-all-start.5 = ((bf16[1,1024,3,1,192]{4,2,3,0,1:T(4,128)(2,1)}), bf16[1,1024,3,1,192]{4,2,3,0,1:T(4,128)(2,1)S(1)}, u32[]{:S(2)}, u32[]{:S(2)}) async-start(bf16[1,1024,3,1,192]{4,2,3,0,1:T(4,128)(2,1)} %copy.352), calls=%async_computation.5 | async-start | bytes 4194304 | tf_op jit(solution)/shard_map/all_to_all | solution.py:316
  379.6 246.6 %reduce-scatter.13.cloned.1.call-start = ((), (), s32[]{:S(2)}) async-start(), calls=%async_computation.19 | async-start | bytes 31850496 | tf_op jit(solution)/shard_map/reduce_scatter | solution.py:74
  405.5 25.7 %copy-start.7 = (f32[256,768]{1,0:T(8,128)S(1)}, f32[256,768]{1,0:T(8,128)}, u32[]{:S(2)}) copy-start(f32[256,768]{1,0:T(8,128)} %copy-done.6) | copy-start | bytes 2359300
  405.5 25.7 %copy-start.68 = (f32[768]{0:T(1024)S(1)}, f32[768]{0:T(1024)}, u32[]{:S(2)}) copy-start(f32[768]{0:T(1024)} %copy-done.67) | copy-start | bytes 9220
  405.5 25.8 %copy-start.75 = (f32[768]{0:T(1024)S(1)}, f32[768]{0:T(1024)}, u32[]{:S(2)}) copy-start(f32[768]{0:T(1024)} %copy-done.74) | copy-start | bytes 9220
  405.5 25.8 %copy-start.84 = (f32[256]{0:T(256)S(1)}, f32[256]{0:T(256)}, u32[]{:S(2)}) copy-start(f32[256]{0:T(256)} %copy-done.83) | copy-start | bytes 3076
  405.5 25.8 %copy-start.95 = (f32[256]{0:T(256)S(1)}, f32[256]{0:T(256)}, u32[]{:S(2)}) copy-start(f32[256]{0:T(256)} %copy-done.94) | copy-start | bytes 3076
  478.3 16.0 %all-to-all-start.6 = ((bf16[1,256,4,192]{1,3,0,2:T(8,128)(2,1)}), bf16[1,256,4,192]{1,3,0,2:T(8,128)(2,1)S(1)}, u32[]{:S(2)}, u32[]{:S(2)}) async-start(bf16[1,256,4,192]{1,3,0,2:T(8,128)(2,1)} %bitcast.74), calls=%async_computation.6 | async-start | bytes 786432 | tf_op jit(solution)/shard_map/all_to_all | solution.py:302
  543.0 52.7 %all-to-all-start.7 = ((bf16[1,1024,3,1,192]{4,2,3,0,1:T(4,128)(2,1)}), bf16[1,1024,3,1,192]{4,2,3,0,1:T(4,128)(2,1)}, u32[]{:S(2)}, u32[]{:S(2)}) async-start(bf16[1,1024,3,1,192]{4,2,3,0,1:T(4,128)(2,1)} %copy.359), calls=%async_computation.7 | async-start | bytes 4194304 | tf_op jit(solution)/shard_map/all_to_all | solution.py:316
  547.5 255.5 %reduce-scatter.9.cloned.1.call-start = ((), (), s32[]{:S(2)}) async-start(), calls=%async_computation.16 | async-start | bytes 31850496 | tf_op jit(solution)/shard_map/reduce_scatter | solution.py:74
  572.0 29.0 %copy-start.14 = (bf16[1,256,768]{2,1,0:T(8,128)(2,1)S(1)}, bf16[1,256,768]{2,1,0:T(8,128)(2,1)}, u32[]{:S(2)}) copy-start(bf16[1,256,768]{2,1,0:T(8,128)(2,1)} %param.19) | copy-start | bytes 1179652
  572.0 29.0 %copy-start.63 = (f32[768]{0:T(1024)S(1)}, f32[768]{0:T(1024)}, u32[]{:S(2)}) copy-start(f32[768]{0:T(1024)} %copy-done.62) | copy-start | bytes 9220
  572.0 29.0 %copy-start.71 = (f32[768]{0:T(1024)S(1)}, f32[768]{0:T(1024)}, u32[]{:S(2)}) copy-start(f32[768]{0:T(1024)} %copy-done.70) | copy-start | bytes 9220
  572.1 29.0 %copy-start.78 = (f32[256]{0:T(256)S(1)}, f32[256]{0:T(256)}, u32[]{:S(2)}) copy-start(f32[256]{0:T(256)} %copy-done.77) | copy-start | bytes 3076
  572.1 29.0 %copy-start.80 = (f32[256]{0:T(256)S(1)}, f32[256]{0:T(256)}, u32[]{:S(2)}) copy-start(f32[256]{0:T(256)} %copy-done.79) | copy-start | bytes 3076
  625.8 218.3 %reduce-scatter.15.cloned.1.call-start = ((), (), s32[]{:S(2)}) async-start(), calls=%async_computation.20 | async-start | bytes 2211840 | tf_op jit(solution)/shard_map/reduce_scatter | solution.py:78
  629.6 250.8 %reduce-scatter.19.cloned.1.call-start = ((), (), s32[]{:S(2)}) async-start(), calls=%async_computation.23 | async-start | bytes 442368 | tf_op jit(solution)/shard_map/reduce_scatter | solution.py:75
  641.6 164.9 %copy-start.115 = (f32[768]{0:T(1024)S(1)}, f32[768]{0:T(1024)}, u32[]{:S(2)}) copy-start(f32[768]{0:T(1024)} %get-tuple-element.348) | copy-start | bytes 9220
  641.6 165.1 %copy-start.114 = (f32[768]{0:T(1024)S(1)}, f32[768]{0:T(1024)}, u32[]{:S(2)}) copy-start(f32[768]{0:T(1024)} %get-tuple-element.356) | copy-start | bytes 9220
  641.6 166.0 %copy-start.89 = (f32[768]{0:T(1024)S(1)}, f32[768]{0:T(1024)}, u32[]{:S(2)}) copy-start(f32[768]{0:T(1024)} %get-tuple-element.453) | copy-start | bytes 9220
  641.6 166.9 %copy-start.88 = (f32[768]{0:T(1024)S(1)}, f32[768]{0:T(1024)}, u32[]{:S(2)}) copy-start(f32[768]{0:T(1024)} %get-tuple-element.451) | copy-start | bytes 9220
  641.6 167.9 %copy-start.98 = (f32[3072]{0:T(1024)S(1)}, f32[3072]{0:T(1024)}, u32[]{:S(2)}) copy-start(f32[3072]{0:T(1024)} %get-tuple-element.522) | copy-start | bytes 36868
  641.6 280.2 %reduce-scatter.11.cloned.1.call-start = ((), (), s32[]{:S(2)}) async-start(), calls=%async_computation.17 | async-start | bytes 2211840 | tf_op jit(solution)/shard_map/reduce_scatter | solution.py:78
  806.5 152.0 %reduce-scatter.17.cloned.1.call-start = ((), (), s32[]{:S(2)}) async-start(), calls=%async_computation.22 | async-start | bytes 442368 | tf_op jit(solution)/shard_map/reduce_scatter | solution.py:75
  817.9 28.3 %copy-start.12 = (f32[256,768]{1,0:T(8,128)S(1)}, f32[256,768]{1,0:T(8,128)}, u32[]{:S(2)}) copy-start(f32[256,768]{1,0:T(8,128)} %copy-done.10) | copy-start | bytes 2359300
  825.9 175.7 %all-gather.15.cloned.1.call-start = ((), (), s32[]{:S(2)}) async-start(), calls=%async_computation.21 | async-start | bytes 2211840 | tf_op jit(solution)/shard_map/all_gather | solution.py:86
  844.2 197.3 %all-gather.13.cloned.1.call-start = ((), (), s32[]{:S(2)}) async-start(), calls=%async_computation.18 | async-start | bytes 2211840 | tf_op jit(solution)/shard_map/all_gather | solution.py:86
  846.2 76.3 %copy-start.23 = (f32[256,768]{1,0:T(8,128)S(1)}, f32[256,768]{1,0:T(8,128)}, u32[]{:S(2)}) copy-start(f32[256,768]{1,0:T(8,128)} %copy-done.22) | copy-start | bytes 2359300
  846.2 76.3 %copy-start.40 = (f32[256,768]{1,0:T(8,128)S(1)}, f32[256,768]{1,0:T(8,128)}, u32[]{:S(2)}) copy-start(f32[256,768]{1,0:T(8,128)} %copy-done.39) | copy-start | bytes 2359300
  846.2 76.3 %copy-start.101 = (f32[256]{0:T(256)S(1)}, f32[256]{0:T(256)}, u32[]{:S(2)}) copy-start(f32[256]{0:T(256)} %copy-done.100) | copy-start | bytes 3076
  (105 other events, 577.6 us)
Sparse Core Ops, SparseCore 0:
  12.5 81.5 all-gather.8
  96.5 78.7 all-gather.10
  454.8 171.3 reduce-scatter.12
  629.7 173.2 reduce-scatter.8
  805.8 38.3 reduce-scatter.14
  847.4 32.9 reduce-scatter.18
  883.4 38.3 reduce-scatter.10
  925.4 32.9 reduce-scatter.16
  960.0 40.9 all-gather.14
  1002.4 39.1 all-gather.12
where the time goes:
time: 1070 us
  waiting for transfers between devices  498 us (47%)
  matrix products  177 us (17%)
  local copies, waits for them, and re-layouts  163 us (15%)
  other arithmetic  101 us (9%)
  blocking collectives  58.2 us (5%)
  starting transfers between devices  35 us (3%)
  between operations  17 us (2%)
  loops' own time  15.4 us (1%)
    reduce_scatter x2, waiting for transfers between devices, settle(): lax.psum_scatter(matrix_grads, 'fsdp', scatter_dimension=0, tiled=True)  162 us
    reduce_scatter x2, waiting for transfers between devices, settle(): lax.psum_scatter(vector_grads, 'fsdp', scatter_dimension=0, tiled=True)  63.2 us
    reduce_scatter x2, waiting for transfers between devices, settle(): lax.psum_scatter(matrix_grads.astype(jnp.bfloat16), 'sp', scatter_dimensi...  58.9 us
    all_gather x2, waiting for transfers between devices, fetch(): lax.all_gather(matrices, 'fsdp', axis=0, tiled=True)  57.2 us
    all_to_all x2, waiting for transfers between devices, local(): lax.all_to_all(projected.reshape(clips, frames, 3, groups, width // group...  56 us
    all_to_all x2, waiting for transfers between devices, local(): lax.all_to_all(stacked, 'sp', split_axis=1, concat_axis=3, tiled=True)  44 us
    concatenate x2, other arithmetic, local(): jnp.concatenate([grad_qkv, grad_out, grad_up, grad_down.reshape(width, hi...  39.8 us
    dot_general x8, matrix products, product(): return jnp.dot(left, right, preferred_element_type=jnp.float32)  39 us
  transfers between devices with their start and end apart: 18, of which 14 were waited for; matrix products, arithmetic and copies ran while one was open for 26% of the time, Pallas kernels for 0%

commit v1 on v0

--- a/solution.py
+++ b/solution.py
@@ -36,60 +36,56 @@
     return jnp.sum(values.astype(jnp.float32), axis=0)
 
 
-def pack_layer(
-    layer_index, w_qkv, w_out, w_up, w_down, norm_gain, norm_shift, qv_bias, branch_bias, up_bias
-):
-    shard = w_out.shape[1]
-    matrices = jnp.concatenate(
-        [
-            w_qkv[layer_index].reshape(shard, -1),
-            w_out[layer_index],
-            w_up[layer_index],
-            w_down[layer_index].reshape(shard, -1),
-        ],
-        axis=1,
-    )
-    vectors = jnp.concatenate(
-        [
-            norm_gain[layer_index].T,
-            norm_shift[layer_index].T,
-            qv_bias[layer_index].T,
-            branch_bias[layer_index].T,
-            up_bias[layer_index].reshape(shard, -1),
-        ],
-        axis=1,
-    )
-    return (matrices, vectors)
-
-
-def fetch(matrices, vectors):
-    return (
-        lax.all_gather(matrices, "fsdp", axis=0, tiled=True),
-        lax.all_gather(vectors, "fsdp", axis=0, tiled=True),
-    )
-
-
-def settle(matrix_grads, vector_grads):
-    matrix_grads, vector_grads = (
-        lax.psum_scatter(matrix_grads, "fsdp", scatter_dimension=0, tiled=True),
-        lax.psum_scatter(vector_grads, "fsdp", scatter_dimension=0, tiled=True),
-    )
-    matrix_grads, vector_grads = (
-        lax.psum_scatter(
-            matrix_grads.astype(jnp.bfloat16), "sp", scatter_dimension=1, tiled=True
-        ).astype(jnp.float32),
-        lax.psum_scatter(
-            vector_grads.astype(jnp.bfloat16), "sp", scatter_dimension=1, tiled=True
-        ).astype(jnp.float32),
-    )
-    return (
-        lax.all_gather(matrix_grads.astype(jnp.bfloat16), "sp", axis=1, tiled=True).astype(
-            matrix_grads.dtype
-        ),
-        lax.all_gather(vector_grads.astype(jnp.bfloat16), "sp", axis=1, tiled=True).astype(
-            vector_grads.dtype
-        ),
-    )
+def gather_rows(shard):
+    return lax.all_gather(shard, "fsdp", axis=0, tiled=True)
+
+
+def log_two(size):
+    return size.bit_length() - 1
+
+
+def exchange_halves(parts, axis_name, bit, axis):
+    size = lax.axis_size(axis_name)
+    mine = (lax.axis_index(axis_name) >> bit) & 1
+    kept = lax.dynamic_index_in_dim(parts, mine, axis, keepdims=False)
+    sent = lax.dynamic_index_in_dim(parts, 1 - mine, axis, keepdims=False)
+    got = lax.ppermute(sent, axis_name, [(i, i ^ (1 << bit)) for i in range(size)])
+    return (kept.astype(jnp.float32) + got.astype(jnp.float32)).astype(jnp.bfloat16)
+
+
+def reduce_owner(grads, order):
+    size = lax.axis_size("fsdp")
+    bits = log_two(size)
+    parts = grads.reshape((2,) * bits + (grads.shape[0] // size, grads.shape[1]))
+    left = list(range(bits - 1, -1, -1))
+    for bit in order:
+        axis = left.index(bit)
+        left.pop(axis)
+        parts = exchange_halves(parts, "fsdp", bit, axis)
+    return parts
+
+
+def reduce_frames(grads, axis):
+    size = lax.axis_size("sp")
+    bits = log_two(size)
+    shape = grads.shape
+    parts = grads.reshape(
+        shape[:axis] + (2,) * bits + (shape[axis] // size,) + shape[axis + 1 :]
+    )
+    for bit in range(bits):
+        parts = exchange_halves(parts, "sp", bit, axis + bits - 1 - bit)
+    return lax.all_gather(parts, "sp", axis=axis, tiled=True)
+
+
+def settle(grads, axis):
+    bits = log_two(lax.axis_size("fsdp"))
+    half = grads.shape[1] // 2
+    forward = [0] + list(range(1, bits))
+    backward = [0] + list(range(bits - 1, 0, -1))
+    low = grads.astype(jnp.bfloat16)
+    first = reduce_owner(low[:, :half], forward)
+    second = reduce_owner(low[:, half:], backward)
+    return reduce_frames(jnp.concatenate([first, second], axis=1), axis)
 
 
 def attend(query_rows, key_rows, value_rows):
@@ -186,25 +182,39 @@
     rows_all = clips * frames
     stream = inputs.astype(jnp.float32).reshape(rows_all, width)
     kept = []
+    shard = w_out.shape[1]
+    vectors = jnp.concatenate(
+        [
+            part
+            for l in range(LAYERS)
+            for part in (
+                norm_gain[l].T,
+                norm_shift[l].T,
+                qv_bias[l].T,
+                branch_bias[l].T,
+                up_bias[l].reshape(shard, -1),
+            )
+        ],
+        axis=1,
+    )
+    count = vectors.shape[1] // LAYERS
+    spare = 128 - vectors.shape[1]
+    first = jnp.concatenate(
+        [w_qkv[0].reshape(shard, -1), jnp.pad(vectors, ((0, 0), (0, spare)))], axis=1
+    )
+    first = gather_rows(first)
+    vectors = first[:, 3 * width :]
     for layer_index in range(LAYERS):
-        matrices, vectors = pack_layer(
-            layer_index,
-            w_qkv,
-            w_out,
-            w_up,
-            w_down,
-            norm_gain,
-            norm_shift,
-            qv_bias,
-            branch_bias,
-            up_bias,
-        )
-        matrices, vectors = fetch(matrices, vectors)
-        weight_qkv = matrices[:, : 3 * width]
-        weight_out = matrices[:, 3 * width : 4 * width]
-        weight_up = matrices[:, 4 * width : 4 * width + hidden]
-        weight_down = matrices[:, 4 * width + hidden :].reshape(hidden, width)
-        vector_full = vectors.astype(jnp.float32)
+        if layer_index == 0:
+            weight_qkv = first[:, : 3 * width]
+        else:
+            weight_qkv = gather_rows(w_qkv[layer_index].reshape(shard, -1))
+        weight_out = gather_rows(w_out[layer_index])
+        weight_up = gather_rows(w_up[layer_index])
+        weight_down = gather_rows(w_down[layer_index])
+        vector_full = vectors[:, layer_index * count : (layer_index + 1) * count].astype(
+            jnp.float32
+        )
         gains = vector_full[:, 0:2]
         shifts = vector_full[:, 2:4]
         attn_bias = vector_full[:, 4:6]
@@ -264,6 +274,7 @@
     output = stream.astype(jnp.bfloat16).reshape(clips, frames, width)
     grad_stream = cotangent.astype(jnp.float32).reshape(rows_all, width)
     layer_grads = []
+    vector_sums = []
     for layer_index in reversed(range(LAYERS)):
         (
             layer_input,
@@ -285,11 +296,11 @@
             activated,
         ) = kept[layer_index]
         grad_branch = grad_stream.astype(jnp.bfloat16)
-        grad_down = outer_sum(activated, grad_branch)
+        grad_down = settle(outer_sum(activated, grad_branch), 0)
         grad_down_bias = column_sums(grad_branch)
         grad_act = product_back(grad_branch, weight_down)
         grad_pre = jax.vjp(gelu_exact, pre_act)[1](grad_act)[0].astype(jnp.bfloat16)
-        grad_up = outer_sum(normed_two, grad_pre)
+        grad_up = settle(outer_sum(normed_two, grad_pre), 1)
         grad_up_bias = column_sums(grad_pre)
         grad_norm_two = product_back(grad_pre, weight_up)
         norm_pull = jax.vjp(norm_rows, middle, gains[:, 1], shifts[:, 1])[1]
@@ -322,9 +333,7 @@
         norm_pull = jax.vjp(norm_rows, layer_input, gains[:, 0], shifts[:, 0])[1]
         grad_input, grad_gain_one, grad_shift_one = norm_pull(grad_norm_one)
         grad_stream = grad_middle + grad_input
-        matrix_grads = jnp.concatenate(
-            [grad_qkv, grad_out, grad_up, grad_down.reshape(width, hidden)], axis=1
-        )
+        grad_attn = settle(jnp.concatenate([grad_qkv, grad_out], axis=1), 1)
         vector_grads = jnp.concatenate(
             [
                 jnp.stack([grad_gain_one, grad_gain_two], axis=1),
@@ -335,17 +344,23 @@
             ],
             axis=1,
         )
-        layer_grads.append(settle(matrix_grads, vector_grads))
+        layer_grads.append((grad_attn, grad_up, grad_down))
+        vector_sums.append(vector_grads)
     layer_grads = layer_grads[::-1]
     grad_inputs = grad_stream.astype(jnp.bfloat16).reshape(clips, frames, width)
-    shard = w_out.shape[1]
     qkv_list, out_list, up_list, down_list = ([], [], [], [])
     gain_list, shift_list, bias_list, branch_list, upbias_list = ([], [], [], [], [])
-    for matrix_part, vector_part in layer_grads:
-        qkv_list.append(matrix_part[:, : 3 * width].reshape(shard, 3, width))
-        out_list.append(matrix_part[:, 3 * width : 4 * width])
-        up_list.append(matrix_part[:, 4 * width : 4 * width + hidden])
-        down_list.append(matrix_part[:, 4 * width + hidden :].reshape(-1, width))
+    vector_sums = lax.psum(jnp.concatenate(vector_sums[::-1], axis=1), ("fsdp", "sp"))
+    vector_sums = lax.dynamic_slice_in_dim(
+        vector_sums, lax.axis_index("fsdp") * shard, shard, 0
+    )
+    for layer_index, (attn_part, up_part, down_part) in enumerate(layer_grads):
+        vector_part = vector_sums[:, layer_index * count : (layer_index + 1) * count]
+        attn_part = attn_part.astype(jnp.float32)
+        qkv_list.append(attn_part[:, : 3 * width].reshape(shard, 3, width))
+        out_list.append(attn_part[:, 3 * width :])
+        up_list.append(up_part.astype(jnp.float32))
+        down_list.append(down_part.astype(jnp.float32))
         gain_list.append(vector_part[:, 0:2].T)
         shift_list.append(vector_part[:, 2:4].T)
         bias_list.append(vector_part[:, 4:6].T)

time: 1070 us -> 1010 us (0.944)
  waiting for transfers between devices: 498 us -> 358 us
  starting transfers between devices: 35 us -> 85.2 us
  blocking collectives: 58.2 us -> 102 us
  matrix products: 177 us -> 148 us
  local copies, waits for them, and re-layouts: 163 us -> 178 us
    reduce_scatter x6 -> x0, waiting for transfers between devices: 284 us -> none  [the longest x2 162 us: settle(): lax.psum_scatter(matrix_grads, 'fsdp', scatter_dimension=0, tiled=True)]
    psum x0 -> x1, waiting for transfers between devices: none -> 115 us  [local(): lax.psum(jnp.concatenate(vector_sums[::-1], axis=1), ('fsdp', 'sp'))]
    all_gather x4 -> x6, blocking collectives: 37.8 us -> 102 us  [reduce_frames(): return lax.all_gather(parts, 'sp', axis=axis, tiled=True)]
    ppermute x0 -> x48, waiting for transfers between devices: none -> 61.3 us  [exchange_halves(): lax.ppermute(sent, axis_name, [(i, i ^ 1 << bit) for i in range(size)])]
    ppermute x0 -> x48, starting transfers between devices: none -> 48 us  [exchange_halves(): lax.ppermute(sent, axis_name, [(i, i ^ 1 << bit) for i in range(size)])]
    concatenate x4 -> x7, other arithmetic: 42.5 us -> 1.82 us  [the longest x1 1.54 us: local(): jnp.concatenate([w_qkv[0].reshape(shard, -1), jnp.pad(vectors, ((0, 0), (...]
    reshape x4, local copies, waits for them, and re-layouts: 40.8 us -> 1.7 us  [reduce_frames(): grads.reshape(shape[:axis] + (2,) * bits + (shape[axis] // size,) + shape...]
    convert_element_type x8 -> x51, other arithmetic: 10.6 us -> 42.5 us  [the longest x48 39.1 us: exchange_halves(): (kept.astype(jnp.float32) + got.astype(jnp.float32)).astype(jnp.bfloat16)]
  transfers between devices with their start and end apart: 18 -> 65, of which waited for: 14 -> 23; matrix products, arithmetic and copies ran while one was open for 26% -> 34% of each run, Pallas kernels for 0% -> 0%
where the time goes in v1:
time: 1010 us; the launch traced here: 998 us
  waiting for transfers between devices  358 us (35%)
  local copies, waits for them, and re-layouts  178 us (18%)
  matrix products  148 us (15%)
  blocking collectives  102 us (10%)
  other arithmetic  93.7 us (9%)
  starting transfers between devices  85.2 us (8%)
  between operations  16.5 us (2%)
  loops' own time  16.1 us (2%)
    psum x1, waiting for transfers between devices, local(): lax.psum(jnp.concatenate(vector_sums[::-1], axis=1), ('fsdp', 'sp'))  115 us
    all_gather x6, blocking collectives, reduce_frames(): return lax.all_gather(parts, 'sp', axis=axis, tiled=True)  102 us
    all_gather x8, waiting for transfers between devices, gather_rows(): return lax.all_gather(shard, 'fsdp', axis=0, tiled=True)  73.7 us
    ppermute x48, waiting for transfers between devices, exchange_halves(): lax.ppermute(sent, axis_name, [(i, i ^ 1 << bit) for i in range(size)])  61.3 us
    all_to_all x2, waiting for transfers between devices, local(): lax.all_to_all(projected.reshape(clips, frames, 3, groups, width // group...  55.9 us
    ppermute x48, starting transfers between devices, exchange_halves(): lax.ppermute(sent, axis_name, [(i, i ^ 1 << bit) for i in range(size)])  48 us
    convert_element_type x48, other arithmetic, exchange_halves(): (kept.astype(jnp.float32) + got.astype(jnp.float32)).astype(jnp.bfloat16)  39.1 us
    dot_general x8, matrix products, product(): return jnp.dot(left, right, preferred_element_type=jnp.float32)  38.7 us
  transfers between devices with their start and end apart: 65, of which 23 were waited for; matrix products, arithmetic and copies ran while one was open for 34% of the time, Pallas kernels for 0%

profile of v1, /device:TPU:0, one launch (start us, length us, event | category | flops | bytes accessed | tf_op | source)
XLA Modules:
  0.0 998.2 jit_solution(7063857683738780620)
XLA Ops:
  28.3 32.2 %all-gather.15.cloned.1.call-done = bf16[768,2432]{1,0:T(8,128)(2,1)} async-done(((bf16[96,2432]{1,0:T(8,128)(2,1)}), bf16[768,2432]{1,0:T(8,128)(2,1)}) %all-gather.15.cloned.1.call-update) | async-done | bytes 3735568 | tf_op jit(solution)/shard_map/all_gather | solution.py:40
  69.4 4.6 all-to-all-start
  75.3 27.6 %all-to-all-done = bf16[1,256,3,4,192]{1,4,2,0,3:T(8,128)(2,1)S(1)} async-done(((bf16[1,256,3,4,192]{1,4,2,0,3:T(8,128)(2,1)}), bf16[1,256,3,4,192]{1,4,2,0,3:T(8,128)(2,1)S(1)}, u32[]{:S(2)}, u32[]{:S(2)}) %all-to-all-start) | async-done | bytes 1179680 | tf_op jit(solution)/shard_map/all_to_all | solution.py:228
  106.4 20.2 %while.54 = (s32[]{:T(128)}, bf16[2,1,512,3,64]{2,4,3,1,0:T(8,128)(2,1)S(1)}, f32[2,1,3,512]{3,2,1,0:T(4,128)}, s32[2]{0:T(128)}, bf16[1,1024,3,64]{1,3,2,0:T(8,...) while((s32[]{:T(128)}, ...), condition=%wide.region_5.6_spmd, body=%wide.region_2.5_spmd.sunk | while | flops 416905728 | bytes 20109480 | solution.py:112
  128.6 4.0 reduce.53
  138.1 10.8 %all-to-all-done.1 = bf16[4,2,24576]{2,1,0:T(2,128)(2,1)S(1)} async-done(((bf16[4,2,24576]{2,1,0:T(2,128)(2,1)}), bf16[4,2,24576]{2,1,0:T(2,128)(2,1)S(1)}, u32[]{:S(2)}, u32[]{:S(2)}) %all-to-all-start.1) | async-done | bytes 393248 | tf_op jit(solution)/shard_map/all_to_all | solution.py:240
  153.0 11.4 %multiply_convert_fusion.3 = (bf16[256,3072]{1,0:T(8,128)(2,1)S(1)}, f32[256,3072]{1,0:T(8,128)}, f32[256,3072]{1,0:T(8,128)}) fusion(f32[3072]{0:T(1024)S(1)} %add.557, bf16[1,768,3072]{2,1,0:T(8,128)(2,1)} %all-gather.21.cloned.1.call-done, f32[256,768]{1,0:T(8,128)S(1)} %get-tuple-element.538, f32[768]{0:T(1024)S(1)} %get-tuple-element.359, ...), kind=kOutput, calls=%fused_computation.151 | convolution fusion | flops 1260847104 | bytes 13389824 | tf_op jit(solution)/shard_map/dot_general | solution.py:24
  164.4 4.3 all-gather.23.cloned.1.call-done
  168.7 3.8 fusion.277
  172.8 31.6 %all-gather.17.cloned.1.call-done = bf16[768,2304]{1,0:T(8,128)(2,1)} async-done(((bf16[96,2304]{1,0:T(8,128)(2,1)}), bf16[768,2304]{1,0:T(8,128)(2,1)}) %all-gather.17.cloned.1.call-update) | async-done | bytes 3538960 | tf_op jit(solution)/shard_map/all_gather | solution.py:40
  204.4 4.2 fusion.115
  211.3 4.6 all-to-all-start.2
  216.6 28.2 %all-to-all-done.2 = bf16[1,256,3,4,192]{1,4,2,0,3:T(8,128)(2,1)S(1)} async-done(((bf16[1,256,3,4,192]{1,4,2,0,3:T(8,128)(2,1)}), bf16[1,256,3,4,192]{1,4,2,0,3:T(8,128)(2,1)S(1)}, u32[]{:S(2)}, u32[]{:S(2)}) %all-to-all-start.2) | async-done | bytes 1179680 | tf_op jit(solution)/shard_map/all_to_all | solution.py:228
  250.4 19.1 %while.55 = (s32[]{:T(128)}, bf16[2,1,512,3,64]{2,4,3,1,0:T(8,128)(2,1)S(1)}, f32[2,1,3,512]{3,2,1,0:T(4,128)S(1)}, s32[2]{0:T(128)}, bf16[1,1024,3,64]{1,3,2,0:...) while((s32[]{:T(128)}, ...), condition=%wide.region_13.14_spmd, body=%wide.region_10.13_spmd.sunk | while | flops 416905728 | bytes 20113576 | solution.py:112
  271.0 4.0 reduce.54
  276.4 3.8 all-to-all-start.3
  280.7 10.8 %all-to-all-done.3 = bf16[4,2,24576]{2,1,0:T(2,128)(2,1)S(1)} async-done(((bf16[4,2,24576]{2,1,0:T(2,128)(2,1)}), bf16[4,2,24576]{2,1,0:T(2,128)(2,1)S(1)}, u32[]{:S(2)}, u32[]{:S(2)}) %all-to-all-start.3) | async-done | bytes 393248 | tf_op jit(solution)/shard_map/all_to_all | solution.py:240
  295.5 12.1 %multiply_convert_fusion.2 = (bf16[256,3072]{1,0:T(8,128)(2,1)}, f32[256,3072]{1,0:T(8,128)}, f32[256,3072]{1,0:T(8,128)}) fusion(f32[3072]{0:T(1024)S(1)} %add.578, bf16[1,768,3072]{2,1,0:T(8,128)(2,1)} %all-gather.27.cloned.1.call-done, f32[256,768]{1,0:T(8,128)S(1)} %get-tuple-element.543, f32[768]{0:T(1024)S(1)} %copy-done.99, f32[768]{0:T(1024)S(1)} %copy-done.92, ...), kind=kOutput, calls=%fused_computation.138 | convolution fusion | flops 1260847104 | bytes 13389824 | tf_op jit(solution)/shard_map/dot_general | solution.py:24
  307.6 5.5 all-gather.29.cloned.1.call-done
  313.1 6.8 convert_reduce_fusion
  320.0 3.8 convolution_convert_fusion.2
  329.3 5.0 all-to-all-start.4
  334.3 4.1 fusion.262
  358.7 40.0 %while.56 = (s32[]{:T(128)}, f32[1,1024,3,64]{1,3,2,0:T(8,128)}, f32[1,1024,3,64]{1,3,2,0:T(8,128)}, bf16[2,1,512,3,64]{2,4,3,1,0:T(8,128)(2,1)}, s32[2]{0:T(128...) while((s32[]{:T(128)}, f32[1,1024,3,64]{1,3,2,0:T(8,128)}, ...), condition=%wide.region_20.21_spmd.clone, body=%wide.region_18.20_spmd.clone.sunk | while | flops 1026685440 | bytes 106113400 | solution.py:159
  365.0 3.7 multiply_reduce_fusion.19
  405.4 5.2 all-to-all-start.5
  429.7 29.1 %all-to-all-done.5 = bf16[1,1024,3,1,192]{4,2,3,0,1:T(4,128)(2,1)S(1)} async-done(((bf16[1,1024,3,1,192]{4,2,3,0,1:T(4,128)(2,1)}), bf16[1,1024,3,1,192]{4,2,3,0,1:T(4,128)(2,1)S(1)}, u32[]{:S(2)}, u32[]{:S(2)}) %all-to-all-start.5) | async-done | bytes 1179680 | tf_op jit(solution)/shard_map/all_to_all | solution.py:327
  468.8 3.9 convolution_convert_fusion.1
  486.6 4.3 all-to-all-start.6
  524.9 39.5 %while.57 = (s32[]{:T(128)}, f32[1,1024,3,64]{1,3,2,0:T(8,128)}, f32[1,1024,3,64]{1,3,2,0:T(8,128)}, bf16[2,1,512,3,64]{2,4,3,1,0:T(8,128)(2,1)}, s32[2]{0:T(128...) while((s32[]{:T(128)}, f32[1,1024,3,64]{1,3,2,0:T(8,128)}, ...), condition=%wide.region_27.28_spmd.clone, body=%wide.region_25.27_spmd.clone.sunk | while | flops 1026685440 | bytes 106015048 | solution.py:159
  531.0 3.7 multiply_reduce_fusion.20
  571.1 5.2 all-to-all-start.7
  592.0 4.5 collective-permute-done.12
  600.4 8.7 collective-permute-done.20
  613.1 11.8 %collective-permute-done.41 = bf16[2,384,384]{2,1,0:T(8,128)(2,1)S(1)} collective-permute-done((bf16[2,384,384]{2,1,0:T(8,128)(2,1)S(1)}, bf16[2,384,384]{2,1,0:T(8,128)(2,1)S(1)}, u32[]{:S(2)}, u32[]{:S(2)}) %collective-permute-start.41) | collective-permute-done | bytes 589856 | tf_op jit(solution)/shard_map/ppermute | solution.py:52
  628.9 8.6 collective-permute-done.33
  644.8 5.4 collective-permute-done.21
  666.6 4.1 copy.460
  700.5 4.0 concatenate.55
  708.0 115.4 %all-reduce.3.cloned.1.call-done = f32[768,24]{0,1:T(8,128)} async-done(((f32[768,24]{0,1:T(8,128)}), f32[768,24]{0,1:T(8,128)}) %all-reduce.3.cloned.1.call-update) | async-done | bytes 73744 | tf_op jit(solution)/shard_map/psum | solution.py:353
  831.6 18.1 %all_gather.53 = bf16[96,3072]{1,0:T(8,128)(2,1)S(1)} all-gather(bf16[96,768]{1,0:T(8,128)(2,1)S(1)} %fusion.238), channel_id=1, replica_groups=mesh['fsdp'=8,'sp'=4] {'sp'}, dimensions={1}, use_global_device_ids=true | all-gather | bytes 737280 | tf_op jit(solution)/shard_map/all_gather | solution.py:77
  850.6 19.7 %all_gather.55 = bf16[384,768]{1,0:T(8,128)(2,1)S(1)} all-gather(bf16[96,768]{1,0:T(8,128)(2,1)S(1)} %fusion.236), channel_id=1, replica_groups=mesh['fsdp'=8,'sp'=4] {'sp'}, dimensions={0}, use_global_device_ids=true | all-gather | bytes 737280 | tf_op jit(solution)/shard_map/all_gather | solution.py:77
  870.3 16.3 %all_gather.54 = bf16[384,768]{1,0:T(8,128)(2,1)S(1)} all-gather(bf16[96,768]{1,0:T(8,128)(2,1)S(1)} %fusion.237), channel_id=1, replica_groups=mesh['fsdp'=8,'sp'=4] {'sp'}, dimensions={0}, use_global_device_ids=true | all-gather | bytes 737280 | tf_op jit(solution)/shard_map/all_gather | solution.py:77
  888.3 15.2 %all_gather.52 = bf16[96,3072]{1,0:T(8,128)(2,1)S(1)} all-gather(bf16[96,768]{1,0:T(8,128)(2,1)S(1)} %fusion.234), channel_id=1, replica_groups=mesh['fsdp'=8,'sp'=4] {'sp'}, dimensions={1}, use_global_device_ids=true | all-gather | bytes 737280 | tf_op jit(solution)/shard_map/all_gather | solution.py:77
  912.3 7.7 collective-permute-done.9
  943.0 6.3 collective-permute-done.6
  950.4 17.9 %all_gather.51 = bf16[96,3072]{1,0:T(8,128)(2,1)S(1)} all-gather(bf16[96,768]{1,0:T(8,128)(2,1)S(1)} %fusion.239), channel_id=1, replica_groups=mesh['fsdp'=8,'sp'=4] {'sp'}, dimensions={1}, use_global_device_ids=true | all-gather | bytes 737280 | tf_op jit(solution)/shard_map/all_gather | solution.py:77
  969.5 14.9 %all_gather.50 = bf16[96,3072]{1,0:T(8,128)(2,1)S(1)} all-gather(bf16[96,768]{1,0:T(8,128)(2,1)S(1)} %fusion.235), channel_id=1, replica_groups=mesh['fsdp'=8,'sp'=4] {'sp'}, dimensions={1}, use_global_device_ids=true | all-gather | bytes 737280 | tf_op jit(solution)/shard_map/all_gather | solution.py:77
  (802 shorter events, 408.6 us)
Async XLA Ops:
  7.2 53.3 %all-gather.15.cloned.1.call-start = ((), (), s32[]{:S(2)}) async-start(), calls=%async_computation.8 | async-start | bytes 4202496 | tf_op jit(solution)/shard_map/all_gather | solution.py:40
  22.9 127.8 %all-gather.19.cloned.1.call-start = ((), (), s32[]{:S(2)}) async-start(), calls=%async_computation.11 | async-start | bytes 1327104 | tf_op jit(solution)/shard_map/all_gather | solution.py:40
  23.7 129.3 %all-gather.21.cloned.1.call-start = ((), (), s32[]{:S(2)}) async-start(), calls=%async_computation.12 | async-start | bytes 5308416 | tf_op jit(solution)/shard_map/all_gather | solution.py:40
  24.8 143.8 %all-gather.23.cloned.1.call-start = ((), (), s32[]{:S(2)}) async-start(), calls=%async_computation.13 | async-start | bytes 5308416 | tf_op jit(solution)/shard_map/all_gather | solution.py:40
  26.0 178.4 %all-gather.17.cloned.1.call-start = ((), (), s32[]{:S(2)}) async-start(), calls=%async_computation.9 | async-start | bytes 3981312 | tf_op jit(solution)/shard_map/all_gather | solution.py:40
  27.3 265.9 %all-gather.25.cloned.1.call-start = ((), (), s32[]{:S(2)}) async-start(), calls=%async_computation.14 | async-start | bytes 1327104 | tf_op jit(solution)/shard_map/all_gather | solution.py:40
  69.4 33.6 %all-to-all-start = ((bf16[1,256,3,4,192]{1,4,2,0,3:T(8,128)(2,1)}), bf16[1,256,3,4,192]{1,4,2,0,3:T(8,128)(2,1)S(1)}, u32[]{:S(2)}, u32[]{:S(2)}) async-start(bf16[1,256,3,4,192]{1,4,2,0,3:T(8,128)(2,1)} %copy.391), calls=%async_computation | async-start | bytes 2359296 | tf_op jit(solution)/shard_map/all_to_all | solution.py:228
  74.0 221.5 %all-gather.27.cloned.1.call-start = ((), (), s32[]{:S(2)}) async-start(), calls=%async_computation.15 | async-start | bytes 5308416 | tf_op jit(solution)/shard_map/all_gather | solution.py:40
  211.3 33.6 %all-to-all-start.2 = ((bf16[1,256,3,4,192]{1,4,2,0,3:T(8,128)(2,1)}), bf16[1,256,3,4,192]{1,4,2,0,3:T(8,128)(2,1)S(1)}, u32[]{:S(2)}, u32[]{:S(2)}) async-start(bf16[1,256,3,4,192]{1,4,2,0,3:T(8,128)(2,1)} %copy.399), calls=%async_computation.2 | async-start | bytes 2359296 | tf_op jit(solution)/shard_map/all_to_all | solution.py:228
  215.9 97.2 %all-gather.29.cloned.1.call-start = ((), (), s32[]{:S(2)}) async-start(), calls=%async_computation.16 | async-start | bytes 5308416 | tf_op jit(solution)/shard_map/all_gather | solution.py:40
  329.3 19.8 %all-to-all-start.4 = ((bf16[1,256,4,192]{1,3,0,2:T(8,128)(2,1)}), bf16[1,256,4,192]{1,3,0,2:T(8,128)(2,1)S(1)}, u32[]{:S(2)}, u32[]{:S(2)}) async-start(bf16[1,256,4,192]{1,3,0,2:T(8,128)(2,1)} %bitcast.62), calls=%async_computation.4 | async-start | bytes 786432 | tf_op jit(solution)/shard_map/all_to_all | solution.py:313
  353.3 61.1 %collective-permute-start.28 = (bf16[2,96,1536]{2,1,0:T(8,128)(2,1)}, bf16[2,96,1536]{2,1,0:T(8,128)(2,1)}, u32[]{:S(2)}, u32[]{:S(2)}) collective-permute-start(bf16[2,96,1536]{2,1,0:T(8,128)(2,1)} %dynamic-slice_bitcast_fusion.12), channel_id=1, source_target_pairs={{0,16},{4,20},{8,24},{12,28},{16,0},{20,4},{24,8},{28,12},{1,17},{... | collective-permute-start | bytes 1769480 | tf_op jit(solution)/shard_map/ppermute | solution.py:52
  357.2 53.5 %collective-permute-start.44 = (bf16[2,384,384]{2,1,0:T(8,128)(2,1)}, bf16[2,384,384]{2,1,0:T(8,128)(2,1)}, u32[]{:S(2)}, u32[]{:S(2)}) collective-permute-start(bf16[2,384,384]{2,1,0:T(8,128)(2,1)} %dynamic-slice_bitcast_fusion.8), channel_id=1, source_target_pairs={{0,16},{4,20},{8,24},{12,28},{16,0},{20,4},{24,8},{28,12},{1,17},{... | collective-permute-start | bytes 1769480 | tf_op jit(solution)/shard_map/ppermute | solution.py:52
  405.4 53.5 %all-to-all-start.5 = ((bf16[1,1024,3,1,192]{4,2,3,0,1:T(4,128)(2,1)}), bf16[1,1024,3,1,192]{4,2,3,0,1:T(4,128)(2,1)S(1)}, u32[]{:S(2)}, u32[]{:S(2)}) async-start(bf16[1,1024,3,1,192]{4,2,3,0,1:T(4,128)(2,1)} %copy.409), calls=%async_computation.5 | async-start | bytes 4194304 | tf_op jit(solution)/shard_map/all_to_all | solution.py:327
  486.6 35.3 %all-to-all-start.6 = ((bf16[1,256,4,192]{1,3,0,2:T(8,128)(2,1)}), bf16[1,256,4,192]{1,3,0,2:T(8,128)(2,1)}, u32[]{:S(2)}, u32[]{:S(2)}) async-start(bf16[1,256,4,192]{1,3,0,2:T(8,128)(2,1)} %bitcast.877), calls=%async_computation.6 | async-start | bytes 786432 | tf_op jit(solution)/shard_map/all_to_all | solution.py:313
  496.4 81.9 %collective-permute-start.11 = (bf16[2,2,96,1536]{3,2,1,0:T(8,128)(2,1)}, bf16[2,2,96,1536]{3,2,1,0:T(8,128)(2,1)}, u32[]{:S(2)}, u32[]{:S(2)}) collective-permute-start(bf16[2,2,96,1536]{3,2,1,0:T(8,128)(2,1)} %dynamic-slice_bitcast_fusion.6), channel_id=1, source_target_pairs={{0,4},{4,0},{8,12},{12,8},{16,20},{20,16},{24,28},{28,24},{1,5},{5... | collective-permute-start | bytes 3538952 | tf_op jit(solution)/shard_map/ppermute | solution.py:52
  502.4 73.9 %collective-permute-start.24 = (bf16[2,2,96,1536]{3,2,0,1:T(8,128)(2,1)}, bf16[2,2,96,1536]{3,2,0,1:T(8,128)(2,1)}, u32[]{:S(2)}, u32[]{:S(2)}) collective-permute-start(bf16[2,2,96,1536]{3,2,0,1:T(8,128)(2,1)} %bitcast.736), channel_id=1, source_target_pairs={{0,4},{4,0},{8,12},{12,8},{16,20},{20,16},{24,28},{28,24},{1,5},{5... | collective-permute-start | bytes 3538952 | tf_op jit(solution)/shard_map/ppermute | solution.py:52
  503.7 79.6 %collective-permute-start.19 = (bf16[2,2,96,1536]{3,2,1,0:T(8,128)(2,1)}, bf16[2,2,96,1536]{3,2,1,0:T(8,128)(2,1)}, u32[]{:S(2)}, u32[]{:S(2)}) collective-permute-start(bf16[2,2,96,1536]{3,2,1,0:T(8,128)(2,1)} %dynamic-slice_bitcast_fusion.5), channel_id=1, source_target_pairs={{0,4},{4,0},{8,12},{12,8},{16,20},{20,16},{24,28},{28,24},{1,5},{5... | collective-permute-start | bytes 3538952 | tf_op jit(solution)/shard_map/ppermute | solution.py:52
  505.2 75.1 %collective-permute-start.16 = (bf16[2,2,96,1536]{3,2,0,1:T(8,128)(2,1)}, bf16[2,2,96,1536]{3,2,0,1:T(8,128)(2,1)}, u32[]{:S(2)}, u32[]{:S(2)}) collective-permute-start(bf16[2,2,96,1536]{3,2,0,1:T(8,128)(2,1)} %bitcast.737), channel_id=1, source_target_pairs={{0,4},{4,0},{8,12},{12,8},{16,20},{20,16},{24,28},{28,24},{1,5},{5... | collective-permute-start | bytes 3538952 | tf_op jit(solution)/shard_map/ppermute | solution.py:52
  510.1 77.6 %collective-permute-start.40 = (bf16[2,2,384,384]{3,2,0,1:T(8,128)(2,1)}, bf16[2,2,384,384]{3,2,0,1:T(8,128)(2,1)}, u32[]{:S(2)}, u32[]{:S(2)}) collective-permute-start(bf16[2,2,384,384]{3,2,0,1:T(8,128)(2,1)} %bitcast.734), channel_id=1, source_target_pairs={{0,4},{4,0},{8,12},{12,8},{16,20},{20,16},{24,28},{28,24},{1,5},{5... | collective-permute-start | bytes 3538952 | tf_op jit(solution)/shard_map/ppermute | solution.py:52
  571.1 95.5 %all-to-all-start.7 = ((bf16[1,1024,3,1,192]{4,2,3,0,1:T(4,128)(2,1)}), bf16[1,1024,3,1,192]{4,2,3,0,1:T(4,128)(2,1)}, u32[]{:S(2)}, u32[]{:S(2)}) async-start(bf16[1,1024,3,1,192]{4,2,3,0,1:T(4,128)(2,1)} %copy.416), calls=%async_computation.7 | async-start | bytes 4194304 | tf_op jit(solution)/shard_map/all_to_all | solution.py:327
  576.3 247.1 %all-reduce.3.cloned.1.call-start = ((), (), s32[]{:S(2)}) async-start(), calls=%async_computation.10 | async-start | bytes 147456 | tf_op jit(solution)/shard_map/psum | solution.py:353
  580.3 16.2 %collective-permute-start.12 = (bf16[2,96,1536]{2,1,0:T(8,128)(2,1)S(1)}, bf16[2,96,1536]{2,1,0:T(8,128)(2,1)S(1)}, u32[]{:S(2)}, u32[]{:S(2)}) collective-permute-start(bf16[2,96,1536]{2,1,0:T(8,128)(2,1)S(1)} %dynamic-slice_bitcast_fusion.16), channel_id=1, source_target_pairs={{0,16},{4,20},{8,24},{12,28},{16,0},{20,4},{24,8},{28,12},{1,17},{... | collective-permute-start | bytes 1769480 | tf_op jit(solution)/shard_map/ppermute | solution.py:52
  583.3 16.3 %collective-permute-start.25 = (bf16[2,96,1536]{2,1,0:T(8,128)(2,1)S(1)}, bf16[2,96,1536]{2,1,0:T(8,128)(2,1)S(1)}, u32[]{:S(2)}, u32[]{:S(2)}) collective-permute-start(bf16[2,96,1536]{2,1,0:T(8,128)(2,1)S(1)} %dynamic-slice_bitcast_fusion.13), channel_id=1, source_target_pairs={{0,8},{4,12},{8,0},{12,4},{16,24},{20,28},{24,16},{28,20},{1,9},{5... | collective-permute-start | bytes 1769480 | tf_op jit(solution)/shard_map/ppermute | solution.py:52
  585.8 23.3 %collective-permute-start.20 = (bf16[2,96,1536]{2,1,0:T(8,128)(2,1)S(1)}, bf16[2,96,1536]{2,1,0:T(8,128)(2,1)S(1)}, u32[]{:S(2)}, u32[]{:S(2)}) collective-permute-start(bf16[2,96,1536]{2,1,0:T(8,128)(2,1)S(1)} %dynamic-slice_bitcast_fusion.14), channel_id=1, source_target_pairs={{0,16},{4,20},{8,24},{12,28},{16,0},{20,4},{24,8},{28,12},{1,17},{... | collective-permute-start | bytes 1769480 | tf_op jit(solution)/shard_map/ppermute | solution.py:52
  587.7 24.5 %collective-permute-start.17 = (bf16[2,96,1536]{2,1,0:T(8,128)(2,1)S(1)}, bf16[2,96,1536]{2,1,0:T(8,128)(2,1)S(1)}, u32[]{:S(2)}, u32[]{:S(2)}) collective-permute-start(bf16[2,96,1536]{2,1,0:T(8,128)(2,1)S(1)} %dynamic-slice_bitcast_fusion.15), channel_id=1, source_target_pairs={{0,8},{4,12},{8,0},{12,4},{16,24},{20,28},{24,16},{28,20},{1,9},{5... | collective-permute-start | bytes 1769480 | tf_op jit(solution)/shard_map/ppermute | solution.py:52
  590.1 34.7 %collective-permute-start.41 = (bf16[2,384,384]{2,1,0:T(8,128)(2,1)S(1)}, bf16[2,384,384]{2,1,0:T(8,128)(2,1)S(1)}, u32[]{:S(2)}, u32[]{:S(2)}) collective-permute-start(bf16[2,384,384]{2,1,0:T(8,128)(2,1)S(1)} %dynamic-slice_bitcast_fusion.9), channel_id=1, source_target_pairs={{0,8},{4,12},{8,0},{12,4},{16,24},{20,28},{24,16},{28,20},{1,9},{5... | collective-permute-start | bytes 1769480 | tf_op jit(solution)/shard_map/ppermute | solution.py:52
  596.5 30.7 %collective-permute-start.36 = (bf16[2,384,384]{2,1,0:T(8,128)(2,1)S(1)}, bf16[2,384,384]{2,1,0:T(8,128)(2,1)S(1)}, u32[]{:S(2)}, u32[]{:S(2)}) collective-permute-start(bf16[2,384,384]{2,1,0:T(8,128)(2,1)S(1)} %dynamic-slice_bitcast_fusion.10), channel_id=1, source_target_pairs={{0,16},{4,20},{8,24},{12,28},{16,0},{20,4},{24,8},{28,12},{1,17},{... | collective-permute-start | bytes 1769480 | tf_op jit(solution)/shard_map/ppermute | solution.py:52
  599.6 37.9 %collective-permute-start.33 = (bf16[2,384,384]{2,1,0:T(8,128)(2,1)S(1)}, bf16[2,384,384]{2,1,0:T(8,128)(2,1)S(1)}, u32[]{:S(2)}, u32[]{:S(2)}) collective-permute-start(bf16[2,384,384]{2,1,0:T(8,128)(2,1)S(1)} %dynamic-slice_bitcast_fusion.11), channel_id=1, source_target_pairs={{0,8},{4,12},{8,0},{12,4},{16,24},{20,28},{24,16},{28,20},{1,9},{5... | collective-permute-start | bytes 1769480 | tf_op jit(solution)/shard_map/ppermute | solution.py:52
  609.2 56.4 %collective-permute-start.13 = (bf16[96,1536]{1,0:T(8,128)(2,1)}, bf16[96,1536]{1,0:T(8,128)(2,1)}, u32[]{:S(2)}, u32[]{:S(2)}) collective-permute-start(bf16[96,1536]{1,0:T(8,128)(2,1)} %dynamic-slice_bitcast_fusion.30), channel_id=1, source_target_pairs={{0,8},{4,12},{8,0},{12,4},{16,24},{20,28},{24,16},{28,20},{1,9},{5... | collective-permute-start | bytes 884744 | tf_op jit(solution)/shard_map/ppermute | solution.py:52
  612.2 27.7 %collective-permute-start.26 = (bf16[96,1536]{1,0:T(8,128)(2,1)S(1)}, bf16[96,1536]{1,0:T(8,128)(2,1)S(1)}, u32[]{:S(2)}, u32[]{:S(2)}) collective-permute-start(bf16[96,1536]{1,0:T(8,128)(2,1)S(1)} %dynamic-slice_bitcast_fusion.27), channel_id=1, source_target_pairs={{0,16},{4,20},{8,24},{12,28},{16,0},{20,4},{24,8},{28,12},{1,17},{... | collective-permute-start | bytes 884744 | tf_op jit(solution)/shard_map/ppermute | solution.py:52
  624.8 25.4 %collective-permute-start.21 = (bf16[96,1536]{1,0:T(8,128)(2,1)}, bf16[96,1536]{1,0:T(8,128)(2,1)}, u32[]{:S(2)}, u32[]{:S(2)}) collective-permute-start(bf16[96,1536]{1,0:T(8,128)(2,1)} %dynamic-slice_bitcast_fusion.28), channel_id=1, source_target_pairs={{0,8},{4,12},{8,0},{12,4},{16,24},{20,28},{24,16},{28,20},{1,9},{5... | collective-permute-start | bytes 884744 | tf_op jit(solution)/shard_map/ppermute | solution.py:52
  627.2 24.7 %collective-permute-start.18 = (bf16[96,1536]{1,0:T(8,128)(2,1)}, bf16[96,1536]{1,0:T(8,128)(2,1)}, u32[]{:S(2)}, u32[]{:S(2)}) collective-permute-start(bf16[96,1536]{1,0:T(8,128)(2,1)} %dynamic-slice_bitcast_fusion.29), channel_id=1, source_target_pairs={{0,16},{4,20},{8,24},{12,28},{16,0},{20,4},{24,8},{28,12},{1,17},{... | collective-permute-start | bytes 884744 | tf_op jit(solution)/shard_map/ppermute | solution.py:52
  637.5 20.3 %collective-permute-start.42 = (bf16[384,384]{1,0:T(8,128)(2,1)}, bf16[384,384]{1,0:T(8,128)(2,1)}, u32[]{:S(2)}, u32[]{:S(2)}) collective-permute-start(bf16[384,384]{1,0:T(8,128)(2,1)} %dynamic-slice_bitcast_fusion.22), channel_id=1, source_target_pairs={{0,16},{4,20},{8,24},{12,28},{16,0},{20,4},{24,8},{28,12},{1,17},{... | collective-permute-start | bytes 884744 | tf_op jit(solution)/shard_map/ppermute | solution.py:52
  639.9 19.8 %collective-permute-start.37 = (bf16[384,384]{1,0:T(8,128)(2,1)}, bf16[384,384]{1,0:T(8,128)(2,1)}, u32[]{:S(2)}, u32[]{:S(2)}) collective-permute-start(bf16[384,384]{1,0:T(8,128)(2,1)} %dynamic-slice_bitcast_fusion.24), channel_id=1, source_target_pairs={{0,8},{4,12},{8,0},{12,4},{16,24},{20,28},{24,16},{28,20},{1,9},{5... | collective-permute-start | bytes 884744 | tf_op jit(solution)/shard_map/ppermute | solution.py:52
  652.0 35.2 %collective-permute-start.30 = (bf16[96,2,768]{2,0,1:T(8,128)(2,1)}, bf16[96,2,768]{2,0,1:T(8,128)(2,1)}, u32[]{:S(2)}, u32[]{:S(2)}) collective-permute-start(bf16[96,2,768]{2,0,1:T(8,128)(2,1)} %bitcast.740), channel_id=1, source_target_pairs={{0,1},{1,0},{2,3},{3,2},{4,5},{5,4},{6,7},{7,6},{8,9},{9,8},{10,11... | collective-permute-start | bytes 884744 | tf_op jit(solution)/shard_map/ppermute | solution.py:52
  657.7 25.0 %collective-permute-start.22 = (bf16[96,2,768]{2,1,0:T(2,128)(2,1)}, bf16[96,2,768]{2,1,0:T(2,128)(2,1)}, u32[]{:S(2)}, u32[]{:S(2)}) collective-permute-start(bf16[96,2,768]{2,1,0:T(2,128)(2,1)} %copy.435), channel_id=1, source_target_pairs={{0,1},{1,0},{2,3},{3,2},{4,5},{5,4},{6,7},{7,6},{8,9},{9,8},{10,11... | collective-permute-start | bytes 884744 | tf_op jit(solution)/shard_map/ppermute | solution.py:52
  659.7 30.0 %collective-permute-start.46 = (bf16[2,96,768]{2,1,0:T(8,128)(2,1)}, bf16[2,96,768]{2,1,0:T(8,128)(2,1)}, u32[]{:S(2)}, u32[]{:S(2)}) collective-permute-start(bf16[2,96,768]{2,1,0:T(8,128)(2,1)} %dynamic-slice_bitcast_fusion.20), channel_id=1, source_target_pairs={{0,1},{1,0},{2,3},{3,2},{4,5},{5,4},{6,7},{7,6},{8,9},{9,8},{10,11... | collective-permute-start | bytes 884744 | tf_op jit(solution)/shard_map/ppermute | solution.py:52
  665.5 41.4 %collective-permute-start.38 = (bf16[2,96,768]{2,1,0:T(8,128)(2,1)}, bf16[2,96,768]{2,1,0:T(8,128)(2,1)}, u32[]{:S(2)}, u32[]{:S(2)}) collective-permute-start(bf16[2,96,768]{2,1,0:T(8,128)(2,1)} %dynamic-slice_bitcast_fusion.23), channel_id=1, source_target_pairs={{0,1},{1,0},{2,3},{3,2},{4,5},{5,4},{6,7},{7,6},{8,9},{9,8},{10,11... | collective-permute-start | bytes 884744 | tf_op jit(solution)/shard_map/ppermute | solution.py:52
  680.0 225.0 %collective-permute-start.8 = (bf16[2,2,96,1536]{3,2,0,1:T(8,128)(2,1)}, bf16[2,2,96,1536]{3,2,0,1:T(8,128)(2,1)}, u32[]{:S(2)}, u32[]{:S(2)}) collective-permute-start(bf16[2,2,96,1536]{3,2,0,1:T(8,128)(2,1)} %bitcast.738), channel_id=1, source_target_pairs={{0,4},{4,0},{8,12},{12,8},{16,20},{20,16},{24,28},{28,24},{1,5},{5... | collective-permute-start | bytes 3538952 | tf_op jit(solution)/shard_map/ppermute | solution.py:52
  682.7 224.7 %collective-permute-start.3 = (bf16[2,2,96,1536]{3,2,1,0:T(8,128)(2,1)}, bf16[2,2,96,1536]{3,2,1,0:T(8,128)(2,1)}, u32[]{:S(2)}, u32[]{:S(2)}) collective-permute-start(bf16[2,2,96,1536]{3,2,1,0:T(8,128)(2,1)} %dynamic-slice_bitcast_fusion.7), channel_id=1, source_target_pairs={{0,4},{4,0},{8,12},{12,8},{16,20},{20,16},{24,28},{28,24},{1,5},{5... | collective-permute-start | bytes 3538952 | tf_op jit(solution)/shard_map/ppermute | solution.py:52
  687.2 222.1 %collective-permute-start = (bf16[2,2,96,1536]{3,2,0,1:T(8,128)(2,1)}, bf16[2,2,96,1536]{3,2,0,1:T(8,128)(2,1)}, u32[]{:S(2)}, u32[]{:S(2)}) collective-permute-start(bf16[2,2,96,1536]{3,2,0,1:T(8,128)(2,1)} %bitcast.739), channel_id=1, source_target_pairs={{0,4},{4,0},{8,12},{12,8},{16,20},{20,16},{24,28},{28,24},{1,5},{5... | collective-permute-start | bytes 3538952 | tf_op jit(solution)/shard_map/ppermute | solution.py:52
  689.7 137.7 %collective-permute-start.31 = (bf16[96,768]{1,0:T(8,128)(2,1)}, bf16[96,768]{1,0:T(8,128)(2,1)}, u32[]{:S(2)}, u32[]{:S(2)}) collective-permute-start(bf16[96,768]{1,0:T(8,128)(2,1)} %dynamic-slice_bitcast_fusion.36), channel_id=1, source_target_pairs={{0,2},{1,3},{2,0},{3,1},{4,6},{5,7},{6,4},{7,5},{8,10},{9,11},{10,... | collective-permute-start | bytes 442376 | tf_op jit(solution)/shard_map/ppermute | solution.py:52
  706.9 181.4 %collective-permute-start.23 = (bf16[96,768]{1,0:T(8,128)(2,1)}, bf16[96,768]{1,0:T(8,128)(2,1)S(1)}, u32[]{:S(2)}, u32[]{:S(2)}) collective-permute-start(bf16[96,768]{1,0:T(8,128)(2,1)} %bitcast.744), channel_id=1, source_target_pairs={{0,2},{1,3},{2,0},{3,1},{4,6},{5,7},{6,4},{7,5},{8,10},{9,11},{10,... | collective-permute-start | bytes 442376 | tf_op jit(solution)/shard_map/ppermute | solution.py:52
  827.4 22.3 %collective-permute-start.47 = (bf16[96,768]{1,0:T(8,128)(2,1)}, bf16[96,768]{1,0:T(8,128)(2,1)S(1)}, u32[]{:S(2)}, u32[]{:S(2)}) collective-permute-start(bf16[96,768]{1,0:T(8,128)(2,1)} %dynamic-slice_bitcast_fusion.34), channel_id=1, source_target_pairs={{0,2},{1,3},{2,0},{3,1},{4,6},{5,7},{6,4},{7,5},{8,10},{9,11},{10,... | collective-permute-start | bytes 442376 | tf_op jit(solution)/shard_map/ppermute | solution.py:52
  849.7 20.6 %collective-permute-start.39 = (bf16[96,768]{1,0:T(8,128)(2,1)S(1)}, bf16[96,768]{1,0:T(8,128)(2,1)S(1)}, u32[]{:S(2)}, u32[]{:S(2)}) collective-permute-start(bf16[96,768]{1,0:T(8,128)(2,1)S(1)} %dynamic-slice_bitcast_fusion.35), channel_id=1, source_target_pairs={{0,2},{1,3},{2,0},{3,1},{4,6},{5,7},{6,4},{7,5},{8,10},{9,11},{10,... | collective-permute-start | bytes 442376 | tf_op jit(solution)/shard_map/ppermute | solution.py:52
  911.0 15.3 %collective-permute-start.1 = (bf16[2,96,1536]{2,1,0:T(8,128)(2,1)S(1)}, bf16[2,96,1536]{2,1,0:T(8,128)(2,1)S(1)}, u32[]{:S(2)}, u32[]{:S(2)}) collective-permute-start(bf16[2,96,1536]{2,1,0:T(8,128)(2,1)S(1)} %dynamic-slice_bitcast_fusion.19), channel_id=1, source_target_pairs={{0,8},{4,12},{8,0},{12,4},{16,24},{20,28},{24,16},{28,20},{1,9},{5... | collective-permute-start | bytes 1769480 | tf_op jit(solution)/shard_map/ppermute | solution.py:52
  950.3 19.2 %collective-permute-start.7 = (bf16[96,768]{1,0:T(8,128)(2,1)S(1)}, bf16[96,768]{1,0:T(8,128)(2,1)S(1)}, u32[]{:S(2)}, u32[]{:S(2)}) collective-permute-start(bf16[96,768]{1,0:T(8,128)(2,1)S(1)} %bitcast.890), channel_id=1, source_target_pairs={{0,2},{1,3},{2,0},{3,1},{4,6},{5,7},{6,4},{7,5},{8,10},{9,11},{10,... | collective-permute-start | bytes 442376 | tf_op jit(solution)/shard_map/ppermute | solution.py:52
  (178 other events, 1958.0 us)
Sparse Core Ops, SparseCore 0:
  23.0 37.4 all-gather.14
  62.4 24.0 all-gather.18
  88.9 38.9 all-gather.20
  129.6 38.9 all-gather.22
  170.4 33.9 all-gather.16
  206.1 24.0 all-gather.24
  232.7 38.9 all-gather.26
  274.1 38.9 all-gather.28
  704.6 118.7 all-reduce.2

commit v2 on v1

--- a/solution.py
+++ b/solution.py
@@ -50,7 +50,16 @@
     kept = lax.dynamic_index_in_dim(parts, mine, axis, keepdims=False)
     sent = lax.dynamic_index_in_dim(parts, 1 - mine, axis, keepdims=False)
     got = lax.ppermute(sent, axis_name, [(i, i ^ (1 << bit)) for i in range(size)])
-    return (kept.astype(jnp.float32) + got.astype(jnp.float32)).astype(jnp.bfloat16)
+    return (kept.astype(jnp.float32) + got.astype(jnp.float32)).astype(parts.dtype)
+
+
+def gather_halves(part, axis_name, bit, axis):
+    size = lax.axis_size(axis_name)
+    mine = (lax.axis_index(axis_name) >> bit) & 1
+    got = lax.ppermute(part, axis_name, [(i, i ^ (1 << bit)) for i in range(size)])
+    return jnp.stack(
+        [jnp.where(mine == 0, part, got), jnp.where(mine == 0, got, part)], axis=axis
+    )
 
 
 def reduce_owner(grads, order):
@@ -74,7 +83,21 @@
     )
     for bit in range(bits):
         parts = exchange_halves(parts, "sp", bit, axis + bits - 1 - bit)
-    return lax.all_gather(parts, "sp", axis=axis, tiled=True)
+    for bit in reversed(range(bits)):
+        parts = gather_halves(parts, "sp", bit, axis + bits - 1 - bit)
+    return parts.reshape(shape)
+
+
+def settle_vectors(grads):
+    size = lax.axis_size("fsdp")
+    bits = log_two(size)
+    parts = grads.reshape((2,) * bits + grads.shape[1:])
+    for bit in range(bits):
+        parts = exchange_halves(parts, "fsdp", bit, bits - 1 - bit)
+    groups = lax.axis_size("sp")
+    for bit in range(log_two(groups)):
+        parts = parts + lax.ppermute(parts, "sp", [(i, i ^ (1 << bit)) for i in range(groups)])
+    return parts
 
 
 def settle(grads, axis):
@@ -336,12 +359,18 @@
         grad_attn = settle(jnp.concatenate([grad_qkv, grad_out], axis=1), 1)
         vector_grads = jnp.concatenate(
             [
-                jnp.stack([grad_gain_one, grad_gain_two], axis=1),
-                jnp.stack([grad_shift_one, grad_shift_two], axis=1),
-                jnp.stack([proj_sums[:width], proj_sums[2 * width :]], axis=1),
-                jnp.stack([grad_out_bias, grad_down_bias], axis=1),
-                grad_up_bias.reshape(width, hidden // width),
-            ],
+                grad_gain_one,
+                grad_gain_two,
+                grad_shift_one,
+                grad_shift_two,
+                proj_sums[:width],
+                proj_sums[2 * width :],
+                grad_out_bias,
+                grad_down_bias,
+            ]
+        ).reshape(8, -1, shard)
+        vector_grads = jnp.concatenate(
+            [jnp.swapaxes(vector_grads, 0, 1), grad_up_bias.reshape(width // shard, -1, shard)],
             axis=1,
         )
         layer_grads.append((grad_attn, grad_up, grad_down))
@@ -350,22 +379,19 @@
     grad_inputs = grad_stream.astype(jnp.bfloat16).reshape(clips, frames, width)
     qkv_list, out_list, up_list, down_list = ([], [], [], [])
     gain_list, shift_list, bias_list, branch_list, upbias_list = ([], [], [], [], [])
-    vector_sums = lax.psum(jnp.concatenate(vector_sums[::-1], axis=1), ("fsdp", "sp"))
-    vector_sums = lax.dynamic_slice_in_dim(
-        vector_sums, lax.axis_index("fsdp") * shard, shard, 0
-    )
+    vector_sums = settle_vectors(jnp.concatenate(vector_sums[::-1], axis=1))
     for layer_index, (attn_part, up_part, down_part) in enumerate(layer_grads):
-        vector_part = vector_sums[:, layer_index * count : (layer_index + 1) * count]
+        vector_part = vector_sums[layer_index * count : (layer_index + 1) * count]
         attn_part = attn_part.astype(jnp.float32)
         qkv_list.append(attn_part[:, : 3 * width].reshape(shard, 3, width))
         out_list.append(attn_part[:, 3 * width :])
         up_list.append(up_part.astype(jnp.float32))
         down_list.append(down_part.astype(jnp.float32))
-        gain_list.append(vector_part[:, 0:2].T)
-        shift_list.append(vector_part[:, 2:4].T)
-        bias_list.append(vector_part[:, 4:6].T)
-        branch_list.append(vector_part[:, 6:8].T)
-        upbias_list.append(vector_part[:, 8:].reshape(-1))
+        gain_list.append(vector_part[0:2])
+        shift_list.append(vector_part[2:4])
+        bias_list.append(vector_part[4:6])
+        branch_list.append(vector_part[6:8])
+        upbias_list.append(vector_part[8:].reshape(-1))
     return (
         output,
         grad_inputs,

time: 1010 us -> 912 us (0.903)
  blocking collectives: 102 us -> 0 us
  local copies, waits for them, and re-layouts: 178 us -> 203 us
  waiting for transfers between devices: 358 us -> 338 us
    psum x1 -> x0, waiting for transfers between devices: 115 us -> none  [local(): lax.psum(jnp.concatenate(vector_sums[::-1], axis=1), ('fsdp', 'sp'))]
    all_gather x6 -> x0, blocking collectives: 102 us -> none  [reduce_frames(): return lax.all_gather(parts, 'sp', axis=axis, tiled=True)]
    ppermute x0 -> x14, waiting for transfers between devices: none -> 51.7 us  [the longest x12 45.5 us: gather_halves(): lax.ppermute(part, axis_name, [(i, i ^ 1 << bit) for i in range(size)])]
    ppermute x48 -> x51, waiting for transfers between devices: 61.3 us -> 104 us  [exchange_halves(): lax.ppermute(sent, axis_name, [(i, i ^ 1 << bit) for i in range(size)])]
    unnamed x300 -> x316, local copies, waits for them, and re-layouts: 27.1 us -> 40.9 us
    ppermute x48 -> x51, starting transfers between devices: 48 us -> 41.8 us  [exchange_halves(): lax.ppermute(sent, axis_name, [(i, i ^ 1 << bit) for i in range(size)])]
    squeeze x38 -> x41, local copies, waits for them, and re-layouts: 20.7 us -> 18.6 us  [exchange_halves(): sent = lax.dynamic_index_in_dim(parts, 1 - mine, axis, keepdims=False)]
  transfers between devices with their start and end apart: 65 -> 81, of which waited for: 23 -> 43; matrix products, arithmetic and copies ran while one was open for 34% -> 41% of each run, Pallas kernels for 0% -> 0%
where the time goes in v2:
time: 912 us; the launch traced here: 902 us
  waiting for transfers between devices  338 us (37%)
  local copies, waits for them, and re-layouts  203 us (22%)
  matrix products  148 us (16%)
  other arithmetic  99.4 us (11%)
  starting transfers between devices  81.3 us (9%)
  between operations  17 us (2%)
  loops' own time  15.3 us (2%)
    ppermute x51, waiting for transfers between devices, exchange_halves(): lax.ppermute(sent, axis_name, [(i, i ^ 1 << bit) for i in range(size)])  104 us
    all_gather x8, waiting for transfers between devices, gather_rows(): return lax.all_gather(shard, 'fsdp', axis=0, tiled=True)  73.5 us
    all_to_all x2, waiting for transfers between devices, local(): lax.all_to_all(projected.reshape(clips, frames, 3, groups, width // group...  55.9 us
    ppermute x12, waiting for transfers between devices, gather_halves(): lax.ppermute(part, axis_name, [(i, i ^ 1 << bit) for i in range(size)])  45.5 us
    ppermute x51, starting transfers between devices, exchange_halves(): lax.ppermute(sent, axis_name, [(i, i ^ 1 << bit) for i in range(size)])  41.8 us
    convert_element_type x48, other arithmetic, exchange_halves(): (kept.astype(jnp.float32) + got.astype(jnp.float32)).astype(parts.dtype)  41.1 us
    unnamed x316, local copies, waits for them, and re-layouts  40.9 us
    dot_general x8, matrix products, product(): return jnp.dot(left, right, preferred_element_type=jnp.float32)  38.7 us
  transfers between devices with their start and end apart: 81, of which 43 were waited for; matrix products, arithmetic and copies ran while one was open for 41% of the time, Pallas kernels for 0%

profile of v2, /device:TPU:0, one launch (start us, length us, event | category | flops | bytes accessed | tf_op | source)
XLA Modules:
  0.0 901.7 jit_solution(10446070915490970131)
XLA Ops:
  28.4 32.2 %all-gather.15.cloned.1.call-done = bf16[768,2432]{1,0:T(8,128)(2,1)} async-done(((bf16[96,2432]{1,0:T(8,128)(2,1)}), bf16[768,2432]{1,0:T(8,128)(2,1)}) %all-gather.15.cloned.1.call-update) | async-done | bytes 3735568 | tf_op jit(solution)/shard_map/all_gather | solution.py:40
  69.4 4.6 all-to-all-start
  75.4 27.6 %all-to-all-done = bf16[1,256,3,4,192]{1,4,2,0,3:T(8,128)(2,1)S(1)} async-done(((bf16[1,256,3,4,192]{1,4,2,0,3:T(8,128)(2,1)}), bf16[1,256,3,4,192]{1,4,2,0,3:T(8,128)(2,1)S(1)}, u32[]{:S(2)}, u32[]{:S(2)}) %all-to-all-start) | async-done | bytes 1179680 | tf_op jit(solution)/shard_map/all_to_all | solution.py:251
  106.4 20.2 %while.54 = (s32[]{:T(128)}, bf16[2,1,512,3,64]{2,4,3,1,0:T(8,128)(2,1)S(1)}, f32[2,1,3,512]{3,2,1,0:T(4,128)}, s32[2]{0:T(128)}, bf16[1,1024,3,64]{1,3,2,0:T(8,...) while((s32[]{:T(128)}, ...), condition=%wide.region_5.6_spmd, body=%wide.region_2.5_spmd.sunk | while | flops 416905728 | bytes 20109480 | solution.py:135
  128.6 4.0 reduce.53
  138.1 10.8 %all-to-all-done.1 = bf16[4,2,24576]{2,1,0:T(2,128)(2,1)S(1)} async-done(((bf16[4,2,24576]{2,1,0:T(2,128)(2,1)}), bf16[4,2,24576]{2,1,0:T(2,128)(2,1)S(1)}, u32[]{:S(2)}, u32[]{:S(2)}) %all-to-all-start.1) | async-done | bytes 393248 | tf_op jit(solution)/shard_map/all_to_all | solution.py:263
  153.0 11.3 %multiply_convert_fusion.3 = (bf16[256,3072]{1,0:T(8,128)(2,1)S(1)}, f32[256,3072]{1,0:T(8,128)}, f32[256,3072]{1,0:T(8,128)}) fusion(f32[3072]{0:T(1024)S(1)} %add.576, bf16[1,768,3072]{2,1,0:T(8,128)(2,1)} %all-gather.21.cloned.1.call-done, f32[256,768]{1,0:T(8,128)S(1)} %get-tuple-element.569, f32[768]{0:T(1024)S(1)} %get-tuple-element.370, ...), kind=kOutput, calls=%fused_computation.151 | convolution fusion | flops 1260847104 | bytes 13389824 | tf_op jit(solution)/shard_map/dot_general | solution.py:24
  164.4 4.3 all-gather.23.cloned.1.call-done
  172.8 31.6 %all-gather.17.cloned.1.call-done = bf16[768,2304]{1,0:T(8,128)(2,1)} async-done(((bf16[96,2304]{1,0:T(8,128)(2,1)}), bf16[768,2304]{1,0:T(8,128)(2,1)}) %all-gather.17.cloned.1.call-update) | async-done | bytes 3538960 | tf_op jit(solution)/shard_map/all_gather | solution.py:40
  204.4 4.2 fusion.115
  211.3 4.6 all-to-all-start.2
  216.6 28.2 %all-to-all-done.2 = bf16[1,256,3,4,192]{1,4,2,0,3:T(8,128)(2,1)S(1)} async-done(((bf16[1,256,3,4,192]{1,4,2,0,3:T(8,128)(2,1)}), bf16[1,256,3,4,192]{1,4,2,0,3:T(8,128)(2,1)S(1)}, u32[]{:S(2)}, u32[]{:S(2)}) %all-to-all-start.2) | async-done | bytes 1179680 | tf_op jit(solution)/shard_map/all_to_all | solution.py:251
  250.5 19.1 %while.55 = (s32[]{:T(128)}, bf16[2,1,512,3,64]{2,4,3,1,0:T(8,128)(2,1)S(1)}, f32[2,1,3,512]{3,2,1,0:T(4,128)S(1)}, s32[2]{0:T(128)}, bf16[1,1024,3,64]{1,3,2,0:...) while((s32[]{:T(128)}, ...), condition=%wide.region_13.14_spmd, body=%wide.region_10.13_spmd.sunk | while | flops 416905728 | bytes 20113576 | solution.py:135
  271.1 4.0 reduce.54
  280.8 10.8 %all-to-all-done.3 = bf16[4,2,24576]{2,1,0:T(2,128)(2,1)S(1)} async-done(((bf16[4,2,24576]{2,1,0:T(2,128)(2,1)}), bf16[4,2,24576]{2,1,0:T(2,128)(2,1)S(1)}, u32[]{:S(2)}, u32[]{:S(2)}) %all-to-all-start.3) | async-done | bytes 393248 | tf_op jit(solution)/shard_map/all_to_all | solution.py:263
  295.6 12.1 %multiply_convert_fusion.2 = (bf16[256,3072]{1,0:T(8,128)(2,1)}, f32[256,3072]{1,0:T(8,128)}, f32[256,3072]{1,0:T(8,128)}) fusion(f32[3072]{0:T(1024)S(1)} %add.597, bf16[1,768,3072]{2,1,0:T(8,128)(2,1)} %all-gather.27.cloned.1.call-done, f32[256,768]{1,0:T(8,128)S(1)} %get-tuple-element.574, f32[768]{0:T(1024)S(1)} %copy-done.102, ...), kind=kOutput, calls=%fused_computation.138 | convolution fusion | flops 1260847104 | bytes 13389824 | tf_op jit(solution)/shard_map/dot_general | solution.py:24
  307.7 5.4 all-gather.29.cloned.1.call-done
  313.1 6.8 convert_reduce_fusion
  329.4 5.0 all-to-all-start.4
  334.4 4.1 fusion.267
  358.7 38.9 %while.56 = (s32[]{:T(128)}, f32[1,1024,3,64]{1,3,2,0:T(8,128)}, f32[1,1024,3,64]{1,3,2,0:T(8,128)}, bf16[2,1,512,3,64]{2,4,3,1,0:T(8,128)(2,1)}, s32[2]{0:T(128...) while((s32[]{:T(128)}, f32[1,1024,3,64]{1,3,2,0:T(8,128)}, ...), condition=%wide.region_20.21_spmd.clone, body=%wide.region_18.20_spmd.clone.sunk | while | flops 1026685440 | bytes 106113400 | solution.py:182
  404.4 5.2 all-to-all-start.5
  428.8 29.1 %all-to-all-done.5 = bf16[1,1024,3,1,192]{4,2,3,0,1:T(4,128)(2,1)S(1)} async-done(((bf16[1,1024,3,1,192]{4,2,3,0,1:T(4,128)(2,1)}), bf16[1,1024,3,1,192]{4,2,3,0,1:T(4,128)(2,1)S(1)}, u32[]{:S(2)}, u32[]{:S(2)}) %all-to-all-start.5) | async-done | bytes 1179680 | tf_op jit(solution)/shard_map/all_to_all | solution.py:350
  485.5 4.3 all-to-all-start.6
  532.1 39.4 %while.57 = (s32[]{:T(128)}, f32[1,1024,3,64]{1,3,2,0:T(8,128)}, f32[1,1024,3,64]{1,3,2,0:T(8,128)}, bf16[2,1,512,3,64]{2,4,3,1,0:T(8,128)(2,1)}, s32[2]{0:T(128...) while((s32[]{:T(128)}, f32[1,1024,3,64]{1,3,2,0:T(8,128)}, ...), condition=%wide.region_27.28_spmd.clone, body=%wide.region_25.27_spmd.clone.sunk | while | flops 1026685440 | bytes 106015048 | solution.py:182
  578.3 5.6 all-to-all-start.7
  599.6 4.5 collective-permute-done.14
  608.0 8.7 collective-permute-done.24
  620.6 11.8 %collective-permute-done.51 = bf16[2,384,384]{2,1,0:T(8,128)(2,1)S(1)} collective-permute-done((bf16[2,384,384]{2,1,0:T(8,128)(2,1)S(1)}, bf16[2,384,384]{2,1,0:T(8,128)(2,1)S(1)}, u32[]{:S(2)}, u32[]{:S(2)}) %collective-permute-start.51) | collective-permute-done | bytes 589856 | tf_op jit(solution)/shard_map/ppermute | solution.py:52
  636.4 8.6 collective-permute-done.41
  652.4 5.4 collective-permute-done.25
  675.4 4.1 copy.512
  735.3 4.0 collective-permute-done.64
  745.2 7.5 collective-permute-done.27
  753.6 6.8 collective-permute-done.57
  761.4 5.4 collective-permute-done.47
  766.8 6.3 collective-permute-done.38
  773.1 4.8 collective-permute-done.28
  780.5 4.6 collective-permute-done.48
  785.9 5.2 collective-permute-done.39
  791.1 6.3 collective-permute-done.29
  798.2 5.4 collective-permute-done.49
  824.4 9.5 %collective-permute-done.11 = bf16[2,96,1536]{2,1,0:T(8,128)(2,1)S(1)} collective-permute-done((bf16[2,96,1536]{2,1,0:T(8,128)(2,1)S(1)}, bf16[2,96,1536]{2,1,0:T(8,128)(2,1)S(1)}, u32[]{:S(2)}, u32[]{:S(2)}) %collective-permute-start.11) | collective-permute-done | bytes 589856 | tf_op jit(solution)/shard_map/ppermute | solution.py:52
  837.2 5.3 collective-permute-done.1
  854.9 6.9 collective-permute-done.6
  862.0 4.0 collective-permute-done.17
  866.1 4.9 collective-permute-done.7
  873.3 4.5 collective-permute-done.8
  (880 shorter events, 478.9 us)
Async XLA Ops:
  7.2 53.4 %all-gather.15.cloned.1.call-start = ((), (), s32[]{:S(2)}) async-start(), calls=%async_computation.8 | async-start | bytes 4202496 | tf_op jit(solution)/shard_map/all_gather | solution.py:40
  22.9 127.8 %all-gather.19.cloned.1.call-start = ((), (), s32[]{:S(2)}) async-start(), calls=%async_computation.10 | async-start | bytes 1327104 | tf_op jit(solution)/shard_map/all_gather | solution.py:40
  23.7 129.3 %all-gather.21.cloned.1.call-start = ((), (), s32[]{:S(2)}) async-start(), calls=%async_computation.11 | async-start | bytes 5308416 | tf_op jit(solution)/shard_map/all_gather | solution.py:40
  24.9 143.8 %all-gather.23.cloned.1.call-start = ((), (), s32[]{:S(2)}) async-start(), calls=%async_computation.12 | async-start | bytes 5308416 | tf_op jit(solution)/shard_map/all_gather | solution.py:40
  26.1 178.3 %all-gather.17.cloned.1.call-start = ((), (), s32[]{:S(2)}) async-start(), calls=%async_computation.9 | async-start | bytes 3981312 | tf_op jit(solution)/shard_map/all_gather | solution.py:40
  27.4 265.9 %all-gather.25.cloned.1.call-start = ((), (), s32[]{:S(2)}) async-start(), calls=%async_computation.13 | async-start | bytes 1327104 | tf_op jit(solution)/shard_map/all_gather | solution.py:40
  69.4 33.6 %all-to-all-start = ((bf16[1,256,3,4,192]{1,4,2,0,3:T(8,128)(2,1)}), bf16[1,256,3,4,192]{1,4,2,0,3:T(8,128)(2,1)S(1)}, u32[]{:S(2)}, u32[]{:S(2)}) async-start(bf16[1,256,3,4,192]{1,4,2,0,3:T(8,128)(2,1)} %copy.444), calls=%async_computation | async-start | bytes 2359296 | tf_op jit(solution)/shard_map/all_to_all | solution.py:251
  74.0 221.5 %all-gather.27.cloned.1.call-start = ((), (), s32[]{:S(2)}) async-start(), calls=%async_computation.14 | async-start | bytes 5308416 | tf_op jit(solution)/shard_map/all_gather | solution.py:40
  134.1 14.9 %all-to-all-start.1 = ((bf16[4,2,24576]{2,1,0:T(2,128)(2,1)}), bf16[4,2,24576]{2,1,0:T(2,128)(2,1)S(1)}, u32[]{:S(2)}, u32[]{:S(2)}) async-start(bf16[4,2,24576]{2,1,0:T(2,128)(2,1)} %reshape.852), calls=%async_computation.1 | async-start | bytes 786432 | tf_op jit(solution)/shard_map/all_to_all | solution.py:263
  211.3 33.6 %all-to-all-start.2 = ((bf16[1,256,3,4,192]{1,4,2,0,3:T(8,128)(2,1)}), bf16[1,256,3,4,192]{1,4,2,0,3:T(8,128)(2,1)S(1)}, u32[]{:S(2)}, u32[]{:S(2)}) async-start(bf16[1,256,3,4,192]{1,4,2,0,3:T(8,128)(2,1)} %copy.452), calls=%async_computation.2 | async-start | bytes 2359296 | tf_op jit(solution)/shard_map/all_to_all | solution.py:251
  215.9 97.2 %all-gather.29.cloned.1.call-start = ((), (), s32[]{:S(2)}) async-start(), calls=%async_computation.15 | async-start | bytes 5308416 | tf_op jit(solution)/shard_map/all_gather | solution.py:40
  276.5 15.0 %all-to-all-start.3 = ((bf16[4,2,24576]{2,1,0:T(2,128)(2,1)}), bf16[4,2,24576]{2,1,0:T(2,128)(2,1)S(1)}, u32[]{:S(2)}, u32[]{:S(2)}) async-start(bf16[4,2,24576]{2,1,0:T(2,128)(2,1)} %reshape.854), calls=%async_computation.3 | async-start | bytes 786432 | tf_op jit(solution)/shard_map/all_to_all | solution.py:263
  329.4 19.8 %all-to-all-start.4 = ((bf16[1,256,4,192]{1,3,0,2:T(8,128)(2,1)}), bf16[1,256,4,192]{1,3,0,2:T(8,128)(2,1)S(1)}, u32[]{:S(2)}, u32[]{:S(2)}) async-start(bf16[1,256,4,192]{1,3,0,2:T(8,128)(2,1)} %bitcast.62), calls=%async_computation.4 | async-start | bytes 786432 | tf_op jit(solution)/shard_map/all_to_all | solution.py:336
  353.4 60.1 %collective-permute-start.34 = (bf16[2,96,1536]{2,1,0:T(8,128)(2,1)}, bf16[2,96,1536]{2,1,0:T(8,128)(2,1)}, u32[]{:S(2)}, u32[]{:S(2)}) collective-permute-start(bf16[2,96,1536]{2,1,0:T(8,128)(2,1)} %dynamic-slice_bitcast_fusion.12), channel_id=1, source_target_pairs={{0,16},{4,20},{8,24},{12,28},{16,0},{20,4},{24,8},{28,12},{1,17},{... | collective-permute-start | bytes 1769480 | tf_op jit(solution)/shard_map/ppermute | solution.py:52
  357.2 52.4 %collective-permute-start.54 = (bf16[2,384,384]{2,1,0:T(8,128)(2,1)}, bf16[2,384,384]{2,1,0:T(8,128)(2,1)}, u32[]{:S(2)}, u32[]{:S(2)}) collective-permute-start(bf16[2,384,384]{2,1,0:T(8,128)(2,1)} %dynamic-slice_bitcast_fusion.8), channel_id=1, source_target_pairs={{0,16},{4,20},{8,24},{12,28},{16,0},{20,4},{24,8},{28,12},{1,17},{... | collective-permute-start | bytes 1769480 | tf_op jit(solution)/shard_map/ppermute | solution.py:52
  404.4 53.5 %all-to-all-start.5 = ((bf16[1,1024,3,1,192]{4,2,3,0,1:T(4,128)(2,1)}), bf16[1,1024,3,1,192]{4,2,3,0,1:T(4,128)(2,1)S(1)}, u32[]{:S(2)}, u32[]{:S(2)}) async-start(bf16[1,1024,3,1,192]{4,2,3,0,1:T(4,128)(2,1)} %copy.462), calls=%async_computation.5 | async-start | bytes 4194304 | tf_op jit(solution)/shard_map/all_to_all | solution.py:350
  485.5 43.5 %all-to-all-start.6 = ((bf16[1,256,4,192]{1,3,0,2:T(8,128)(2,1)}), bf16[1,256,4,192]{1,3,0,2:T(8,128)(2,1)}, u32[]{:S(2)}, u32[]{:S(2)}) async-start(bf16[1,256,4,192]{1,3,0,2:T(8,128)(2,1)} %bitcast.915), calls=%async_computation.6 | async-start | bytes 786432 | tf_op jit(solution)/shard_map/all_to_all | solution.py:336
  495.3 90.5 %collective-permute-start.13 = (bf16[2,2,96,1536]{3,2,1,0:T(8,128)(2,1)}, bf16[2,2,96,1536]{3,2,1,0:T(8,128)(2,1)}, u32[]{:S(2)}, u32[]{:S(2)}) collective-permute-start(bf16[2,2,96,1536]{3,2,1,0:T(8,128)(2,1)} %dynamic-slice_bitcast_fusion.6), channel_id=1, source_target_pairs={{0,4},{4,0},{8,12},{12,8},{16,20},{20,16},{24,28},{28,24},{1,5},{5... | collective-permute-start | bytes 3538952 | tf_op jit(solution)/shard_map/ppermute | solution.py:52
  501.4 82.6 %collective-permute-start.30 = (bf16[2,2,96,1536]{3,2,0,1:T(8,128)(2,1)}, bf16[2,2,96,1536]{3,2,0,1:T(8,128)(2,1)}, u32[]{:S(2)}, u32[]{:S(2)}) collective-permute-start(bf16[2,2,96,1536]{3,2,0,1:T(8,128)(2,1)} %bitcast.778), channel_id=1, source_target_pairs={{0,4},{4,0},{8,12},{12,8},{16,20},{20,16},{24,28},{28,24},{1,5},{5... | collective-permute-start | bytes 3538952 | tf_op jit(solution)/shard_map/ppermute | solution.py:52
  502.7 88.2 %collective-permute-start.23 = (bf16[2,2,96,1536]{3,2,1,0:T(8,128)(2,1)}, bf16[2,2,96,1536]{3,2,1,0:T(8,128)(2,1)}, u32[]{:S(2)}, u32[]{:S(2)}) collective-permute-start(bf16[2,2,96,1536]{3,2,1,0:T(8,128)(2,1)} %dynamic-slice_bitcast_fusion.5), channel_id=1, source_target_pairs={{0,4},{4,0},{8,12},{12,8},{16,20},{20,16},{24,28},{28,24},{1,5},{5... | collective-permute-start | bytes 3538952 | tf_op jit(solution)/shard_map/ppermute | solution.py:52
  504.1 83.7 %collective-permute-start.20 = (bf16[2,2,96,1536]{3,2,0,1:T(8,128)(2,1)}, bf16[2,2,96,1536]{3,2,0,1:T(8,128)(2,1)}, u32[]{:S(2)}, u32[]{:S(2)}) collective-permute-start(bf16[2,2,96,1536]{3,2,0,1:T(8,128)(2,1)} %bitcast.779), channel_id=1, source_target_pairs={{0,4},{4,0},{8,12},{12,8},{16,20},{20,16},{24,28},{28,24},{1,5},{5... | collective-permute-start | bytes 3538952 | tf_op jit(solution)/shard_map/ppermute | solution.py:52
  509.0 86.2 %collective-permute-start.50 = (bf16[2,2,384,384]{3,2,0,1:T(8,128)(2,1)}, bf16[2,2,384,384]{3,2,0,1:T(8,128)(2,1)}, u32[]{:S(2)}, u32[]{:S(2)}) collective-permute-start(bf16[2,2,384,384]{3,2,0,1:T(8,128)(2,1)} %bitcast.776), channel_id=1, source_target_pairs={{0,4},{4,0},{8,12},{12,8},{16,20},{20,16},{24,28},{28,24},{1,5},{5... | collective-permute-start | bytes 3538952 | tf_op jit(solution)/shard_map/ppermute | solution.py:52
  578.3 97.1 %all-to-all-start.7 = ((bf16[1,1024,3,1,192]{4,2,3,0,1:T(4,128)(2,1)}), bf16[1,1024,3,1,192]{4,2,3,0,1:T(4,128)(2,1)}, u32[]{:S(2)}, u32[]{:S(2)}) async-start(bf16[1,1024,3,1,192]{4,2,3,0,1:T(4,128)(2,1)} %copy.469), calls=%async_computation.7 | async-start | bytes 4194304 | tf_op jit(solution)/shard_map/all_to_all | solution.py:350
  587.8 16.2 %collective-permute-start.14 = (bf16[2,96,1536]{2,1,0:T(8,128)(2,1)S(1)}, bf16[2,96,1536]{2,1,0:T(8,128)(2,1)S(1)}, u32[]{:S(2)}, u32[]{:S(2)}) collective-permute-start(bf16[2,96,1536]{2,1,0:T(8,128)(2,1)S(1)} %dynamic-slice_bitcast_fusion.16), channel_id=1, source_target_pairs={{0,16},{4,20},{8,24},{12,28},{16,0},{20,4},{24,8},{28,12},{1,17},{... | collective-permute-start | bytes 1769480 | tf_op jit(solution)/shard_map/ppermute | solution.py:52
  590.9 16.3 %collective-permute-start.31 = (bf16[2,96,1536]{2,1,0:T(8,128)(2,1)S(1)}, bf16[2,96,1536]{2,1,0:T(8,128)(2,1)S(1)}, u32[]{:S(2)}, u32[]{:S(2)}) collective-permute-start(bf16[2,96,1536]{2,1,0:T(8,128)(2,1)S(1)} %dynamic-slice_bitcast_fusion.13), channel_id=1, source_target_pairs={{0,8},{4,12},{8,0},{12,4},{16,24},{20,28},{24,16},{28,20},{1,9},{5... | collective-permute-start | bytes 1769480 | tf_op jit(solution)/shard_map/ppermute | solution.py:52
  593.4 23.3 %collective-permute-start.24 = (bf16[2,96,1536]{2,1,0:T(8,128)(2,1)S(1)}, bf16[2,96,1536]{2,1,0:T(8,128)(2,1)S(1)}, u32[]{:S(2)}, u32[]{:S(2)}) collective-permute-start(bf16[2,96,1536]{2,1,0:T(8,128)(2,1)S(1)} %dynamic-slice_bitcast_fusion.14), channel_id=1, source_target_pairs={{0,16},{4,20},{8,24},{12,28},{16,0},{20,4},{24,8},{28,12},{1,17},{... | collective-permute-start | bytes 1769480 | tf_op jit(solution)/shard_map/ppermute | solution.py:52
  595.3 24.5 %collective-permute-start.21 = (bf16[2,96,1536]{2,1,0:T(8,128)(2,1)S(1)}, bf16[2,96,1536]{2,1,0:T(8,128)(2,1)S(1)}, u32[]{:S(2)}, u32[]{:S(2)}) collective-permute-start(bf16[2,96,1536]{2,1,0:T(8,128)(2,1)S(1)} %dynamic-slice_bitcast_fusion.15), channel_id=1, source_target_pairs={{0,8},{4,12},{8,0},{12,4},{16,24},{20,28},{24,16},{28,20},{1,9},{5... | collective-permute-start | bytes 1769480 | tf_op jit(solution)/shard_map/ppermute | solution.py:52
  597.7 34.7 %collective-permute-start.51 = (bf16[2,384,384]{2,1,0:T(8,128)(2,1)S(1)}, bf16[2,384,384]{2,1,0:T(8,128)(2,1)S(1)}, u32[]{:S(2)}, u32[]{:S(2)}) collective-permute-start(bf16[2,384,384]{2,1,0:T(8,128)(2,1)S(1)} %dynamic-slice_bitcast_fusion.9), channel_id=1, source_target_pairs={{0,8},{4,12},{8,0},{12,4},{16,24},{20,28},{24,16},{28,20},{1,9},{5... | collective-permute-start | bytes 1769480 | tf_op jit(solution)/shard_map/ppermute | solution.py:52
  604.1 30.7 %collective-permute-start.44 = (bf16[2,384,384]{2,1,0:T(8,128)(2,1)S(1)}, bf16[2,384,384]{2,1,0:T(8,128)(2,1)S(1)}, u32[]{:S(2)}, u32[]{:S(2)}) collective-permute-start(bf16[2,384,384]{2,1,0:T(8,128)(2,1)S(1)} %dynamic-slice_bitcast_fusion.10), channel_id=1, source_target_pairs={{0,16},{4,20},{8,24},{12,28},{16,0},{20,4},{24,8},{28,12},{1,17},{... | collective-permute-start | bytes 1769480 | tf_op jit(solution)/shard_map/ppermute | solution.py:52
  607.1 37.9 %collective-permute-start.41 = (bf16[2,384,384]{2,1,0:T(8,128)(2,1)S(1)}, bf16[2,384,384]{2,1,0:T(8,128)(2,1)S(1)}, u32[]{:S(2)}, u32[]{:S(2)}) collective-permute-start(bf16[2,384,384]{2,1,0:T(8,128)(2,1)S(1)} %dynamic-slice_bitcast_fusion.11), channel_id=1, source_target_pairs={{0,8},{4,12},{8,0},{12,4},{16,24},{20,28},{24,16},{28,20},{1,9},{5... | collective-permute-start | bytes 1769480 | tf_op jit(solution)/shard_map/ppermute | solution.py:52
  616.7 56.9 %collective-permute-start.15 = (bf16[96,1536]{1,0:T(8,128)(2,1)}, bf16[96,1536]{1,0:T(8,128)(2,1)}, u32[]{:S(2)}, u32[]{:S(2)}) collective-permute-start(bf16[96,1536]{1,0:T(8,128)(2,1)} %dynamic-slice_bitcast_fusion.30), channel_id=1, source_target_pairs={{0,8},{4,12},{8,0},{12,4},{16,24},{20,28},{24,16},{28,20},{1,9},{5... | collective-permute-start | bytes 884744 | tf_op jit(solution)/shard_map/ppermute | solution.py:52
  619.8 27.7 %collective-permute-start.32 = (bf16[96,1536]{1,0:T(8,128)(2,1)S(1)}, bf16[96,1536]{1,0:T(8,128)(2,1)S(1)}, u32[]{:S(2)}, u32[]{:S(2)}) collective-permute-start(bf16[96,1536]{1,0:T(8,128)(2,1)S(1)} %dynamic-slice_bitcast_fusion.27), channel_id=1, source_target_pairs={{0,16},{4,20},{8,24},{12,28},{16,0},{20,4},{24,8},{28,12},{1,17},{... | collective-permute-start | bytes 884744 | tf_op jit(solution)/shard_map/ppermute | solution.py:52
  632.4 25.4 %collective-permute-start.25 = (bf16[96,1536]{1,0:T(8,128)(2,1)}, bf16[96,1536]{1,0:T(8,128)(2,1)}, u32[]{:S(2)}, u32[]{:S(2)}) collective-permute-start(bf16[96,1536]{1,0:T(8,128)(2,1)} %dynamic-slice_bitcast_fusion.28), channel_id=1, source_target_pairs={{0,8},{4,12},{8,0},{12,4},{16,24},{20,28},{24,16},{28,20},{1,9},{5... | collective-permute-start | bytes 884744 | tf_op jit(solution)/shard_map/ppermute | solution.py:52
  634.8 24.8 %collective-permute-start.22 = (bf16[96,1536]{1,0:T(8,128)(2,1)}, bf16[96,1536]{1,0:T(8,128)(2,1)}, u32[]{:S(2)}, u32[]{:S(2)}) collective-permute-start(bf16[96,1536]{1,0:T(8,128)(2,1)} %dynamic-slice_bitcast_fusion.29), channel_id=1, source_target_pairs={{0,16},{4,20},{8,24},{12,28},{16,0},{20,4},{24,8},{28,12},{1,17},{... | collective-permute-start | bytes 884744 | tf_op jit(solution)/shard_map/ppermute | solution.py:52
  645.0 20.9 %collective-permute-start.52 = (bf16[384,384]{1,0:T(8,128)(2,1)}, bf16[384,384]{1,0:T(8,128)(2,1)}, u32[]{:S(2)}, u32[]{:S(2)}) collective-permute-start(bf16[384,384]{1,0:T(8,128)(2,1)} %dynamic-slice_bitcast_fusion.22), channel_id=1, source_target_pairs={{0,16},{4,20},{8,24},{12,28},{16,0},{20,4},{24,8},{28,12},{1,17},{... | collective-permute-start | bytes 884744 | tf_op jit(solution)/shard_map/ppermute | solution.py:52
  647.5 20.4 %collective-permute-start.45 = (bf16[384,384]{1,0:T(8,128)(2,1)}, bf16[384,384]{1,0:T(8,128)(2,1)}, u32[]{:S(2)}, u32[]{:S(2)}) collective-permute-start(bf16[384,384]{1,0:T(8,128)(2,1)} %dynamic-slice_bitcast_fusion.24), channel_id=1, source_target_pairs={{0,8},{4,12},{8,0},{12,4},{16,24},{20,28},{24,16},{28,20},{1,9},{5... | collective-permute-start | bytes 884744 | tf_op jit(solution)/shard_map/ppermute | solution.py:52
  659.5 56.1 %collective-permute-start.36 = (bf16[96,2,768]{2,0,1:T(8,128)(2,1)}, bf16[96,2,768]{2,0,1:T(8,128)(2,1)}, u32[]{:S(2)}, u32[]{:S(2)}) collective-permute-start(bf16[96,2,768]{2,0,1:T(8,128)(2,1)} %bitcast.782), channel_id=1, source_target_pairs={{0,1},{1,0},{2,3},{3,2},{4,5},{5,4},{6,7},{7,6},{8,9},{9,8},{10,11... | collective-permute-start | bytes 884744 | tf_op jit(solution)/shard_map/ppermute | solution.py:52
  665.9 52.9 %collective-permute-start.26 = (bf16[96,2,768]{2,0,1:T(8,128)(2,1)}, bf16[96,2,768]{2,0,1:T(8,128)(2,1)}, u32[]{:S(2)}, u32[]{:S(2)}) collective-permute-start(bf16[96,2,768]{2,0,1:T(8,128)(2,1)} %bitcast.783), channel_id=1, source_target_pairs={{0,1},{1,0},{2,3},{3,2},{4,5},{5,4},{6,7},{7,6},{8,9},{9,8},{10,11... | collective-permute-start | bytes 884744 | tf_op jit(solution)/shard_map/ppermute | solution.py:52
  667.9 46.1 %collective-permute-start.56 = (bf16[2,96,768]{2,1,0:T(8,128)(2,1)}, bf16[2,96,768]{2,1,0:T(8,128)(2,1)}, u32[]{:S(2)}, u32[]{:S(2)}) collective-permute-start(bf16[2,96,768]{2,1,0:T(8,128)(2,1)} %dynamic-slice_bitcast_fusion.20), channel_id=1, source_target_pairs={{0,1},{1,0},{2,3},{3,2},{4,5},{5,4},{6,7},{7,6},{8,9},{9,8},{10,11... | collective-permute-start | bytes 884744 | tf_op jit(solution)/shard_map/ppermute | solution.py:52
  673.6 49.6 %collective-permute-start.46 = (bf16[2,96,768]{2,1,0:T(8,128)(2,1)}, bf16[2,96,768]{2,1,0:T(8,128)(2,1)}, u32[]{:S(2)}, u32[]{:S(2)}) collective-permute-start(bf16[2,96,768]{2,1,0:T(8,128)(2,1)} %dynamic-slice_bitcast_fusion.23), channel_id=1, source_target_pairs={{0,1},{1,0},{2,3},{3,2},{4,5},{5,4},{6,7},{7,6},{8,9},{9,8},{10,11... | collective-permute-start | bytes 884744 | tf_op jit(solution)/shard_map/ppermute | solution.py:52
  690.0 126.0 %collective-permute-start.10 = (bf16[2,2,96,1536]{3,2,0,1:T(8,128)(2,1)}, bf16[2,2,96,1536]{3,2,0,1:T(8,128)(2,1)}, u32[]{:S(2)}, u32[]{:S(2)}) collective-permute-start(bf16[2,2,96,1536]{3,2,0,1:T(8,128)(2,1)} %bitcast.780), channel_id=1, source_target_pairs={{0,4},{4,0},{8,12},{12,8},{16,20},{20,16},{24,28},{28,24},{1,5},{5... | collective-permute-start | bytes 3538952 | tf_op jit(solution)/shard_map/ppermute | solution.py:52
  714.0 105.2 %collective-permute-start.3 = (bf16[2,2,96,1536]{3,2,1,0:T(8,128)(2,1)}, bf16[2,2,96,1536]{3,2,1,0:T(8,128)(2,1)}, u32[]{:S(2)}, u32[]{:S(2)}) collective-permute-start(bf16[2,2,96,1536]{3,2,1,0:T(8,128)(2,1)} %dynamic-slice_bitcast_fusion.7), channel_id=1, source_target_pairs={{0,4},{4,0},{8,12},{12,8},{16,20},{20,16},{24,28},{28,24},{1,5},{5... | collective-permute-start | bytes 3538952 | tf_op jit(solution)/shard_map/ppermute | solution.py:52
  715.7 105.7 %collective-permute-start = (bf16[2,2,96,1536]{3,2,0,1:T(8,128)(2,1)}, bf16[2,2,96,1536]{3,2,0,1:T(8,128)(2,1)}, u32[]{:S(2)}, u32[]{:S(2)}) collective-permute-start(bf16[2,2,96,1536]{3,2,0,1:T(8,128)(2,1)} %bitcast.781), channel_id=1, source_target_pairs={{0,4},{4,0},{8,12},{12,8},{16,20},{20,16},{24,28},{28,24},{1,5},{5... | collective-permute-start | bytes 3538952 | tf_op jit(solution)/shard_map/ppermute | solution.py:52
  720.2 21.1 %collective-permute-start.37 = (bf16[96,768]{1,0:T(8,128)(2,1)S(1)}, bf16[96,768]{1,0:T(8,128)(2,1)}, u32[]{:S(2)}, u32[]{:S(2)}) collective-permute-start(bf16[96,768]{1,0:T(8,128)(2,1)S(1)} %dynamic-slice_bitcast_fusion.36), channel_id=1, source_target_pairs={{0,2},{1,3},{2,0},{3,1},{4,6},{5,7},{6,4},{7,5},{8,10},{9,11},{10,... | collective-permute-start | bytes 442376 | tf_op jit(solution)/shard_map/ppermute | solution.py:52
  741.3 19.1 %collective-permute-start.57 = (bf16[96,768]{1,0:T(8,128)(2,1)S(1)}, bf16[96,768]{1,0:T(8,128)(2,1)S(1)}, u32[]{:S(2)}, u32[]{:S(2)}) collective-permute-start(bf16[96,768]{1,0:T(8,128)(2,1)S(1)} %dynamic-slice_bitcast_fusion.34), channel_id=1, source_target_pairs={{0,2},{1,3},{2,0},{3,1},{4,6},{5,7},{6,4},{7,5},{8,10},{9,11},{10,... | collective-permute-start | bytes 442376 | tf_op jit(solution)/shard_map/ppermute | solution.py:52
  817.6 16.3 %collective-permute-start.11 = (bf16[2,96,1536]{2,1,0:T(8,128)(2,1)S(1)}, bf16[2,96,1536]{2,1,0:T(8,128)(2,1)S(1)}, u32[]{:S(2)}, u32[]{:S(2)}) collective-permute-start(bf16[2,96,1536]{2,1,0:T(8,128)(2,1)S(1)} %dynamic-slice_bitcast_fusion.17), channel_id=1, source_target_pairs={{0,8},{4,12},{8,0},{12,4},{16,24},{20,28},{24,16},{28,20},{1,9},{5... | collective-permute-start | bytes 1769480 | tf_op jit(solution)/shard_map/ppermute | solution.py:52
  820.8 14.7 %collective-permute-start.4 = (bf16[2,96,1536]{2,1,0:T(8,128)(2,1)S(1)}, bf16[2,96,1536]{2,1,0:T(8,128)(2,1)S(1)}, u32[]{:S(2)}, u32[]{:S(2)}) collective-permute-start(bf16[2,96,1536]{2,1,0:T(8,128)(2,1)S(1)} %dynamic-slice_bitcast_fusion.18), channel_id=1, source_target_pairs={{0,16},{4,20},{8,24},{12,28},{16,0},{20,4},{24,8},{28,12},{1,17},{... | collective-permute-start | bytes 1769480 | tf_op jit(solution)/shard_map/ppermute | solution.py:52
  823.1 19.4 %collective-permute-start.1 = (bf16[2,96,1536]{2,1,0:T(8,128)(2,1)S(1)}, bf16[2,96,1536]{2,1,0:T(8,128)(2,1)S(1)}, u32[]{:S(2)}, u32[]{:S(2)}) collective-permute-start(bf16[2,96,1536]{2,1,0:T(8,128)(2,1)S(1)} %dynamic-slice_bitcast_fusion.19), channel_id=1, source_target_pairs={{0,8},{4,12},{8,0},{12,4},{16,24},{20,28},{24,16},{28,20},{1,9},{5... | collective-permute-start | bytes 1769480 | tf_op jit(solution)/shard_map/ppermute | solution.py:52
  (196 other events, 2123.8 us)
Sparse Core Ops, SparseCore 0:
  23.0 37.4 all-gather.14
  62.4 24.0 all-gather.18
  89.0 38.9 all-gather.20
  129.7 38.9 all-gather.22
  170.4 33.9 all-gather.16
  206.2 24.0 all-gather.24
  232.8 38.9 all-gather.26
  274.2 38.8 all-gather.28

commit v3 on v2

--- a/solution.py
+++ b/solution.py
@@ -1,6 +1,8 @@
 import jax
 import jax.numpy as jnp
 from jax import lax
+from jax.experimental import pallas as pl
+from jax.experimental.pallas import tpu as pltpu
 from jax.sharding import PartitionSpec as P
 
 HD = 64
@@ -111,77 +113,87 @@
     return reduce_frames(jnp.concatenate([first, second], axis=1), axis)
 
 
-def attend(query_rows, key_rows, value_rows):
-    clips, length, local_heads, head_size = query_rows.shape
+def dot_of(left, right, left_dim, right_dim):
+    return lax.dot_general(
+        left, right, (((left_dim,), (right_dim,)), ((), ())), preferred_element_type=jnp.float32
+    )
+
+
+def attend_kernel(query_ref, key_ref, value_ref, mixed_ref, total_ref):
+    head_size, length = key_ref.shape[1:]
     block = min(512, length)
     scale = head_size ** (-0.5)
-
-    def one_block(start):
-        query_block = lax.dynamic_slice_in_dim(query_rows, start, block, 1)
-        scores = (
-            jnp.einsum("cqhd,ckhd->chqk", query_block, key_rows, preferred_element_type=jnp.float32)
-            * scale
-        )
-        highest = jnp.max(scores, axis=-1, keepdims=True)
+    keys = key_ref[0]
+    values = value_ref[0]
+    for start in range(0, length, block):
+        rows = slice(start, start + block)
+        scores = dot_of(keys, query_ref[0, :, rows], 0, 0) * scale
+        highest = jnp.max(scores, axis=0, keepdims=True)
         powered = jnp.exp(scores - highest)
-        summed = jnp.sum(powered, axis=-1, keepdims=True)
-        weights_low = (powered / summed).astype(jnp.bfloat16)
-        mixed = jnp.einsum(
-            "chqk,ckhd->cqhd", weights_low, value_rows, preferred_element_type=jnp.float32
-        )
-        return (mixed.astype(jnp.bfloat16), (highest + jnp.log(summed))[..., 0])
-
-    starts = jnp.arange(length // block, dtype=jnp.int32) * block
-    mixed, log_total = lax.map(one_block, starts)
-    mixed = jnp.moveaxis(mixed, 0, 1).reshape(clips, length, local_heads, head_size)
-    log_total = jnp.moveaxis(log_total, 0, 2).reshape(clips, local_heads, length)
-    return (mixed, log_total)
-
-
-def attend_back(query_rows, key_rows, value_rows, log_total, grad_mixed):
-    clips, length, local_heads, head_size = query_rows.shape
+        summed = jnp.sum(powered, axis=0, keepdims=True)
+        weights_low = (powered * (1.0 / summed)).astype(jnp.bfloat16)
+        mixed_ref[0, :, rows] = dot_of(values, weights_low, 1, 0).astype(jnp.bfloat16)
+        total_ref[0, :, rows] = highest + jnp.log(summed)
+
+
+def attend_back_kernel(
+    query_ref, key_ref, value_ref, total_ref, grad_ref, dq_ref, dk_ref, dv_ref
+):
+    head_size, length = key_ref.shape[1:]
     block = min(512, length)
     scale = head_size ** (-0.5)
-
-    def one_block(carry, start):
-        grad_keys, grad_values = carry
-        query_block = lax.dynamic_slice_in_dim(query_rows, start, block, 1)
-        grad_block = lax.dynamic_slice_in_dim(grad_mixed, start, block, 1)
-        total_block = lax.dynamic_slice_in_dim(log_total, start, block, 2)
-        scores = (
-            jnp.einsum("cqhd,ckhd->chqk", query_block, key_rows, preferred_element_type=jnp.float32)
-            * scale
-        )
-        weights_full = jnp.exp(scores - total_block[..., None])
-        grad_weights = jnp.einsum(
-            "cqhd,ckhd->chqk", grad_block, value_rows, preferred_element_type=jnp.float32
-        )
-        inner = jnp.sum(weights_full * grad_weights, axis=-1, keepdims=True)
-        grad_scores = (weights_full * (grad_weights - inner)).astype(jnp.bfloat16)
-        grad_query = (
-            jnp.einsum("chqk,ckhd->cqhd", grad_scores, key_rows, preferred_element_type=jnp.float32)
-            * scale
-        )
-        grad_keys = (
-            grad_keys
-            + jnp.einsum(
-                "chqk,cqhd->ckhd", grad_scores, query_block, preferred_element_type=jnp.float32
-            )
-            * scale
-        )
-        grad_values = grad_values + jnp.einsum(
-            "chqk,cqhd->ckhd",
-            weights_full.astype(jnp.bfloat16),
-            grad_block,
-            preferred_element_type=jnp.float32,
-        )
-        return ((grad_keys, grad_values), grad_query.astype(jnp.bfloat16))
-
-    starts = jnp.arange(length // block, dtype=jnp.int32) * block
-    zeros_start = jnp.zeros(key_rows.shape, jnp.float32)
-    (grad_keys, grad_values), grad_query = lax.scan(one_block, (zeros_start, zeros_start), starts)
-    grad_query = jnp.moveaxis(grad_query, 0, 1).reshape(clips, length, local_heads, head_size)
-    return (grad_query, grad_keys.astype(jnp.bfloat16), grad_values.astype(jnp.bfloat16))
+    keys = key_ref[0]
+    values = value_ref[0]
+    sum_keys = jnp.zeros((head_size, length), jnp.float32)
+    sum_values = jnp.zeros((head_size, length), jnp.float32)
+    for start in range(0, length, block):
+        rows = slice(start, start + block)
+        queries = query_ref[0, :, rows]
+        grads = grad_ref[0, :, rows]
+        weights = jnp.exp(dot_of(keys, queries, 0, 0) * scale - total_ref[0, :, rows])
+        grad_weights = dot_of(values, grads, 0, 0)
+        inner = jnp.sum(weights * grad_weights, axis=0, keepdims=True)
+        grad_scores = (weights * (grad_weights - inner)).astype(jnp.bfloat16)
+        dq_ref[0, :, rows] = (dot_of(keys, grad_scores, 1, 0) * scale).astype(jnp.bfloat16)
+        sum_keys = sum_keys + dot_of(queries, grad_scores, 1, 1)
+        sum_values = sum_values + dot_of(grads, weights.astype(jnp.bfloat16), 1, 1)
+    dk_ref[0] = (sum_keys * scale).astype(jnp.bfloat16)
+    dv_ref[0] = sum_values.astype(jnp.bfloat16)
+
+
+def call_heads(kernel, operands, results):
+    def spec(array):
+        return pl.BlockSpec((1,) + array.shape[1:], lambda i: (i, 0, 0))
+
+    return pl.pallas_call(
+        kernel,
+        grid=(operands[0].shape[0],),
+        in_specs=[spec(array) for array in operands],
+        out_specs=[spec(array) for array in results],
+        out_shape=results,
+        compiler_params=pltpu.CompilerParams(vmem_limit_bytes=40 * 1024 * 1024),
+    )(*operands)
+
+
+def attend(query_rows, key_rows, value_rows):
+    count, _, length = query_rows.shape
+    return call_heads(
+        attend_kernel,
+        (query_rows, key_rows, value_rows),
+        (
+            jax.ShapeDtypeStruct(query_rows.shape, jnp.bfloat16),
+            jax.ShapeDtypeStruct((count, 1, length), jnp.float32),
+        ),
+    )
+
+
+def attend_back(query_rows, key_rows, value_rows, log_total, grad_mixed):
+    shape = jax.ShapeDtypeStruct(query_rows.shape, jnp.bfloat16)
+    return call_heads(
+        attend_back_kernel,
+        (query_rows, key_rows, value_rows, log_total, grad_mixed),
+        (shape, shape, shape),
+    )
 
 
 def local(
@@ -232,8 +244,9 @@
             weight_qkv = first[:, : 3 * width]
         else:
             weight_qkv = gather_rows(w_qkv[layer_index].reshape(shard, -1))
-        weight_out = gather_rows(w_out[layer_index])
-        weight_up = gather_rows(w_up[layer_index])
+        both = gather_rows(jnp.concatenate([w_out[layer_index], w_up[layer_index]], axis=1))
+        weight_out = both[:, :width]
+        weight_up = both[:, width:]
         weight_down = gather_rows(w_down[layer_index])
         vector_full = vectors[:, layer_index * count : (layer_index + 1) * count].astype(
             jnp.float32
@@ -249,25 +262,24 @@
         )
         projected = (product(normed, weight_qkv) + bias_qkv).astype(jnp.bfloat16)
         heads = lax.all_to_all(
-            projected.reshape(clips, frames, 3, groups, width // groups),
+            jnp.transpose(projected.reshape(clips, frames, 3, width), (0, 2, 3, 1)),
             "sp",
-            split_axis=3,
+            split_axis=2,
+            concat_axis=3,
+            tiled=True,
+        )
+        query_rows = heads[:, 0].reshape(clips * local_heads, HD, length)
+        key_rows = heads[:, 1].reshape(clips * local_heads, HD, length)
+        value_rows = heads[:, 2].reshape(clips * local_heads, HD, length)
+        mixed, log_total = attend(query_rows, key_rows, value_rows)
+        returned = lax.all_to_all(
+            mixed.reshape(clips, width // groups, length),
+            "sp",
+            split_axis=2,
             concat_axis=1,
             tiled=True,
         )
-        heads = heads.reshape(clips, length, 3, local_heads, HD)
-        query_rows = heads[:, :, 0]
-        key_rows = heads[:, :, 1]
-        value_rows = heads[:, :, 2]
-        mixed, log_total = attend(query_rows, key_rows, value_rows)
-        returned = lax.all_to_all(
-            mixed.reshape(clips, length, 1, width // groups),
-            "sp",
-            split_axis=1,
-            concat_axis=2,
-            tiled=True,
-        )
-        mixed_rows = returned.reshape(rows_all, width)
+        mixed_rows = jnp.swapaxes(returned, 1, 2).reshape(rows_all, width)
         middle = stream + product(mixed_rows, weight_out) + branch[:, 0]
         normed_two = norm_rows(middle, gains[:, 1], shifts[:, 1]).astype(jnp.bfloat16)
         pre_act = product(normed_two, weight_up) + up_shift
@@ -334,22 +346,19 @@
         grad_out_bias = column_sums(grad_branch_one)
         grad_mixed = product_back(grad_branch_one, weight_out).astype(jnp.bfloat16)
         grad_heads = lax.all_to_all(
-            grad_mixed.reshape(clips, frames, groups, width // groups),
+            jnp.swapaxes(grad_mixed.reshape(clips, frames, width), 1, 2),
             "sp",
-            split_axis=2,
-            concat_axis=1,
+            split_axis=1,
+            concat_axis=2,
             tiled=True,
         )
-        grad_heads = grad_heads.reshape(clips, length, local_heads, HD)
-        grad_query, grad_key, grad_value = attend_back(
-            query_rows, key_rows, value_rows, log_total, grad_heads
-        )
-        stacked = jnp.stack([grad_query, grad_key, grad_value], axis=2).reshape(
-            clips, length, 3, 1, width // groups
-        )
-        grad_proj = lax.all_to_all(stacked, "sp", split_axis=1, concat_axis=3, tiled=True).reshape(
-            rows_all, 3 * width
-        )
+        grad_heads = grad_heads.reshape(clips * local_heads, HD, length)
+        grad_parts = attend_back(query_rows, key_rows, value_rows, log_total, grad_heads)
+        stacked = jnp.stack(
+            [part.reshape(clips, width // groups, length) for part in grad_parts], axis=1
+        )
+        grad_proj = lax.all_to_all(stacked, "sp", split_axis=3, concat_axis=2, tiled=True)
+        grad_proj = jnp.transpose(grad_proj, (0, 3, 1, 2)).reshape(rows_all, 3 * width)
         grad_qkv = outer_sum(normed, grad_proj)
         proj_sums = column_sums(grad_proj)
         grad_norm_one = product_back(grad_proj, weight_qkv)

time: 912 us -> 814 us (0.89)
  waiting for transfers between devices: 338 us -> 242 us
  blocking collectives: 0 us -> 84.2 us
  matrix products: 148 us -> 81.1 us
  local copies, waits for them, and re-layouts: 203 us -> 159 us
  Pallas kernels: 0 us -> 35.1 us
  starting transfers between devices: 81.3 us -> 98.3 us
  loops' own time: 15.3 us -> 0 us
  other arithmetic: 99.4 us -> 88.3 us
    all_to_all x0 -> x2, blocking collectives: none -> 84.2 us  [local(): lax.all_to_all(jnp.transpose(projected.reshape(clips, frames, 3, width),...]
    dot_general x28 -> x0, matrix products: 72.1 us -> none  [the longest x8 16.8 us: one_block(): jnp.einsum('cqhd,ckhd->chqk', query_block, key_rows, preferred_element_ty...]
    all_to_all x8 -> x6, waiting for transfers between devices: 107 us -> 49.1 us  [the longest x2 21.3 us: local(): lax.all_to_all(stacked, 'sp', split_axis=3, concat_axis=2, tiled=True)]
    pallas_call x0 -> x4, Pallas kernels: none -> 35.1 us  [call_heads(): pl.pallas_call(kernel, grid=(operands[0].shape[0],), in_specs=[spec(array...]
    all_gather x8 -> x6, waiting for transfers between devices: 73.5 us -> 48.7 us  [gather_rows(): return lax.all_gather(shard, 'fsdp', axis=0, tiled=True)]
    ppermute x51, waiting for transfers between devices: 104 us -> 88.2 us  [exchange_halves(): lax.ppermute(sent, axis_name, [(i, i ^ 1 << bit) for i in range(size)])]
    ppermute x51, starting transfers between devices: 41.8 us -> 57.6 us  [exchange_halves(): lax.ppermute(sent, axis_name, [(i, i ^ 1 << bit) for i in range(size)])]
    another operation x4 -> x0, loops' own time: 15.3 us -> none  [the longest x2 7.85 us: attend(): mixed, log_total = lax.map(one_block, starts)]
  transfers between devices with their start and end apart: 81 -> 77, of which waited for: 43 -> 36; matrix products, arithmetic and copies ran while one was open for 41% -> 31% of each run, Pallas kernels for 0% -> 4%
where the time goes in v3:
time: 814 us; the launch traced here: 805 us
  waiting for transfers between devices  242 us (30%)
  local copies, waits for them, and re-layouts  159 us (20%)
  starting transfers between devices  98.3 us (12%)
  other arithmetic  88.3 us (11%)
  blocking collectives  84.2 us (10%)
  matrix products  81.1 us (10%)
  Pallas kernels  35.1 us (4%)
  between operations  17.2 us (2%)
    ppermute x51, waiting for transfers between devices, exchange_halves(): lax.ppermute(sent, axis_name, [(i, i ^ 1 << bit) for i in range(size)])  88.2 us
    all_to_all x2, blocking collectives, local(): lax.all_to_all(jnp.transpose(projected.reshape(clips, frames, 3, width),...  84.2 us
    ppermute x51, starting transfers between devices, exchange_halves(): lax.ppermute(sent, axis_name, [(i, i ^ 1 << bit) for i in range(size)])  57.6 us
    all_gather x6, waiting for transfers between devices, gather_rows(): return lax.all_gather(shard, 'fsdp', axis=0, tiled=True)  48.7 us
    ppermute x12, waiting for transfers between devices, gather_halves(): lax.ppermute(part, axis_name, [(i, i ^ 1 << bit) for i in range(size)])  48.1 us
    dot_general x8, matrix products, product(): return jnp.dot(left, right, preferred_element_type=jnp.float32)  43 us
    convert_element_type x48, other arithmetic, exchange_halves(): (kept.astype(jnp.float32) + got.astype(jnp.float32)).astype(parts.dtype)  36.2 us
    pallas_call x4, Pallas kernels, call_heads(): pl.pallas_call(kernel, grid=(operands[0].shape[0],), in_specs=[spec(array...  35.1 us
  transfers between devices with their start and end apart: 77, of which 36 were waited for; matrix products, arithmetic and copies ran while one was open for 31% of the time, Pallas kernels for 4%

profile of v3, /device:TPU:0, one launch (start us, length us, event | category | flops | bytes accessed | tf_op | source)
XLA Modules:
  0.0 805.1 jit_solution(16390951602623128081)
XLA Ops:
  20.7 31.6 %all-gather.9.cloned.1.call-done = bf16[768,2432]{1,0:T(8,128)(2,1)} async-done(((bf16[96,2432]{1,0:T(8,128)(2,1)}), bf16[768,2432]{1,0:T(8,128)(2,1)}) %all-gather.9.cloned.1.call-update) | async-done | bytes 3735568 | tf_op jit(solution)/shard_map/all_gather | solution.py:42
  62.8 42.0 %all_to_all.138 = bf16[1,3,768,256]{3,1,0,2:T(4,128)(2,1)S(1)} all-to-all(bf16[1,3,768,256]{3,1,0,2:T(4,128)(2,1)S(1)} %copy.240), channel_id=1, replica_groups=mesh['fsdp'=8,'sp'=4] {'sp'}, dimensions={2} | all-to-all | bytes 2359296 | tf_op jit(solution)/shard_map/all_to_all | solution.py:264
  105.2 6.6 shard_map.194
  114.2 4.8 reduce.47
  124.9 10.2 %all-to-all-done.1 = bf16[4,2,24576]{2,1,0:T(2,128)(2,1)S(1)} async-done(((bf16[4,2,24576]{2,1,0:T(2,128)(2,1)}), bf16[4,2,24576]{2,1,0:T(2,128)(2,1)S(1)}, u32[]{:S(2)}, u32[]{:S(2)}) %all-to-all-start.1) | async-done | bytes 393248 | tf_op jit(solution)/shard_map/all_to_all | solution.py:275
  142.0 11.6 %multiply_convert_fusion.1 = (bf16[256,3072]{1,0:T(8,128)(2,1)}, f32[256,3072]{1,0:T(8,128)}, f32[256,3072]{1,0:T(8,128)}) fusion(f32[3072]{0:T(1024)S(1)} %add.506, bf16[768,3840]{1,0:T(8,128)(2,1)} %all-gather.11.cloned.1.call-done, f32[256,768]{1,0:T(8,128)S(1)} %get-tuple-element.220, f32[768]{0:T(1024)S(1)} %get-tuple-element.97, ...), kind=kOutput, calls=%fused_computation.49 | convolution fusion | flops 1260847104 | bytes 13389824 | tf_op jit(solution)/shard_map/dot_general | solution.py:26
  153.7 4.3 fusion.190
  158.3 16.9 %all-gather.13.cloned.1.call-done = bf16[768,2304]{1,0:T(8,128)(2,1)} async-done(((bf16[96,2304]{1,0:T(8,128)(2,1)}), bf16[768,2304]{1,0:T(8,128)(2,1)}) %all-gather.13.cloned.1.call-update) | async-done | bytes 3538960 | tf_op jit(solution)/shard_map/all_gather | solution.py:42
  175.3 4.2 fusion.23
  182.1 42.2 %all_to_all.139 = bf16[1,3,768,256]{3,1,0,2:T(4,128)(2,1)S(1)} all-to-all(bf16[1,3,768,256]{3,1,0,2:T(4,128)(2,1)S(1)} %copy.248), channel_id=1, replica_groups=mesh['fsdp'=8,'sp'=4] {'sp'}, dimensions={2} | all-to-all | bytes 2359296 | tf_op jit(solution)/shard_map/all_to_all | solution.py:264
  224.7 6.6 shard_map.195
  233.3 4.8 reduce.48
  239.5 4.1 all-to-all-start.3
  244.6 10.3 %all-to-all-done.3 = bf16[4,2,24576]{2,1,0:T(2,128)(2,1)} async-done(((bf16[4,2,24576]{2,1,0:T(2,128)(2,1)}), bf16[4,2,24576]{2,1,0:T(2,128)(2,1)}, u32[]{:S(2)}, u32[]{:S(2)}) %all-to-all-start.3) | async-done | bytes 393248 | tf_op jit(solution)/shard_map/all_to_all | solution.py:275
  265.9 11.8 %multiply_convert_fusion = (bf16[256,3072]{1,0:T(8,128)(2,1)}, f32[256,3072]{1,0:T(8,128)}, f32[256,3072]{1,0:T(8,128)}) fusion(f32[3072]{0:T(1024)S(1)} %copy-done.124, bf16[768,3840]{1,0:T(8,128)(2,1)} %all-gather.15.cloned.1.call-done, f32[256,768]{1,0:T(8,128)S(1)} %get-tuple-element.225, f32[768]{0:T(1024)S(1)} %copy-done.95, f32[768]{0:T(1024)S(1)} %copy-done.86, ...), kind=kOutput, calls=%fused_computation.36 | convolution fusion | flops 1260847104 | bytes 13389824 | tf_op jit(solution)/shard_map/dot_general | solution.py:26
  277.8 6.9 convert_reduce_fusion
  302.9 3.9 reduce.49
  311.3 5.0 fusion.74
  316.3 7.3 all-to-all-done.4
  325.3 10.9 %shard_map.196 = (bf16[3,64,1024]{2,1,0:T(8,128)(2,1)S(1)}, bf16[3,64,1024]{2,1,0:T(8,128)(2,1)S(1)}, bf16[3,64,1024]{2,1,0:T(8,128)(2,1)S(1)}) custom-call(bf16[3,64,1024]{2,1,0:T(8,128)(2,1)S(1)} %bitcast.619, bf16[3,64,1024]{2,1,0:T(8,128)(2,1)S(1)} %bitcast.617, bf16[3,64,1024]{2,1,0:T(8,128)(2,1)S(1)} %bitcast.615, f32[3,1,1024]{2,1,0:T(1,128)S(1)} %copy-done.2, ...), custom_call_target="tpu_custom_call" | custom-call | tf_op jit(solution)/shard_map/pallas_call | solution.py:168
  351.3 4.9 pad_maximum_fusion.3
  366.7 7.3 collective-permute-done.34
  386.0 21.3 %all-to-all-done.5 = bf16[1,3,192,1024]{2,1,0,3:T(4,128)(2,1)S(1)} async-done(((bf16[1,3,192,1024]{2,1,0,3:T(4,128)(2,1)}), bf16[1,3,192,1024]{2,1,0,3:T(4,128)(2,1)S(1)}, u32[]{:S(2)}, u32[]{:S(2)}) %all-to-all-start.5) | async-done | bytes 1179680 | tf_op jit(solution)/shard_map/all_to_all | solution.py:360
  408.7 4.4 copy.301
  420.3 3.9 convolution_convert_fusion.1
  427.0 3.7 convolution_convert_fusion.3
  482.6 11.0 %shard_map.197 = (bf16[3,64,1024]{2,1,0:T(8,128)(2,1)S(1)}, bf16[3,64,1024]{2,1,0:T(8,128)(2,1)S(1)}, bf16[3,64,1024]{2,1,0:T(8,128)(2,1)S(1)}) custom-call(bf16[3,64,1024]{2,1,0:T(8,128)(2,1)S(1)} %bitcast.613, bf16[3,64,1024]{2,1,0:T(8,128)(2,1)S(1)} %bitcast.611, bf16[3,64,1024]{2,1,0:T(8,128)(2,1)S(1)} %bitcast.609, ...), custom_call_target="tpu_custom_call" | custom-call | tf_op jit(solution)/shard_map/pallas_call | solution.py:168
  497.2 6.0 pad_maximum_fusion.4
  503.2 5.4 all-to-all-start.7
  524.7 4.7 collective-permute-done.41
  533.5 8.5 %collective-permute-done.51 = bf16[2,384,384]{2,1,0:T(8,128)(2,1)S(1)} collective-permute-done((bf16[2,384,384]{2,1,0:T(8,128)(2,1)S(1)}, bf16[2,384,384]{2,1,0:T(8,128)(2,1)S(1)}, u32[]{:S(2)}, u32[]{:S(2)}) %collective-permute-start.51) | collective-permute-done | bytes 589856 | tf_op jit(solution)/shard_map/ppermute | solution.py:54
  543.3 11.3 %collective-permute-done.21 = bf16[2,96,1536]{2,1,0:T(8,128)(2,1)S(1)} collective-permute-done((bf16[2,96,1536]{2,1,0:T(8,128)(2,1)S(1)}, bf16[2,96,1536]{2,1,0:T(8,128)(2,1)S(1)}, u32[]{:S(2)}, u32[]{:S(2)}) %collective-permute-start.21) | collective-permute-done | bytes 589856 | tf_op jit(solution)/shard_map/ppermute | solution.py:54
  557.3 10.0 %collective-permute-done.31 = bf16[2,96,1536]{2,1,0:T(8,128)(2,1)S(1)} collective-permute-done((bf16[2,96,1536]{2,1,0:T(8,128)(2,1)S(1)}, bf16[2,96,1536]{2,1,0:T(8,128)(2,1)S(1)}, u32[]{:S(2)}, u32[]{:S(2)}) %collective-permute-start.31) | collective-permute-done | bytes 589856 | tf_op jit(solution)/shard_map/ppermute | solution.py:54
  590.5 4.6 copy.302
  627.3 6.0 collective-permute-done.63
  647.5 9.0 %collective-permute-done.48 = bf16[96,768]{1,0:T(8,128)(2,1)S(1)} collective-permute-done((bf16[96,768]{1,0:T(8,128)(2,1)S(1)}, bf16[96,768]{1,0:T(8,128)(2,1)S(1)}, u32[]{:S(2)}, u32[]{:S(2)}) %collective-permute-start.48) | collective-permute-done | bytes 147488 | tf_op jit(solution)/shard_map/ppermute | solution.py:61
  659.5 6.5 collective-permute-done.28
  668.9 3.8 collective-permute-start.29
  678.8 4.2 collective-permute-done.29
  685.1 4.2 collective-permute-done.39
  709.0 9.7 %collective-permute-done.1 = bf16[2,96,1536]{2,1,0:T(8,128)(2,1)S(1)} collective-permute-done((bf16[2,96,1536]{2,1,0:T(8,128)(2,1)S(1)}, bf16[2,96,1536]{2,1,0:T(8,128)(2,1)S(1)}, u32[]{:S(2)}, u32[]{:S(2)}) %collective-permute-start.1) | collective-permute-done | bytes 589856 | tf_op jit(solution)/shard_map/ppermute | solution.py:54
  721.5 9.8 %collective-permute-done.11 = bf16[2,96,1536]{2,1,0:T(8,128)(2,1)S(1)} collective-permute-done((bf16[2,96,1536]{2,1,0:T(8,128)(2,1)S(1)}, bf16[2,96,1536]{2,1,0:T(8,128)(2,1)S(1)}, u32[]{:S(2)}, u32[]{:S(2)}) %collective-permute-start.11) | collective-permute-done | bytes 589856 | tf_op jit(solution)/shard_map/ppermute | solution.py:54
  742.1 4.2 collective-permute-done.6
  746.3 5.3 collective-permute-start.7
  751.8 6.6 collective-permute-start.17
  758.5 9.9 %collective-permute-done.17 = bf16[96,768]{1,0:T(8,128)(2,1)S(1)} collective-permute-done((bf16[96,768]{1,0:T(8,128)(2,1)S(1)}, bf16[96,768]{1,0:T(8,128)(2,1)S(1)}, u32[]{:S(2)}, u32[]{:S(2)}) %collective-permute-start.17) | collective-permute-done | bytes 147488 | tf_op jit(solution)/shard_map/ppermute | solution.py:54
  768.5 6.3 collective-permute-done.8
  777.4 7.5 collective-permute-done.9
  (767 shorter events, 341.7 us)
Async XLA Ops:
  7.2 45.1 %all-gather.9.cloned.1.call-start = ((), (), s32[]{:S(2)}) async-start(), calls=%async_computation.8 | async-start | bytes 4202496 | tf_op jit(solution)/shard_map/all_gather | solution.py:42
  14.7 125.1 %all-gather.11.cloned.1.call-start = ((), (), s32[]{:S(2)}) async-start(), calls=%async_computation.9 | async-start | bytes 6635520 | tf_op jit(solution)/shard_map/all_gather | solution.py:42
  15.8 137.9 %all-gather.17.cloned.1.call-start = ((), (), s32[]{:S(2)}) async-start(), calls=%async_computation.12 | async-start | bytes 5308416 | tf_op jit(solution)/shard_map/all_gather | solution.py:42
  17.4 157.8 %all-gather.13.cloned.1.call-start = ((), (), s32[]{:S(2)}) async-start(), calls=%async_computation.10 | async-start | bytes 3981312 | tf_op jit(solution)/shard_map/all_gather | solution.py:42
  18.7 244.2 %all-gather.15.cloned.1.call-start = ((), (), s32[]{:S(2)}) async-start(), calls=%async_computation.11 | async-start | bytes 6635520 | tf_op jit(solution)/shard_map/all_gather | solution.py:42
  123.9 153.8 %all-gather.19.cloned.1.call-start = ((), (), s32[]{:S(2)}) async-start(), calls=%async_computation.13 | async-start | bytes 5308416 | tf_op jit(solution)/shard_map/all_gather | solution.py:42
  239.5 15.4 %all-to-all-start.3 = ((bf16[4,2,24576]{2,1,0:T(2,128)(2,1)}), bf16[4,2,24576]{2,1,0:T(2,128)(2,1)}, u32[]{:S(2)}, u32[]{:S(2)}) async-start(bf16[4,2,24576]{2,1,0:T(2,128)(2,1)} %reshape.612), calls=%async_computation.3 | async-start | bytes 786432 | tf_op jit(solution)/shard_map/all_to_all | solution.py:275
  294.2 49.2 %collective-permute-start.53 = (bf16[2,2,384,384]{3,2,1,0:T(8,128)(2,1)}, bf16[2,2,384,384]{3,2,1,0:T(8,128)(2,1)}, u32[]{:S(2)}, u32[]{:S(2)}) collective-permute-start(bf16[2,2,384,384]{3,2,1,0:T(8,128)(2,1)} %dynamic-slice_bitcast_fusion), channel_id=1, source_target_pairs={{0,4},{4,0},{8,12},{12,8},{16,20},{20,16},{24,28},{28,24},{1,5},{5... | collective-permute-start | bytes 3538952 | tf_op jit(solution)/shard_map/ppermute | solution.py:54
  297.3 50.4 %collective-permute-start.33 = (bf16[2,2,96,1536]{3,2,1,0:T(8,128)(2,1)}, bf16[2,2,96,1536]{3,2,1,0:T(8,128)(2,1)}, u32[]{:S(2)}, u32[]{:S(2)}) collective-permute-start(bf16[2,2,96,1536]{3,2,1,0:T(8,128)(2,1)} %dynamic-slice_bitcast_fusion.2), channel_id=1, source_target_pairs={{0,4},{4,0},{8,12},{12,8},{16,20},{20,16},{24,28},{28,24},{1,5},{5... | collective-permute-start | bytes 3538952 | tf_op jit(solution)/shard_map/ppermute | solution.py:54
  307.6 15.9 %all-to-all-start.4 = ((bf16[4,2,24576]{2,1,0:T(2,128)(2,1)}), bf16[4,2,24576]{2,1,0:T(2,128)(2,1)S(1)}, u32[]{:S(2)}, u32[]{:S(2)}) async-start(bf16[4,2,24576]{2,1,0:T(2,128)(2,1)} %reshape.614), calls=%async_computation.4 | async-start | bytes 786432 | tf_op jit(solution)/shard_map/all_to_all | solution.py:348
  346.4 16.6 %collective-permute-start.54 = (bf16[2,384,384]{2,1,0:T(8,128)(2,1)}, bf16[2,384,384]{2,1,0:T(8,128)(2,1)}, u32[]{:S(2)}, u32[]{:S(2)}) collective-permute-start(bf16[2,384,384]{2,1,0:T(8,128)(2,1)} %dynamic-slice_bitcast_fusion.6), channel_id=1, source_target_pairs={{0,16},{4,20},{8,24},{12,28},{16,0},{20,4},{24,8},{28,12},{1,17},{... | collective-permute-start | bytes 1769480 | tf_op jit(solution)/shard_map/ppermute | solution.py:54
  350.5 23.5 %collective-permute-start.34 = (bf16[2,96,1536]{2,1,0:T(8,128)(2,1)}, bf16[2,96,1536]{2,1,0:T(8,128)(2,1)}, u32[]{:S(2)}, u32[]{:S(2)}) collective-permute-start(bf16[2,96,1536]{2,1,0:T(8,128)(2,1)} %dynamic-slice_bitcast_fusion.10), channel_id=1, source_target_pairs={{0,16},{4,20},{8,24},{12,28},{16,0},{20,4},{24,8},{28,12},{1,17},{... | collective-permute-start | bytes 1769480 | tf_op jit(solution)/shard_map/ppermute | solution.py:54
  356.2 51.1 %all-to-all-start.5 = ((bf16[1,3,192,1024]{2,1,0,3:T(4,128)(2,1)}), bf16[1,3,192,1024]{2,1,0,3:T(4,128)(2,1)S(1)}, u32[]{:S(2)}, u32[]{:S(2)}) async-start(bf16[1,3,192,1024]{2,1,0,3:T(4,128)(2,1)} %pad_maximum_fusion.3), calls=%async_computation.5 | async-start | bytes 4194304 | tf_op jit(solution)/shard_map/all_to_all | solution.py:360
  365.2 17.2 %collective-permute-start.55 = (bf16[384,384]{1,0:T(8,128)(2,1)}, bf16[384,384]{1,0:T(8,128)(2,1)}, u32[]{:S(2)}, u32[]{:S(2)}) collective-permute-start(bf16[384,384]{1,0:T(8,128)(2,1)} %dynamic-slice_bitcast_fusion.19), channel_id=1, source_target_pairs={{0,8},{4,12},{8,0},{12,4},{16,24},{20,28},{24,16},{28,20},{1,9},{5... | collective-permute-start | bytes 884744 | tf_op jit(solution)/shard_map/ppermute | solution.py:54
  440.9 40.6 %all-to-all-start.6 = ((bf16[4,2,24576]{2,1,0:T(2,128)(2,1)}), bf16[4,2,24576]{2,1,0:T(2,128)(2,1)S(1)}, u32[]{:S(2)}, u32[]{:S(2)}) async-start(bf16[4,2,24576]{2,1,0:T(2,128)(2,1)} %reshape.616), calls=%async_computation.6 | async-start | bytes 786432 | tf_op jit(solution)/shard_map/all_to_all | solution.py:348
  456.6 54.2 %collective-permute-start.40 = (bf16[2,2,384,384]{3,2,0,1:T(8,128)(2,1)}, bf16[2,2,384,384]{3,2,0,1:T(8,128)(2,1)}, u32[]{:S(2)}, u32[]{:S(2)}) collective-permute-start(bf16[2,2,384,384]{3,2,0,1:T(8,128)(2,1)} %bitcast.599), channel_id=1, source_target_pairs={{0,4},{4,0},{8,12},{12,8},{16,20},{20,16},{24,28},{28,24},{1,5},{5... | collective-permute-start | bytes 3538952 | tf_op jit(solution)/shard_map/ppermute | solution.py:54
  457.8 50.9 %collective-permute-start.43 = (bf16[2,2,384,384]{3,2,1,0:T(8,128)(2,1)}, bf16[2,2,384,384]{3,2,1,0:T(8,128)(2,1)}, u32[]{:S(2)}, u32[]{:S(2)}) collective-permute-start(bf16[2,2,384,384]{3,2,1,0:T(8,128)(2,1)} %dynamic-slice_bitcast_fusion.1), channel_id=1, source_target_pairs={{0,4},{4,0},{8,12},{12,8},{16,20},{20,16},{24,28},{28,24},{1,5},{5... | collective-permute-start | bytes 3538952 | tf_op jit(solution)/shard_map/ppermute | solution.py:54
  459.5 56.6 %collective-permute-start.50 = (bf16[2,2,384,384]{3,2,0,1:T(8,128)(2,1)}, bf16[2,2,384,384]{3,2,0,1:T(8,128)(2,1)}, u32[]{:S(2)}, u32[]{:S(2)}) collective-permute-start(bf16[2,2,384,384]{3,2,0,1:T(8,128)(2,1)} %bitcast.598), channel_id=1, source_target_pairs={{0,4},{4,0},{8,12},{12,8},{16,20},{20,16},{24,28},{28,24},{1,5},{5... | collective-permute-start | bytes 3538952 | tf_op jit(solution)/shard_map/ppermute | solution.py:54
  464.8 48.3 %collective-permute-start.20 = (bf16[2,2,96,1536]{3,2,0,1:T(8,128)(2,1)}, bf16[2,2,96,1536]{3,2,0,1:T(8,128)(2,1)}, u32[]{:S(2)}, u32[]{:S(2)}) collective-permute-start(bf16[2,2,96,1536]{3,2,0,1:T(8,128)(2,1)} %bitcast.601), channel_id=1, source_target_pairs={{0,4},{4,0},{8,12},{12,8},{16,20},{20,16},{24,28},{28,24},{1,5},{5... | collective-permute-start | bytes 3538952 | tf_op jit(solution)/shard_map/ppermute | solution.py:54
  465.9 52.9 %collective-permute-start.23 = (bf16[2,2,96,1536]{3,2,1,0:T(8,128)(2,1)}, bf16[2,2,96,1536]{3,2,1,0:T(8,128)(2,1)}, u32[]{:S(2)}, u32[]{:S(2)}) collective-permute-start(bf16[2,2,96,1536]{3,2,1,0:T(8,128)(2,1)} %dynamic-slice_bitcast_fusion.3), channel_id=1, source_target_pairs={{0,4},{4,0},{8,12},{12,8},{16,20},{20,16},{24,28},{28,24},{1,5},{5... | collective-permute-start | bytes 3538952 | tf_op jit(solution)/shard_map/ppermute | solution.py:54
  503.2 87.2 %all-to-all-start.7 = ((bf16[1,3,192,1024]{2,1,0,3:T(4,128)(2,1)}), bf16[1,3,192,1024]{2,1,0,3:T(4,128)(2,1)}, u32[]{:S(2)}, u32[]{:S(2)}) async-start(bf16[1,3,192,1024]{2,1,0,3:T(4,128)(2,1)} %pad_maximum_fusion.4), calls=%async_computation.7 | async-start | bytes 4194304 | tf_op jit(solution)/shard_map/all_to_all | solution.py:360
  513.1 16.2 %collective-permute-start.41 = (bf16[2,384,384]{2,1,0:T(8,128)(2,1)S(1)}, bf16[2,384,384]{2,1,0:T(8,128)(2,1)S(1)}, u32[]{:S(2)}, u32[]{:S(2)}) collective-permute-start(bf16[2,384,384]{2,1,0:T(8,128)(2,1)S(1)} %dynamic-slice_bitcast_fusion.9), channel_id=1, source_target_pairs={{0,8},{4,12},{8,0},{12,4},{16,24},{20,28},{24,16},{28,20},{1,9},{5... | collective-permute-start | bytes 1769480 | tf_op jit(solution)/shard_map/ppermute | solution.py:54
  516.1 16.3 %collective-permute-start.44 = (bf16[2,384,384]{2,1,0:T(8,128)(2,1)S(1)}, bf16[2,384,384]{2,1,0:T(8,128)(2,1)S(1)}, u32[]{:S(2)}, u32[]{:S(2)}) collective-permute-start(bf16[2,384,384]{2,1,0:T(8,128)(2,1)S(1)} %dynamic-slice_bitcast_fusion.8), channel_id=1, source_target_pairs={{0,16},{4,20},{8,24},{12,28},{16,0},{20,4},{24,8},{28,12},{1,17},{... | collective-permute-start | bytes 1769480 | tf_op jit(solution)/shard_map/ppermute | solution.py:54
  518.8 23.2 %collective-permute-start.51 = (bf16[2,384,384]{2,1,0:T(8,128)(2,1)S(1)}, bf16[2,384,384]{2,1,0:T(8,128)(2,1)S(1)}, u32[]{:S(2)}, u32[]{:S(2)}) collective-permute-start(bf16[2,384,384]{2,1,0:T(8,128)(2,1)S(1)} %dynamic-slice_bitcast_fusion.7), channel_id=1, source_target_pairs={{0,8},{4,12},{8,0},{12,4},{16,24},{20,28},{24,16},{28,20},{1,9},{5... | collective-permute-start | bytes 1769480 | tf_op jit(solution)/shard_map/ppermute | solution.py:54
  521.6 33.1 %collective-permute-start.21 = (bf16[2,96,1536]{2,1,0:T(8,128)(2,1)S(1)}, bf16[2,96,1536]{2,1,0:T(8,128)(2,1)S(1)}, u32[]{:S(2)}, u32[]{:S(2)}) collective-permute-start(bf16[2,96,1536]{2,1,0:T(8,128)(2,1)S(1)} %dynamic-slice_bitcast_fusion.13), channel_id=1, source_target_pairs={{0,8},{4,12},{8,0},{12,4},{16,24},{20,28},{24,16},{28,20},{1,9},{5... | collective-permute-start | bytes 1769480 | tf_op jit(solution)/shard_map/ppermute | solution.py:54
  523.0 33.1 %collective-permute-start.24 = (bf16[2,96,1536]{2,1,0:T(8,128)(2,1)S(1)}, bf16[2,96,1536]{2,1,0:T(8,128)(2,1)S(1)}, u32[]{:S(2)}, u32[]{:S(2)}) collective-permute-start(bf16[2,96,1536]{2,1,0:T(8,128)(2,1)S(1)} %dynamic-slice_bitcast_fusion.12), channel_id=1, source_target_pairs={{0,16},{4,20},{8,24},{12,28},{16,0},{20,4},{24,8},{28,12},{1,17},{... | collective-permute-start | bytes 1769480 | tf_op jit(solution)/shard_map/ppermute | solution.py:54
  529.4 37.9 %collective-permute-start.31 = (bf16[2,96,1536]{2,1,0:T(8,128)(2,1)S(1)}, bf16[2,96,1536]{2,1,0:T(8,128)(2,1)S(1)}, u32[]{:S(2)}, u32[]{:S(2)}) collective-permute-start(bf16[2,96,1536]{2,1,0:T(8,128)(2,1)S(1)} %dynamic-slice_bitcast_fusion.11), channel_id=1, source_target_pairs={{0,8},{4,12},{8,0},{12,4},{16,24},{20,28},{24,16},{28,20},{1,9},{5... | collective-permute-start | bytes 1769480 | tf_op jit(solution)/shard_map/ppermute | solution.py:54
  532.3 36.2 %collective-permute-start.14 = (bf16[2,96,1536]{2,1,0:T(8,128)(2,1)S(1)}, bf16[2,96,1536]{2,1,0:T(8,128)(2,1)S(1)}, u32[]{:S(2)}, u32[]{:S(2)}) collective-permute-start(bf16[2,96,1536]{2,1,0:T(8,128)(2,1)S(1)} %dynamic-slice_bitcast_fusion.14), channel_id=1, source_target_pairs={{0,16},{4,20},{8,24},{12,28},{16,0},{20,4},{24,8},{28,12},{1,17},{... | collective-permute-start | bytes 1769480 | tf_op jit(solution)/shard_map/ppermute | solution.py:54
  542.0 29.3 %collective-permute-start.42 = (bf16[384,384]{1,0:T(8,128)(2,1)S(1)}, bf16[384,384]{1,0:T(8,128)(2,1)S(1)}, u32[]{:S(2)}, u32[]{:S(2)}) collective-permute-start(bf16[384,384]{1,0:T(8,128)(2,1)S(1)} %dynamic-slice_bitcast_fusion.23), channel_id=1, source_target_pairs={{0,16},{4,20},{8,24},{12,28},{16,0},{20,4},{24,8},{28,12},{1,17},{... | collective-permute-start | bytes 884744 | tf_op jit(solution)/shard_map/ppermute | solution.py:54
  554.6 19.0 %collective-permute-start.45 = (bf16[384,384]{1,0:T(8,128)(2,1)S(1)}, bf16[384,384]{1,0:T(8,128)(2,1)S(1)}, u32[]{:S(2)}, u32[]{:S(2)}) collective-permute-start(bf16[384,384]{1,0:T(8,128)(2,1)S(1)} %dynamic-slice_bitcast_fusion.22), channel_id=1, source_target_pairs={{0,8},{4,12},{8,0},{12,4},{16,24},{20,28},{24,16},{28,20},{1,9},{5... | collective-permute-start | bytes 884744 | tf_op jit(solution)/shard_map/ppermute | solution.py:54
  556.1 19.8 %collective-permute-start.52 = (bf16[384,384]{1,0:T(8,128)(2,1)S(1)}, bf16[384,384]{1,0:T(8,128)(2,1)S(1)}, u32[]{:S(2)}, u32[]{:S(2)}) collective-permute-start(bf16[384,384]{1,0:T(8,128)(2,1)S(1)} %dynamic-slice_bitcast_fusion.20), channel_id=1, source_target_pairs={{0,16},{4,20},{8,24},{12,28},{16,0},{20,4},{24,8},{28,12},{1,17},{... | collective-permute-start | bytes 884744 | tf_op jit(solution)/shard_map/ppermute | solution.py:54
  573.6 16.1 %collective-permute-start.15 = (bf16[96,1536]{1,0:T(8,128)(2,1)}, bf16[96,1536]{1,0:T(8,128)(2,1)S(1)}, u32[]{:S(2)}, u32[]{:S(2)}) collective-permute-start(bf16[96,1536]{1,0:T(8,128)(2,1)} %dynamic-slice_bitcast_fusion.28), channel_id=1, source_target_pairs={{0,8},{4,12},{8,0},{12,4},{16,24},{20,28},{24,16},{28,20},{1,9},{5... | collective-permute-start | bytes 884744 | tf_op jit(solution)/shard_map/ppermute | solution.py:54
  575.9 25.7 %collective-permute-start.46 = (bf16[2,96,768]{2,1,0:T(8,128)(2,1)}, bf16[2,96,768]{2,1,0:T(8,128)(2,1)}, u32[]{:S(2)}, u32[]{:S(2)}) collective-permute-start(bf16[2,96,768]{2,1,0:T(8,128)(2,1)} %dynamic-slice_bitcast_fusion.21), channel_id=1, source_target_pairs={{0,1},{1,0},{2,3},{3,2},{4,5},{5,4},{6,7},{7,6},{8,9},{9,8},{10,11... | collective-permute-start | bytes 884744 | tf_op jit(solution)/shard_map/ppermute | solution.py:54
  578.9 27.4 %collective-permute-start.56 = (bf16[2,96,768]{2,1,0:T(8,128)(2,1)}, bf16[2,96,768]{2,1,0:T(8,128)(2,1)}, u32[]{:S(2)}, u32[]{:S(2)}) collective-permute-start(bf16[2,96,768]{2,1,0:T(8,128)(2,1)} %dynamic-slice_bitcast_fusion.18), channel_id=1, source_target_pairs={{0,1},{1,0},{2,3},{3,2},{4,5},{5,4},{6,7},{7,6},{8,9},{9,8},{10,11... | collective-permute-start | bytes 884744 | tf_op jit(solution)/shard_map/ppermute | solution.py:54
  583.3 24.8 %collective-permute-start.26 = (bf16[96,2,768]{2,0,1:T(8,128)(2,1)}, bf16[96,2,768]{2,0,1:T(8,128)(2,1)}, u32[]{:S(2)}, u32[]{:S(2)}) collective-permute-start(bf16[96,2,768]{2,0,1:T(8,128)(2,1)} %bitcast.605), channel_id=1, source_target_pairs={{0,1},{1,0},{2,3},{3,2},{4,5},{5,4},{6,7},{7,6},{8,9},{9,8},{10,11... | collective-permute-start | bytes 884744 | tf_op jit(solution)/shard_map/ppermute | solution.py:54
  589.7 24.6 %collective-permute-start.36 = (bf16[96,2,768]{2,0,1:T(8,128)(2,1)}, bf16[96,2,768]{2,0,1:T(8,128)(2,1)}, u32[]{:S(2)}, u32[]{:S(2)}) collective-permute-start(bf16[96,2,768]{2,0,1:T(8,128)(2,1)} %bitcast.604), channel_id=1, source_target_pairs={{0,1},{1,0},{2,3},{3,2},{4,5},{5,4},{6,7},{7,6},{8,9},{9,8},{10,11... | collective-permute-start | bytes 884744 | tf_op jit(solution)/shard_map/ppermute | solution.py:54
  603.3 36.6 %collective-permute-start.47 = (bf16[96,768]{1,0:T(8,128)(2,1)}, bf16[96,768]{1,0:T(8,128)(2,1)}, u32[]{:S(2)}, u32[]{:S(2)}) collective-permute-start(bf16[96,768]{1,0:T(8,128)(2,1)} %dynamic-slice_bitcast_fusion.33), channel_id=1, source_target_pairs={{0,2},{1,3},{2,0},{3,1},{4,6},{5,7},{6,4},{7,5},{8,10},{9,11},{10,... | collective-permute-start | bytes 442376 | tf_op jit(solution)/shard_map/ppermute | solution.py:54
  608.1 33.3 %collective-permute-start.57 = (bf16[96,768]{1,0:T(8,128)(2,1)}, bf16[96,768]{1,0:T(8,128)(2,1)}, u32[]{:S(2)}, u32[]{:S(2)}) collective-permute-start(bf16[96,768]{1,0:T(8,128)(2,1)} %dynamic-slice_bitcast_fusion.32), channel_id=1, source_target_pairs={{0,2},{1,3},{2,0},{3,1},{4,6},{5,7},{6,4},{7,5},{8,10},{9,11},{10,... | collective-permute-start | bytes 442376 | tf_op jit(solution)/shard_map/ppermute | solution.py:54
  610.0 32.5 %collective-permute-start.27 = (bf16[96,768]{1,0:T(8,128)(2,1)}, bf16[96,768]{1,0:T(8,128)(2,1)}, u32[]{:S(2)}, u32[]{:S(2)}) collective-permute-start(bf16[96,768]{1,0:T(8,128)(2,1)} %dynamic-slice_bitcast_fusion.35), channel_id=1, source_target_pairs={{0,2},{1,3},{2,0},{3,1},{4,6},{5,7},{6,4},{7,5},{8,10},{9,11},{10,... | collective-permute-start | bytes 442376 | tf_op jit(solution)/shard_map/ppermute | solution.py:54
  616.0 29.2 %collective-permute-start.37 = (bf16[96,768]{1,0:T(8,128)(2,1)}, bf16[96,768]{1,0:T(8,128)(2,1)}, u32[]{:S(2)}, u32[]{:S(2)}) collective-permute-start(bf16[96,768]{1,0:T(8,128)(2,1)} %dynamic-slice_bitcast_fusion.34), channel_id=1, source_target_pairs={{0,2},{1,3},{2,0},{3,1},{4,6},{5,7},{6,4},{7,5},{8,10},{9,11},{10,... | collective-permute-start | bytes 442376 | tf_op jit(solution)/shard_map/ppermute | solution.py:54
  638.0 62.4 %collective-permute-start = (bf16[2,2,96,1536]{3,2,0,1:T(8,128)(2,1)}, bf16[2,2,96,1536]{3,2,0,1:T(8,128)(2,1)}, u32[]{:S(2)}, u32[]{:S(2)}) collective-permute-start(bf16[2,2,96,1536]{3,2,0,1:T(8,128)(2,1)} %bitcast.603), channel_id=1, source_target_pairs={{0,4},{4,0},{8,12},{12,8},{16,20},{20,16},{24,28},{28,24},{1,5},{5... | collective-permute-start | bytes 3538952 | tf_op jit(solution)/shard_map/ppermute | solution.py:54
  640.0 63.8 %collective-permute-start.3 = (bf16[2,2,96,1536]{3,2,1,0:T(8,128)(2,1)}, bf16[2,2,96,1536]{3,2,1,0:T(8,128)(2,1)}, u32[]{:S(2)}, u32[]{:S(2)}) collective-permute-start(bf16[2,2,96,1536]{3,2,1,0:T(8,128)(2,1)} %dynamic-slice_bitcast_fusion.5), channel_id=1, source_target_pairs={{0,4},{4,0},{8,12},{12,8},{16,20},{20,16},{24,28},{28,24},{1,5},{5... | collective-permute-start | bytes 3538952 | tf_op jit(solution)/shard_map/ppermute | solution.py:54
  641.4 64.9 %collective-permute-start.10 = (bf16[2,2,96,1536]{3,2,0,1:T(8,128)(2,1)}, bf16[2,2,96,1536]{3,2,0,1:T(8,128)(2,1)}, u32[]{:S(2)}, u32[]{:S(2)}) collective-permute-start(bf16[2,2,96,1536]{3,2,0,1:T(8,128)(2,1)} %bitcast.602), channel_id=1, source_target_pairs={{0,4},{4,0},{8,12},{12,8},{16,20},{20,16},{24,28},{28,24},{1,5},{5... | collective-permute-start | bytes 3538952 | tf_op jit(solution)/shard_map/ppermute | solution.py:54
  702.4 16.3 %collective-permute-start.1 = (bf16[2,96,1536]{2,1,0:T(8,128)(2,1)S(1)}, bf16[2,96,1536]{2,1,0:T(8,128)(2,1)S(1)}, u32[]{:S(2)}, u32[]{:S(2)}) collective-permute-start(bf16[2,96,1536]{2,1,0:T(8,128)(2,1)S(1)} %dynamic-slice_bitcast_fusion.17), channel_id=1, source_target_pairs={{0,8},{4,12},{8,0},{12,4},{16,24},{20,28},{24,16},{28,20},{1,9},{5... | collective-permute-start | bytes 1769480 | tf_op jit(solution)/shard_map/ppermute | solution.py:54
  705.4 15.8 %collective-permute-start.4 = (bf16[2,96,1536]{2,1,0:T(8,128)(2,1)S(1)}, bf16[2,96,1536]{2,1,0:T(8,128)(2,1)S(1)}, u32[]{:S(2)}, u32[]{:S(2)}) collective-permute-start(bf16[2,96,1536]{2,1,0:T(8,128)(2,1)S(1)} %dynamic-slice_bitcast_fusion.16), channel_id=1, source_target_pairs={{0,16},{4,20},{8,24},{12,28},{16,0},{20,4},{24,8},{28,12},{1,17},{... | collective-permute-start | bytes 1769480 | tf_op jit(solution)/shard_map/ppermute | solution.py:54
  707.9 23.4 %collective-permute-start.11 = (bf16[2,96,1536]{2,1,0:T(8,128)(2,1)S(1)}, bf16[2,96,1536]{2,1,0:T(8,128)(2,1)S(1)}, u32[]{:S(2)}, u32[]{:S(2)}) collective-permute-start(bf16[2,96,1536]{2,1,0:T(8,128)(2,1)S(1)} %dynamic-slice_bitcast_fusion.15), channel_id=1, source_target_pairs={{0,8},{4,12},{8,0},{12,4},{16,24},{20,28},{24,16},{28,20},{1,9},{5... | collective-permute-start | bytes 1769480 | tf_op jit(solution)/shard_map/ppermute | solution.py:54
  751.8 16.7 %collective-permute-start.17 = (bf16[96,768]{1,0:T(8,128)(2,1)S(1)}, bf16[96,768]{1,0:T(8,128)(2,1)S(1)}, u32[]{:S(2)}, u32[]{:S(2)}) collective-permute-start(bf16[96,768]{1,0:T(8,128)(2,1)S(1)} %dynamic-slice_bitcast_fusion.36), channel_id=1, source_target_pairs={{0,2},{1,3},{2,0},{3,1},{4,6},{5,7},{6,4},{7,5},{8,10},{9,11},{10,... | collective-permute-start | bytes 442376 | tf_op jit(solution)/shard_map/ppermute | solution.py:54
  758.4 16.4 %collective-permute-start.8 = (bf16[96,768]{1,0:T(8,128)(2,1)S(1)}, bf16[96,768]{1,0:T(8,128)(2,1)S(1)}, u32[]{:S(2)}, u32[]{:S(2)}) collective-permute-start(bf16[96,768]{1,0:T(8,128)(2,1)S(1)} %fusion.149), channel_id=1, source_target_pairs={{0,2},{1,3},{2,0},{3,1},{4,6},{5,7},{6,4},{7,5},{8,10},{9,11},{10,... | collective-permute-start | bytes 442376 | tf_op jit(solution)/shard_map/ppermute | solution.py:61
  (181 other events, 1395.4 us)
Sparse Core Ops, SparseCore 0:
  14.8 37.4 all-gather.8
  54.8 43.8 all-gather.10
  100.6 38.9 all-gather.16
  141.2 33.9 all-gather.12
  177.6 43.8 all-gather.14
  223.8 38.9 all-gather.18
